TPU v7x, 256 devices: a whole 4x4x8 slice. The times are simulated.
256 devices in a mesh: seq: 32 (over z, y), head: 8 (over x, core).
Axes of the slice: x: 4, y: 4, z: 8, core: 2. Of those that a mesh axis runs over, the one named last changes fastest.
Arguments:
- queries: bfloat16 [32768, 32, 128], P('seq', 'head'), may hold values from -0.59765625 to 0.59765625
- keys: bfloat16 [32768, 32, 128], P('seq', 'head'), may hold values from -6 to 6
- values: bfloat16 [32768, 32, 128], P('seq', 'head'), may hold values from -6 to 6
- log_decay: float32 [32768, 32], P('seq', 'head'), may hold values from -0.8 to 0, as said below
- level_weight: float32 [32768, 32, 10], P('seq', 'head'), may hold values from 0.1 to 2
- norm_gain: float32 [32, 128], P('head'), may hold values from 0.25 to 1.75
- out_weight: bfloat16 [4096, 4096], P('head'), may hold values from -0.09375 to 0.09375
Outputs:
- mixed: bfloat16 [32768, 4096], P(('seq', 'head'))
Inputs may be any that keep to these rules, and one draw needn't show every extreme that they name: `log_decay`: negative logarithms of decay factors.
All inputs are finite; a program needn't handle non-finite values.
Results may differ from a plain program's by a relative error of at most 0.023.
Values may be sent and summed in bfloat16 or wider, within the bound.
No kernel may reach another device: no remote copies, remote signals or barrier semaphores. Data moves between devices by JAX's collectives and lax.ppermute only.
A program may use at most 128 MiB of HBM per device.

v0:
```python
import jax
import jax.numpy as jnp
import numpy as np
from jax import lax
from jax.sharding import PartitionSpec as P

SPAN = 64


def span_terms(query_blocks, key_blocks, value_blocks, inner):
    size = inner.shape[1]
    scores = jnp.einsum(
        "cthd,cshd->chts", query_blocks, key_blocks, preferred_element_type=jnp.float32
    )
    leading = jnp.transpose(inner, (0, 2, 1))
    causal = np.tril(np.ones((size, size), dtype=bool))
    spread = jnp.where(causal, leading[:, :, :, None] - leading[:, :, None, :], 0.0)
    weight = jnp.where(causal, jnp.exp(spread), 0.0)
    probs = (scores * weight).astype(jnp.bfloat16)
    within = jnp.einsum("chts,cshe->cthe", probs, value_blocks, preferred_element_type=jnp.float32)
    scaled = (jnp.exp(inner[:, -1:, :] - inner)[:, :, :, None] * key_blocks).astype(jnp.bfloat16)
    states = jnp.einsum("cshd,cshe->chde", scaled, value_blocks, preferred_element_type=jnp.float32)
    return (within, states)


def local_levels(query_blocks, inner, states, totals, before, weights):
    count = states.shape[0]
    depth = count.bit_length() - 1
    output = jnp.zeros(query_blocks.shape, jnp.float32)
    blocks = states
    block_total = totals
    span_ids = np.arange(count)
    for level_now in range(1, depth + 1):
        shift_by = level_now - 1
        present = (span_ids >> shift_by & 1).astype(np.float32)
        source = np.maximum((span_ids >> shift_by) - 1, 0)
        middle = span_ids >> shift_by << shift_by
        picked = blocks[source].astype(jnp.bfloat16)
        readout = jnp.einsum(
            "cthd,chde->cthe", query_blocks, picked, preferred_element_type=jnp.float32
        )
        factor = (
            jnp.exp((before - before[middle])[:, None, :] + inner)
            * weights[:, :, :, level_now]
            * present[:, None, None]
        )
        output = output + factor[:, :, :, None] * readout
        blocks = jnp.exp(block_total[1::2])[:, :, None, None] * blocks[0::2] + blocks[1::2]
        block_total = block_total[0::2] + block_total[1::2]
    return (output, blocks[0], block_total[0])


def body(queries, keys, values, log_decay, level_weight, norm_gain, out_weight):
    row_count, head_count, head_width = queries.shape
    span_count = row_count // SPAN
    local_depth = span_count.bit_length() - 1
    seq_bits = lax.axis_size("seq").bit_length() - 1
    position = lax.axis_index("seq")
    shaped = (span_count, SPAN, head_count, head_width)
    query_blocks = queries.reshape(shaped)
    key_blocks = keys.reshape(shaped)
    value_blocks = values.reshape(shaped)
    weights = level_weight.reshape(span_count, SPAN, head_count, level_weight.shape[2])
    inner = jnp.cumsum(log_decay.reshape(span_count, SPAN, head_count), axis=1)
    totals = inner[:, -1, :]
    before = jnp.cumsum(totals, axis=0) - totals
    within, states = span_terms(query_blocks, key_blocks, value_blocks, inner)
    output = within * weights[:, :, :, 0:1]
    nearby, summary, summary_total = local_levels(
        query_blocks, inner, states, totals, before, weights
    )
    output = output + nearby
    all_totals = lax.all_gather(summary_total[None], "seq", axis=0, tiled=True)
    device_before = jnp.cumsum(all_totals, axis=0) - all_totals
    own_before = lax.dynamic_index_in_dim(device_before, position, 0, keepdims=False)
    bit_range = jnp.arange(seq_bits, dtype=jnp.int32)
    middles = position >> bit_range << bit_range
    middle_before = jnp.take(device_before, middles, axis=0)
    initial = jnp.zeros((seq_bits,) + summary.shape, jnp.float32)
    piece = lax.all_gather(summary[None].astype(jnp.bfloat16), "seq", axis=0, tiled=True).astype(
        jnp.float32
    )
    piece_rows = piece.shape[0]
    sources = jnp.arange(piece_rows, dtype=jnp.int32)
    mixed_bits = sources ^ position
    level_of = jnp.zeros((piece_rows,), jnp.int32)
    for bit_now in range(1, seq_bits):
        level_of = level_of + (mixed_bits >> bit_now > 0).astype(jnp.int32)
    valid = sources < position
    select = (level_of[:, None] == bit_range[None, :]) & valid[:, None]
    source_end = device_before + all_totals
    gap = middle_before[None, :, :] - source_end[:, None, :]
    gap = jnp.where(select[:, :, None], gap, 0.0)
    factor = select.astype(jnp.float32)[:, :, None] * jnp.exp(gap)
    far_states = initial + jnp.einsum(
        "mbh,mhde->bhde", factor, piece, precision=lax.Precision.HIGHEST
    )
    far_offset = own_before[None, :] - middle_before
    far_flag = (position >> bit_range & 1).astype(jnp.float32)
    far_cast = far_states.astype(jnp.bfloat16)
    far_read = jnp.einsum(
        "cthd,bhde->ctbhe", query_blocks, far_cast, preferred_element_type=jnp.float32
    )
    far_weight = jnp.transpose(weights[:, :, :, local_depth + 1 :], (0, 1, 3, 2))
    exponent = far_offset[None, None, :, :] + (before[:, None, :] + inner)[:, :, None, :]
    far_factor = jnp.exp(exponent) * far_flag[None, None, :, None] * far_weight
    output = output + jnp.sum(far_factor[:, :, :, :, None] * far_read, axis=2)
    attention = output.reshape(row_count, head_count, head_width)
    mean_square = jnp.mean(attention * attention, axis=-1, keepdims=True)
    normed = (attention * lax.rsqrt(mean_square + 1e-06) * norm_gain[None]).astype(jnp.bfloat16)
    normed = normed.reshape(row_count, head_count * head_width)
    return lax.psum_scatter(
        jnp.dot(normed, out_weight, preferred_element_type=jnp.float32).astype(jnp.bfloat16),
        "head",
        scatter_dimension=0,
        tiled=True,
    )


def solution(mesh):
    return jax.shard_map(
        body,
        mesh=mesh,
        in_specs=(
            P("seq", "head", None),
            P("seq", "head", None),
            P("seq", "head", None),
            P("seq", "head"),
            P("seq", "head", None),
            P("head", None),
            P("head", None),
        ),
        out_specs=P(("seq", "head"), None),
        check_vma=False,
    )
```

profile of v0, /device:TPU:1, one launch (start us, length us, event | category | flops | bytes accessed | tf_op | source)
XLA Modules:
  0.0 213.9 jit_solution(3391887613653050703)
XLA Ops:
  6.5 0.9 reshape.274
  7.5 0.3 copy.261
  7.8 6.3 %fusion.92 = f32[16,64,4]{2,0,1:T(8,128)S(1)} fusion(f32[16,64,4]{2,0,1:T(8,128)S(1)} %copy.261), kind=kOutput, calls=%fused_computation.144 | output fusion | flops 258048 | bytes 32768 | tf_op jit(solution)/shard_map/jit(cumsum)/reduce_window_sum | solution.py:64
  15.3 0.7 exponential_reduce_fusion
  16.1 0.6 gather_fusion
  16.7 0.5 fusion.76
  17.4 0.9 broadcast_add_fusion
  18.3 0.3 copy.275
  18.5 2.3 %fusion.24 = f32[16,4,128,128]{3,2,1,0:T(8,128)S(1)} fusion(f32[16,64,4]{1,2,0:T(4,128)S(1)} %copy.275, bf16[16,64,4,128]{3,2,1,0:T(4,128)(2,1)S(1)} %bitcast.162, bf16[16,64,4,128]{3,2,1,0:T(4,128)(2,1)S(1)} %bitcast.170), kind=kOutput, calls=%fused_computation.41 | convolution fusion | flops 135790592 | bytes 6307840 | tf_op jit(solution)/shard_map/cshd,cshe->chde/dot_general | solution.py:22
  20.9 0.3 slice_add_fusion
  21.1 1.7 copy-done.2
  22.9 0.2 slice_add_fusion.1
  23.0 1.0 copy-done.5
  24.0 0.1 slice_add_fusion.2
  24.1 0.8 copy-done.3
  24.9 0.7 fusion.58
  25.7 1.1 reshape.276
  26.8 0.6 slice_bitcast_fusion.1
  27.5 0.6 copy.265
  28.1 0.7 pad_clamp_fusion.2
  28.8 0.6 gather_fusion.6
  29.4 0.7 pad_clamp_fusion.4
  30.1 0.6 gather_fusion.4
  30.7 0.6 gather_fusion.2
  31.4 0.7 copy.271
  32.2 0.7 copy.292
  32.8 0.7 copy.286
  33.5 37.4 %all-gather = f32[32,1,4]{2,1,0:T(1,128)S(1)} all-gather(f32[1,1,4]{2,1,0:T(1,128)} %bitcast.181), channel_id=1, replica_groups=mesh['seq'=32,'head'=8] {'seq'}, dimensions={0}, use_global_device_ids=true | all-gather | bytes 528 | tf_op jit(solution)/shard_map/all_gather | solution.py:73
  70.9 0.6 copy.297
  71.5 0.7 copy.298
  72.2 0.6 reduce_window_sum.41
  72.9 1.3 fusion.84
  74.2 1.4 copy.305
  75.6 0.6 gather_fusion.8
  76.2 0.7 broadcast_subtract_fusion
  76.9 0.6 copy.303
  77.5 1.3 copy.262
  78.8 1.8 copy.324
  80.6 1.8 copy.323
  82.4 1.8 copy.322
  84.3 1.1 copy.325
  85.3 3.3 %fusion.45 = (f32[16,64,4]{2,0,1:T(8,128)}, f32[16,64,4]{2,0,1:T(8,128)}, f32[16,64,4]{2,0,1:T(8,128)}, f32[16,64,4]{2,0,1:T(8,128)}) fusion(f32[16,64,4,1]{2,0,1,3:T(8,128)} %copy.322, f32[16,64,4]{2,0,1:T(8,128)} %copy-done.6, f32[16]{0:T(128)} %constant.105, f32[16,4]{1,0:T(8,128)S(1)} %copy.271, f32[16]{0:T(128)} %constant.108, ...), kind=kLoop, calls=%fused_computation.63 | loop fusion | flops 49152 | bytes 148736 | tf_op jit(solution)/shard_map/mul | solution.py:47
  88.6 1.3 copy.273
  89.9 1.9 copy.282
  91.8 1.9 copy.288
  93.7 1.9 copy.294
  95.6 1.9 copy.301
  97.5 4.3 %gather_fusion.1 = bf16[16,4,128,128]{3,2,1,0:T(8,128)(2,1)} fusion(f32[16,4,128,128]{3,2,1,0:T(8,128)} %copy-done.2, s32[1024]{0:T(1024)S(1)} %pad_clamp_fusion.7), kind=kCustom, calls=%fused_computation.1 | custom fusion | bytes 4194368 | tf_op jit(solution)/shard_map/gather | solution.py:38
  101.9 2.1 gather_fusion.3
  104.0 3.4 %gather_fusion.5 = bf16[16,4,128,128]{3,2,1,0:T(8,128)(2,1)} fusion(f32[4,4,128,128]{3,2,1,0:T(8,128)} %copy-done.5, s32[1024]{0:T(1024)S(1)} %pad_clamp_fusion.3), kind=kCustom, calls=%fused_computation.5 | custom fusion | bytes 4194368 | tf_op jit(solution)/shard_map/gather | solution.py:38
  107.5 2.1 gather_fusion.7
  109.6 0.5 and_convert_fusion
  110.1 3.8 %fusion.16 = f32[16,4,128,64]{2,3,1,0:T(8,128)} fusion(bf16[16,4,128,128]{3,2,1,0:T(8,128)(2,1)} %gather_fusion.1, bf16[16,64,4,128]{3,2,1,0:T(4,128)(2,1)S(1)} %bitcast.163), kind=kOutput, calls=%fused_computation.35 | convolution fusion | flops 134217728 | bytes 5242880 | tf_op jit(solution)/shard_map/cthd,chde->cthe/dot_general | solution.py:39
  113.9 2.1 fusion.14
  116.0 2.1 fusion.12
  118.1 2.0 fusion.10
  120.2 5.7 %fusion.21 = bf16[5,4,128,128,1]{3,0,2,1,4:T(8,128)(2,1)S(1)} fusion(bf16[32,4,128,128]{3,2,1,0:T(8,128)(2,1)} %all-gather.3.cloned.1.call-done, f32[32,4]{0,1:T(4,128)S(1)} %copy-done.15, f32[5,4]{0,1:T(4,128)S(1)} %copy-done.16, f32[32,5]{0,1:T(8,128)S(1)} %get-tuple-element.34, pred[32,5]{0,1:T(8,128)(4,1)S(1)} %get-tuple-element.33), kind=kOutput, calls=%fused_computation.40 | convolution fusion | flops 126158720 | bytes 4851056 | tf_op jit(solution)/shard_map/mbh,mhde->bhde/dot_general | solution.py:95
  125.9 4.4 %fusion = f32[16,64,4,128]{3,1,0,2:T(8,128)} fusion(bf16[16,64,4,128,1]{3,2,1,0,4:T(4,128)(2,1)S(1)} %bitcast.167, bf16[5,4,128,128,1]{3,0,2,1,4:T(8,128)(2,1)S(1)} %fusion.21, f32[16,64,4,10]{1,0,2,3:T(8,128)S(1)} %reshape.276, f32[5]{0:T(128)S(1)} %copy-done.23, f32[16,64,4]{1,0,2:T(8,128)S(1)} %copy-done.12, f32[5,4]{1,0:T(8,128)S(1)} %copy-done.14), kind=kOutput, calls=%fused_computation.10 | convolution fusion | flops 675868672 | bytes 4395520 | tf_op jit(solution)/shard_map/cthd,bhde->ctbhe/dot_general | solution.py:101
  130.4 7.4 %multiply_reduce_fusion = (f32[16,64,4]{1,2,0:T(4,128)S(1)}, f32[16,64,4,128]{3,1,2,0:T(8,128)}) fusion(f32[16,64,4,128]{3,1,0,2:T(8,128)} %fusion, f32[16,4,128,64]{2,3,1,0:T(8,128)} %fusion.10, f32[16,64,4]{1,2,0:T(4,128)} %copy.294, f32[16,4,128,64]{2,3,1,0:T(8,128)} %fusion.12, f32[16,64,4]{1,2,0:T(4,128)} %copy.288, f32[16,4,128,64]{2,3,1,0:T(8,128)} %fusion.14, ...), kind=kOutput, calls=%fused_computation.27 | convolution fusion | flops 141815808 | bytes 15847424 | tf_op jit(solution)/shard_map/chts,cshe->cthe/dot_general | solution.py:20
  137.8 0.2 copy.320
  138.1 3.1 %copy.310 = f32[16,64,4,128]{3,2,1,0:T(4,128)S(1)} copy(f32[16,64,4,128]{3,1,2,0:T(8,128)} %get-tuple-element.36) | data formatting | bytes 4194304 | tf_op jit(solution)/shard_map/add | solution.py:107
  141.2 1.2 mul.259
  142.5 6.7 %convolution_convert_fusion = bf16[1024,4096]{1,0:T(8,128)(2,1)} fusion(bf16[512,4096]{1,0:T(8,128)(2,1)S(1)} %copy-done.21, f32[128,8,4,128]{3,2,1,0:T(4,128)S(1)} %bitcast.172, f32[128,8,4,128]{3,2,1,0:T(4,128)S(1)} %bitcast.174, f32[512]{0:T(512)S(1)} %bitcast.182), kind=kOutput, calls=%fused_computation.11 | convolution fusion | flops 4300734464 | bytes 16779264 | tf_op jit(solution)/shard_map/dot_general | solution.py:113
  149.3 57.8 %reduce-scatter.2.cloned.1.call-done = bf16[128,4096]{1,0:T(8,128)(2,1)} async-done(((bf16[1024,4096]{1,0:T(8,128)(2,1)}), bf16[128,4096]{1,0:T(8,128)(2,1)}) %reduce-scatter.2.cloned.1.call-update) | async-done | bytes 1048592 | tf_op jit(solution)/shard_map/reduce_scatter | solution.py:112
  (91 shorter events, 2.0 us)
Async XLA Ops:
  6.5 12.0 %copy-start = (bf16[1024,4,128]{2,1,0:T(4,128)(2,1)S(1)}, bf16[1024,4,128]{2,1,0:T(4,128)(2,1)}, u32[]{:S(2)}) copy-start(bf16[1024,4,128]{2,1,0:T(4,128)(2,1)} %param.30) | copy-start | bytes 3145732
  6.5 12.0 %copy-start.10 = (bf16[1024,4,128]{2,1,0:T(4,128)(2,1)S(1)}, bf16[1024,4,128]{2,1,0:T(4,128)(2,1)}, u32[]{:S(2)}) copy-start(bf16[1024,4,128]{2,1,0:T(4,128)(2,1)} %param.29) | copy-start | bytes 3145732
  6.5 113.6 %all-gather.3.cloned.1.call-start = ((), (), s32[]{:S(2)}) async-start(), calls=%async_computation.1 | async-start | bytes 4325376 | tf_op jit(solution)/shard_map/all_gather | solution.py:80
  14.2 4.4 %copy-start.6 = (f32[16,64,4]{2,0,1:T(8,128)}, f32[16,64,4]{2,0,1:T(8,128)S(1)}, u32[]{:S(2)}) copy-start(f32[16,64,4]{2,0,1:T(8,128)S(1)} %fusion.92) | copy-start | bytes 49156
  20.9 2.0 copy-start.2
  23.0 1.0 copy-start.5
  24.0 6.7 %copy-start.20 = (s32[16]{0:T(128)S(1)}, s32[16]{0:T(128)}, u32[]{:S(2)}) copy-start(s32[16]{0:T(128)} %constant.116) | copy-start | bytes 196
  24.1 0.8 copy-start.3
  25.7 181.3 %reduce-scatter.2.cloned.1.call-start = ((), (), s32[]{:S(2)}) async-start(), calls=%async_computation.2 | async-start | bytes 9437184 | tf_op jit(solution)/shard_map/reduce_scatter | solution.py:112
  88.6 8.9 %copy-start.19 = (s32[16]{0:T(128)S(1)}, s32[16]{0:T(128)}, u32[]{:S(2)}) copy-start(s32[16]{0:T(128)} %constant.115) | copy-start | bytes 196
  97.5 4.4 %copy-start.18 = (s32[16]{0:T(128)S(1)}, s32[16]{0:T(128)}, u32[]{:S(2)}) copy-start(s32[16]{0:T(128)} %constant.117) | copy-start | bytes 196
  101.9 2.1 copy-start.17
  104.0 3.4 %copy-start.4 = (f32[2,4,128,128]{3,2,1,0:T(8,128)S(1)}, f32[2,4,128,128]{3,2,1,0:T(8,128)}, u32[]{:S(2)}) copy-start(f32[2,4,128,128]{3,2,1,0:T(8,128)} %copy-done.3) | copy-start | bytes 1572868
  107.5 2.6 %copy-start.1 = (bf16[1024,4,128]{2,1,0:T(4,128)(2,1)S(1)}, bf16[1024,4,128]{2,1,0:T(4,128)(2,1)}, u32[]{:S(2)}) copy-start(bf16[1024,4,128]{2,1,0:T(4,128)(2,1)} %param.28) | copy-start | bytes 3145732
  110.1 3.8 %copy-start.7 = (bf16[16,4,128,128]{3,2,1,0:T(8,128)(2,1)S(1)}, bf16[16,4,128,128]{3,2,1,0:T(8,128)(2,1)}, u32[]{:S(2)}) copy-start(bf16[16,4,128,128]{3,2,1,0:T(8,128)(2,1)} %gather_fusion.3) | copy-start | bytes 6291460
  113.9 2.1 copy-start.8
  116.0 2.1 copy-start.9
  118.1 2.1 copy-start.15
  118.1 2.1 copy-start.16
  120.2 5.7 %copy-start.12 = (f32[16,64,4]{1,0,2:T(8,128)S(1)}, f32[16,64,4]{1,0,2:T(8,128)}, u32[]{:S(2)}) copy-start(f32[16,64,4]{1,0,2:T(8,128)} %copy.301) | copy-start | bytes 49156
  120.2 5.7 %copy-start.14 = (f32[5,4]{1,0:T(8,128)S(1)}, f32[5,4]{1,0:T(8,128)}, u32[]{:S(2)}) copy-start(f32[5,4]{1,0:T(8,128)} %get-tuple-element.11) | copy-start | bytes 244
  120.2 5.7 %copy-start.23 = (f32[5]{0:T(128)S(1)}, f32[5]{0:T(128)}, u32[]{:S(2)}) copy-start(f32[5]{0:T(128)} %and_convert_fusion) | copy-start | bytes 64
  125.9 4.5 %copy-start.11 = (bf16[1024,4,128]{2,1,0:T(4,128)(2,1)S(1)}, bf16[1024,4,128]{2,1,0:T(4,128)(2,1)}, u32[]{:S(2)}) copy-start(bf16[1024,4,128]{2,1,0:T(4,128)(2,1)} %param.29) | copy-start | bytes 3145732
  125.9 4.5 %copy-start.13 = (pred[64,64]{1,0:T(32,128)(4,1)S(1)}, pred[64,64]{1,0:T(32,128)(4,1)}, u32[]{:S(2)}) copy-start(pred[64,64]{1,0:T(32,128)(4,1)} %constant.86.clone) | copy-start | bytes 12292
  138.1 4.4 %copy-start.21 = (bf16[512,4096]{1,0:T(8,128)(2,1)S(1)}, bf16[512,4096]{1,0:T(8,128)(2,1)}, u32[]{:S(2)}) copy-start(bf16[512,4096]{1,0:T(8,128)(2,1)} %param.34) | copy-start | bytes 12582916
  141.2 1.3 copy-start.22
Sparse Core Ops, SparseCore 0:
  25.8 82.9 all-gather.2
  149.4 57.5 reduce-scatter.1
where the time goes:
time: 215 us; the launch traced here: 214 us
  waiting for transfers between devices  57.8 us (27%)
  local copies, waits for them, and re-layouts  50.5 us (23%)
  blocking collectives  37.4 us (17%)
  matrix products  36.6 us (17%)
  other arithmetic  17.7 us (8%)
  between operations  13.8 us (6%)
    reduce_scatter x1, waiting for transfers between devices, body(): lax.psum_scatter(jnp.dot(normed, out_weight, preferred_element_type=jnp.f...  57.8 us
    all_gather x1, blocking collectives, body(): all_totals = lax.all_gather(summary_total[None], 'seq', axis=0, tiled=True)  37.4 us
    gather x4, local copies, waits for them, and re-layouts, local_levels(): picked = blocks[source].astype(jnp.bfloat16)  12 us
    unnamed x54, local copies, waits for them, and re-layouts  10.9 us
    dot_general x4, matrix products, local_levels(): jnp.einsum('cthd,chde->cthe', query_blocks, picked, preferred_element_typ...  9.98 us
    dot_general x1, matrix products, span_terms(): jnp.einsum('chts,cshe->cthe', probs, value_blocks, preferred_element_type...  7.42 us
    mul x4, local copies, waits for them, and re-layouts, local_levels(): output = output + factor[:, :, :, None] * readout  7.01 us
    dot_general x1, matrix products, body(): jnp.dot(normed, out_weight, preferred_element_type=jnp.float32)  6.72 us
  transfers between devices with their start and end apart: 2, of which 1 were waited for; matrix products, arithmetic and copies ran while one was open for 27% of the time, Pallas kernels for 0%

commit v1 on v0

v1 whole, which is shorter than its diff:
```python
import functools
import jax
import jax.numpy as jnp
from jax import lax
from jax.experimental import pallas as pl
from jax.experimental.pallas import tpu as pltpu
from jax.sharding import PartitionSpec as P

SPAN = 64
HD = 128
BF = jnp.bfloat16
F32 = jnp.float32
VMEM_LIMIT = 48 * 1024 * 1024


def params(**kw):
    return pltpu.CompilerParams(vmem_limit_bytes=VMEM_LIMIT, **kw)


def dot(a, b):
    return jnp.dot(a, b, preferred_element_type=F32)


def lane_cumsum(x):
    lanes = lax.broadcasted_iota(jnp.int32, (x.shape[0], 128), 1)
    carry = jnp.zeros((x.shape[0], 1), F32)
    chunks = []
    for i in range(x.shape[1] // 128):
        c = x[:, i * 128 : (i + 1) * 128]
        step = 1
        while step < 128:
            c = c + jnp.where(lanes >= step, pltpu.roll(c, step, 1), 0.0)
            step *= 2
        chunks.append(c)
    out = []
    for c in chunks:
        out.append(c + carry)
        carry = carry + c[:, 127:128]
    return jnp.concatenate(out, axis=1)


def total_rows(total):
    high = total.astype(BF).astype(F32)
    mid = (total - high).astype(BF).astype(F32)
    low = total - high - mid
    rows = jnp.concatenate([high, mid, low, jnp.zeros_like(low)], axis=0)
    return rows.astype(BF)


def summary_kernel(ld_ref, k_ref, v_ref, state_ref, pay_ref, cum_ref, tot_ref, w_ref):
    h = pl.program_id(0)
    heads = ld_ref.shape[0]

    @pl.when(h == 0)
    def _():
        cum = lane_cumsum(ld_ref[...])
        total = cum[:, -1:]
        cum_ref[...] = cum
        w_ref[...] = jnp.exp(total - cum)
        wide = jnp.broadcast_to(total, (heads, 128))
        tot_ref[...] = wide
        pay_ref[heads * HD :, :] = total_rows(wide)

    row = w_ref[pl.ds(h, 1), :]
    vt = (v_ref[...].astype(F32).T * row).astype(BF)
    state = dot(vt, k_ref[...])
    state_ref[...] = state
    pay_ref[pl.ds(pl.multiple_of(h * HD, HD), HD), :] = state.astype(BF)


def summary(ld, k, v):
    heads, rows = ld.shape
    full = lambda *shape: pl.BlockSpec(shape, lambda h: (0,) * len(shape))
    return pl.pallas_call(
        summary_kernel,
        grid=(heads,),
        in_specs=[
            full(heads, rows),
            pl.BlockSpec((rows, HD), lambda h: (0, h)),
            pl.BlockSpec((rows, HD), lambda h: (0, h)),
        ],
        out_specs=[
            pl.BlockSpec((HD, HD), lambda h: (h, 0)),
            full(heads * HD + 16, 128),
            full(heads, rows),
            full(heads, 128),
        ],
        out_shape=[
            jax.ShapeDtypeStruct((heads * HD, HD), F32),
            jax.ShapeDtypeStruct((heads * HD + 16, 128), BF),
            jax.ShapeDtypeStruct((heads, rows), F32),
            jax.ShapeDtypeStruct((heads, 128), F32),
        ],
        scratch_shapes=[pltpu.VMEM((heads, rows), F32)],
        compiler_params=params(),
        name="summary",
        cost_estimate=pl.CostEstimate(flops=140_000_000, bytes_accessed=3_000_000, transcendentals=4096),
    )(ld, k, v)


def merge_kernel(pos_ref, recv_ref, state_ref, tot_ref, off_ref, state_out, pay_out, tot_out, off_out, *, bit):
    heads = tot_ref.shape[0]
    right = ((pos_ref[0] >> bit) & 1).astype(F32)
    rows = recv_ref[heads * HD :, :].astype(F32)
    there = rows[:heads] + rows[heads : 2 * heads] + rows[2 * heads : 3 * heads]
    here = tot_ref[...]
    total = here + there
    tot_out[...] = total
    off_out[...] = off_ref[...] + right * there
    pay_out[heads * HD :, :] = total_rows(total)
    keep = right + (1.0 - right) * jnp.exp(there)
    take = (1.0 - right) + right * jnp.exp(here)
    for h in range(heads):
        block = pl.ds(h * HD, HD)
        state = state_ref[block, :] * keep[h : h + 1] + recv_ref[block, :].astype(F32) * take[h : h + 1]
        state_out[block, :] = state
        pay_out[block, :] = state.astype(BF)


def merge(pos, recv, state, tot, off, bit):
    vm = pl.BlockSpec(memory_space=pltpu.VMEM)
    return pl.pallas_call(
        functools.partial(merge_kernel, bit=bit),
        in_specs=[pl.BlockSpec(memory_space=pltpu.SMEM), vm, vm, vm, vm],
        out_specs=[vm, vm, vm, vm],
        out_shape=[
            jax.ShapeDtypeStruct(state.shape, F32),
            jax.ShapeDtypeStruct(recv.shape, BF),
            jax.ShapeDtypeStruct(tot.shape, F32),
            jax.ShapeDtypeStruct(off.shape, F32),
        ],
        compiler_params=params(),
        name=f"merge{bit}",
        cost_estimate=pl.CostEstimate(flops=200_000, bytes_accessed=800_000, transcendentals=1024),
    )(pos, recv, state, tot, off)


def local_kernel(q_ref, k_ref, v_ref, cum_ref, lw_ref, acc_ref, qt_ref, *, head):
    rows = q_ref.shape[0]
    pair = 2 * SPAN
    qt = q_ref[...].astype(F32).T.astype(BF)
    qt_ref[...] = qt
    vt = v_ref[...].astype(F32).T
    cum = cum_ref[head : head + 1, :]
    weight = lambda level: lw_ref[level, head : head + 1, :]
    s_pos = lax.broadcasted_iota(jnp.int32, (pair, pair), 0)
    t_pos = lax.broadcasted_iota(jnp.int32, (pair, pair), 1)
    same = jnp.logical_and(s_pos <= t_pos, (s_pos >= SPAN) == (t_pos >= SPAN))
    cross = jnp.logical_and(s_pos < SPAN, t_pos >= SPAN)
    for i in range(rows // pair):
        at = slice(i * pair, (i + 1) * pair)
        middle = cum[:, i * pair + SPAN - 1 : i * pair + SPAN]
        grow = jnp.exp(cum[:, at] - middle)
        scores = dot(k_ref[at, :], qt[:, at])
        probs = scores * jnp.where(same, weight(0)[:, at], jnp.where(cross, weight(1)[:, at], 0.0))
        held = (vt[:, at] * jnp.exp(middle - cum[:, at])).astype(BF)
        acc_ref[:, at] = dot(held, probs.astype(BF)) * grow
    level, half = 2, pair
    while half < rows:
        for i in range(rows // (2 * half)):
            left = slice(2 * i * half, (2 * i + 1) * half)
            right = slice((2 * i + 1) * half, (2 * i + 2) * half)
            end = cum[:, left.stop - 1 : left.stop]
            held = (vt[:, left] * jnp.exp(end - cum[:, left])).astype(BF)
            bucket = dot(held, k_ref[left, :]).astype(BF)
            factor = weight(level)[:, right] * jnp.exp(cum[:, right] - end)
            acc_ref[:, right] += dot(bucket, qt[:, right]) * factor
        level, half = level + 1, half * 2


def local(q, k, v, cum, lw, head):
    rows = q.shape[0]
    col = pl.BlockSpec((rows, HD), lambda i: (0, head))
    return pl.pallas_call(
        functools.partial(local_kernel, head=head),
        grid=(1,),
        in_specs=[
            col,
            col,
            col,
            pl.BlockSpec(cum.shape, lambda i: (0, 0)),
            pl.BlockSpec(lw.shape, lambda i: (0, 0, 0)),
        ],
        out_specs=[pl.BlockSpec((HD, rows), lambda i: (0, 0))] * 2,
        out_shape=[jax.ShapeDtypeStruct((HD, rows), F32), jax.ShapeDtypeStruct((HD, rows), BF)],
        compiler_params=params(),
        name=f"local{head}",
        cost_estimate=pl.CostEstimate(flops=2_000_000_000, bytes_accessed=3_000_000, transcendentals=16384),
    )(q, k, v, cum, lw)


def far_term(pos_ref, recv_ref, off, qt, cum, lw_ref, head, bit, base):
    flag = ((pos_ref[0] >> bit) & 1).astype(F32)
    factor = lw_ref[base + bit, head : head + 1, :] * jnp.exp(off[head : head + 1, :1] + cum) * flag
    return dot(recv_ref[head * HD : (head + 1) * HD, :], qt) * factor


def far_kernel(pos_ref, *refs, heads, bits, base):
    accs, qts = refs[:heads], refs[heads : 2 * heads]
    recvs, offs = refs[2 * heads : 2 * heads + bits], refs[2 * heads + bits : 2 * heads + 2 * bits]
    cum_ref, lw_ref, out_ref = refs[2 * heads + 2 * bits :]
    for h in range(heads):
        acc = accs[h][...]
        qt = qts[h][...]
        cum = cum_ref[h : h + 1, :]
        for b in range(bits):
            acc = acc + far_term(pos_ref, recvs[b], offs[b][...], qt, cum, lw_ref, h, b, base)
        out_ref[h * HD : (h + 1) * HD, :] = acc


def far(pos, accs, qts, recvs, offs, cum, lw, base):
    heads, rows, bits = len(accs), cum.shape[1], len(recvs)
    width = min(256, rows)
    chunk = lambda *lead: pl.BlockSpec((*lead, width), lambda i: (0,) * len(lead) + (i,))
    whole = lambda a: pl.BlockSpec(a.shape, lambda i: (0,) * a.ndim)
    return pl.pallas_call(
        functools.partial(far_kernel, heads=heads, bits=bits, base=base),
        grid=(rows // width,),
        in_specs=[pl.BlockSpec(memory_space=pltpu.SMEM)]
        + [chunk(HD)] * (2 * heads)
        + [whole(a) for a in recvs]
        + [whole(a) for a in offs]
        + [chunk(heads), chunk(lw.shape[0], heads)],
        out_specs=chunk(heads * HD),
        out_shape=jax.ShapeDtypeStruct((heads * HD, rows), F32),
        compiler_params=params(),
        name="far",
        cost_estimate=pl.CostEstimate(flops=2_000_000_000, bytes_accessed=6_000_000, transcendentals=16384),
    )(pos, *accs, *qts, *recvs, *offs, cum, lw)


def norm_kernel(pick_ref, *refs, heads, bit, base):
    acc_ref, qts = refs[0], refs[1 : 1 + heads]
    recv_ref, off_ref, cum_ref, lw_ref, gain_ref, mine_ref, other_ref, tile_ref = refs[1 + heads :]
    flag = ((pick_ref[0] >> bit) & 1).astype(F32)
    core = pick_ref[1]
    for h in range(heads):
        at = slice(h * HD, (h + 1) * HD)
        factor = lw_ref[base + bit, h : h + 1, :] * jnp.exp(off_ref[h : h + 1, :1] + cum_ref[h : h + 1, :]) * flag
        att = acc_ref[at, :] + dot(recv_ref[at, :], qts[h][...]) * factor
        mean = jnp.mean(att * att, axis=0, keepdims=True)
        normed = (att * lax.rsqrt(mean + 1e-6)).T * gain_ref[h : h + 1, :]
        tile_ref[:, at] = normed.astype(BF)
    size = mine_ref.shape[0]
    mine_ref[...] = tile_ref[pl.ds(pl.multiple_of(core * size, size), size), :]
    other_ref[...] = tile_ref[pl.ds(pl.multiple_of((1 - core) * size, size), size), :]


def norm(pick, acc, qts, recv, off, cum, lw, gain, bit, base, slots):
    heads, rows = cum.shape
    width = rows // slots
    half = width // 2
    chunk = lambda *lead: pl.BlockSpec((*lead, width), lambda i, p: (0,) * len(lead) + (p[2 + i],))
    whole = lambda a: pl.BlockSpec(a.shape, lambda i, p: (0,) * a.ndim)
    return pl.pallas_call(
        functools.partial(norm_kernel, heads=heads, bit=bit, base=base),
        grid_spec=pltpu.PrefetchScalarGridSpec(
            num_scalar_prefetch=1,
            grid=(slots,),
            in_specs=[chunk(heads * HD)]
            + [chunk(HD)] * heads
            + [whole(recv), whole(off), chunk(heads), chunk(lw.shape[0], heads), whole(gain)],
            out_specs=[pl.BlockSpec((half, heads * HD), lambda i, p: (i, 0))] * 2,
            scratch_shapes=[pltpu.VMEM((width, heads * HD), BF)],
        ),
        out_shape=[jax.ShapeDtypeStruct((slots * half, heads * HD), BF)] * 2,
        compiler_params=params(),
        name="norm",
        cost_estimate=pl.CostEstimate(flops=300_000_000, bytes_accessed=5_000_000, transcendentals=8192),
    )(pick, acc, *qts, recv, off, cum, lw, gain)


def project_kernel(a_ref, b_ref, wa_ref, wb_ref, *refs):
    out_ref = refs[-1]
    total = dot(a_ref[...], wa_ref[...]) + dot(b_ref[...], wb_ref[...])
    for add in refs[:-1]:
        total = total + add[...].astype(F32)
    out_ref[...] = total.astype(out_ref.dtype)


def project(a, b, wa, wb, slot, rows, col0, cols, adds=(), out=BF, tile=512):
    depth = wa.shape[0]
    tiles = cols // tile
    first = col0 // tile
    left = pl.BlockSpec((rows, depth), lambda j: (slot, 0))
    weight = pl.BlockSpec((depth, tile), lambda j: (0, first + j))
    result = pl.BlockSpec((rows, tile), lambda j: (0, j))
    return pl.pallas_call(
        project_kernel,
        grid=(tiles,),
        in_specs=[left, left, weight, weight] + [result] * len(adds),
        out_specs=result,
        out_shape=jax.ShapeDtypeStruct((rows, cols), out),
        compiler_params=params(),
        name=f"project{slot}",
        cost_estimate=pl.CostEstimate(
            flops=4 * rows * depth * cols, bytes_accessed=4 * depth * cols, transcendentals=0
        ),
    )(a, b, wa, wb, *adds)


def finish_kernel(own_ref, lo1, lo2, hi1, hi2, out_ref):
    half = lo1.shape[1]
    out_ref[:, :half] = (own_ref[:, :half] + lo1[...].astype(F32) + lo2[...].astype(F32)).astype(BF)
    out_ref[:, half:] = (own_ref[:, half:] + hi1[...].astype(F32) + hi2[...].astype(F32)).astype(BF)


def finish(own, lo1, lo2, hi1, hi2):
    vm = pl.BlockSpec(memory_space=pltpu.VMEM)
    return pl.pallas_call(
        finish_kernel,
        in_specs=[vm] * 5,
        out_specs=vm,
        out_shape=jax.ShapeDtypeStruct(own.shape, BF),
        compiler_params=params(),
        name="finish",
        cost_estimate=pl.CostEstimate(flops=2_000_000, bytes_accessed=5_000_000, transcendentals=0),
    )(own, lo1, lo2, hi1, hi2)


def body(queries, keys, values, log_decay, level_weight, norm_gain, out_weight):
    rows, heads, _ = queries.shape
    seq_size, head_size = lax.axis_size("seq"), lax.axis_size("head")
    bits = seq_size.bit_length() - 1
    base = (rows // SPAN).bit_length()
    ring = head_size // 2
    pos = lax.axis_index("seq").astype(jnp.int32)
    lane = lax.axis_index("head").astype(jnp.int32)
    x, core = lane // 2, lane % 2
    pos1 = pos[None]
    pick = jnp.stack([pos, core] + [(x + d) % ring for d in (2, 1, 3, 0)])
    swap = [(i, i ^ 1) for i in range(head_size)]
    up = [(i, (i + 2) % head_size) for i in range(head_size)]
    down = [(i, (i - 2) % head_size) for i in range(head_size)]

    w_other = lax.ppermute(out_weight, "head", swap)
    k2 = keys.reshape(rows, heads * HD)
    v2 = values.reshape(rows, heads * HD)
    q2 = queries.reshape(rows, heads * HD)
    ld = jnp.transpose(log_decay, (1, 0))
    lw = jnp.transpose(level_weight, (2, 1, 0))

    state, pay, cum, tot = summary(ld, k2, v2)
    off = jnp.zeros((heads, 128), F32)
    recvs, offs, accs, qts = [], [], [], []
    for b in range(bits):
        pairs = [(i, i ^ (1 << b)) for i in range(seq_size)]
        if b == bits - 1:
            pairs = [(i, j) for i, j in pairs if i < j]
        recv = lax.ppermute(pay, "seq", pairs)
        recvs.append(recv)
        offs.append(off)
        if b < heads:
            acc, qt = local(q2, k2, v2, cum, lw, b)
            accs.append(acc)
            qts.append(qt)
        if b < bits - 1:
            state, pay, tot, off = merge(pos1, recv, state, tot, off, b)
    acc = far(pos1, accs, qts, recvs[:-1], offs[:-1], cum, lw, base)
    mine, other = norm(pick, acc, qts, recvs[-1], offs[-1], cum, lw, norm_gain, bits - 1, base, ring)
    theirs = lax.ppermute(other, "head", swap)

    depth = out_weight.shape[1]
    half = depth // 2
    part = mine.shape[0] // ring
    proj = functools.partial(project, mine, theirs, out_weight, w_other)
    a_lo = proj(0, part, 0, half)
    from_low = lax.ppermute(a_lo, "head", up)
    a_hi = proj(0, part, half, half)
    from_high = lax.ppermute(a_hi, "head", down)
    p_hi = proj(1, part, half, half)
    hi1 = lax.ppermute(p_hi, "head", up)
    m_lo = proj(2, part, 0, half)
    lo1 = lax.ppermute(m_lo, "head", down)
    own = proj(3, part, 0, depth, out=F32)
    p_lo = proj(1, part, 0, half, adds=(from_low,))
    lo2 = lax.ppermute(p_lo, "head", up)
    m_hi = proj(2, part, half, half, adds=(from_high,))
    hi2 = lax.ppermute(m_hi, "head", down)
    return finish(own, lo1, lo2, hi1, hi2)


def solution(mesh):
    return jax.shard_map(
        body,
        mesh=mesh,
        in_specs=(
            P("seq", "head", None),
            P("seq", "head", None),
            P("seq", "head", None),
            P("seq", "head"),
            P("seq", "head", None),
            P("head", None),
            P("head", None),
        ),
        out_specs=P(("seq", "head"), None),
        check_vma=False,
    )
```

time: 215 us -> 94.9 us (0.44)
  local copies, waits for them, and re-layouts: 50.5 us -> 5.63 us
  Pallas kernels: 0 us -> 40.4 us
  blocking collectives: 37.4 us -> 0 us
  matrix products: 36.6 us -> 0 us
  waiting for transfers between devices: 57.8 us -> 22.6 us
  starting transfers between devices: 0.04 us -> 25.1 us
  other arithmetic: 17.7 us -> 0 us
  between operations: 13.8 us -> 0.26 us
    reduce_scatter x1 -> x0, waiting for transfers between devices: 57.8 us -> none  [body(): lax.psum_scatter(jnp.dot(normed, out_weight, preferred_element_type=jnp.f...]
    pallas_call x0 -> x19, Pallas kernels: none -> 40.4 us  [the longest x7 26.7 us: project(): pl.pallas_call(project_kernel, grid=(tiles,), in_specs=[left, left, weigh...]
    all_gather x1 -> x0, blocking collectives: 37.4 us -> none  [body(): all_totals = lax.all_gather(summary_total[None], 'seq', axis=0, tiled=True)]
    dot_general x9 -> x0, matrix products: 36.6 us -> none  [the longest x4 9.98 us: local_levels(): jnp.einsum('cthd,chde->cthe', query_blocks, picked, preferred_element_typ...]
    ppermute x0 -> x13, starting transfers between devices: none -> 25.1 us  [the longest x5 9.94 us: body(): recv = lax.ppermute(pay, 'seq', pairs)]
    ppermute x0 -> x13, waiting for transfers between devices: none -> 22.6 us  [the longest x5 12.1 us: body(): recv = lax.ppermute(pay, 'seq', pairs)]
    gather x13 -> x0, local copies, waits for them, and re-layouts: 15.1 us -> none  [the longest x4 12 us: local_levels(): picked = blocks[source].astype(jnp.bfloat16)]
    mul x7 -> x0, local copies, waits for them, and re-layouts: 9.5 us -> none  [the longest x4 7.01 us: local_levels(): output = output + factor[:, :, :, None] * readout]
  transfers between devices with their start and end apart: 2 -> 13, of which waited for: 1 -> 8; matrix products, arithmetic and copies ran while one was open for 27% -> 4% of each run, Pallas kernels for 0% -> 38%
where the time goes in v1:
time: 94.9 us; the launch traced here: 94 us
  Pallas kernels  40.4 us (43%)
  starting transfers between devices  25.1 us (26%)
  waiting for transfers between devices  22.6 us (24%)
  local copies, waits for them, and re-layouts  5.63 us (6%)
    pallas_call x7, Pallas kernels, project(): pl.pallas_call(project_kernel, grid=(tiles,), in_specs=[left, left, weigh...  26.7 us
    ppermute x5, waiting for transfers between devices, body(): recv = lax.ppermute(pay, 'seq', pairs)  12.1 us
    ppermute x5, starting transfers between devices, body(): recv = lax.ppermute(pay, 'seq', pairs)  9.94 us
    ppermute x1, waiting for transfers between devices, body(): lo2 = lax.ppermute(p_lo, 'head', up)  7.86 us
    ppermute x1, starting transfers between devices, body(): theirs = lax.ppermute(other, 'head', swap)  4.46 us
    unnamed x17, local copies, waits for them, and re-layouts  3.66 us
    pallas_call x4, Pallas kernels, local(): pl.pallas_call(functools.partial(local_kernel, head=head), grid=(1,), in_...  3.33 us
    ppermute x1, starting transfers between devices, body(): w_other = lax.ppermute(out_weight, 'head', swap)  3.24 us
  transfers between devices with their start and end apart: 13, of which 8 were waited for; matrix products, arithmetic and copies ran while one was open for 4% of the time, Pallas kernels for 38%

profile of v1, /device:TPU:1, one launch (start us, length us, event | category | flops | bytes accessed | tf_op | source)
XLA Modules:
  0.0 94.0 jit_solution(2840877579048838103)
XLA Ops:
  0.0 0.0 copy-start.3
  0.0 3.2 %collective-permute-start.6 = (bf16[512,4096]{1,0:T(8,128)(2,1)}, bf16[512,4096]{1,0:T(8,128)(2,1)}, u32[]{:S(2)}, u32[]{:S(2)}) collective-permute-start(bf16[512,4096]{1,0:T(8,128)(2,1)} %wa_ref.13), channel_id=1, source_target_pairs={{0,1},{1,0},{2,3},{3,2},{4,5},{5,4},{6,7},{7,6},{8,9},{9,8},{10,11... | collective-permute-start | bytes 12582920 | tf_op jit(solution)/shard_map/ppermute | solution.py:336
  3.2 1.9 %copy_bitcast_fusion = (bf16[1024,512]{1,0:T(8,128)(2,1)S(1)}, bf16[1024,512]{1,0:T(8,128)(2,1)S(1)}) fusion(bf16[128,8,4,128]{3,2,1,0:T(4,128)(2,1)} %bitcast.30, bf16[128,8,4,128]{3,2,1,0:T(4,128)(2,1)} %bitcast.31), kind=kLoop, calls=%fused_computation | loop fusion | bytes 4194304 | tf_op jit(solution)/shard_map/reshape | solution.py:338
  5.1 0.0 copy-done.3
  5.1 2.9 %summary.1 = (f32[512,128]{1,0:T(8,128)S(1)}, bf16[528,128]{1,0:T(8,128)(2,1)}, f32[4,1024]{1,0:T(4,128)S(1)}, f32[4,128]{1,0:T(4,128)S(1)}) custom-call(f32[4,1024]{1,0:T(4,128)S(1)} %bitcast.28, bf16[1024,512]{1,0:T(8,128)(2,1)S(1)} %get-tuple-element.62.k_ref, bf16[1024,512]{1,0:T(8,128)(2,1)S(1)} %get-tuple-element.61.v_ref), custom_call_target="tpu_custom_call" | custom-call | flops 140000000 | bytes 3000000 | tf_op jit(solution)/shard_map/summary/pallas_call | solution.py:74
  8.0 0.0 copy-start.4
  8.0 0.6 copy-done.4
  8.6 0.0 collective-permute-start
  8.6 1.4 %copy.14 = bf16[128,8,4,128]{3,1,2,0:T(8,128)(2,1)S(1)} copy(bf16[128,8,4,128]{3,2,1,0:T(4,128)(2,1)} %bitcast.29) | data formatting | bytes 2097152
  10.1 0.1 stack.27.pick_ref
  10.2 0.0 copy-start.1
  10.2 0.9 copy-done.1
  11.1 0.0 copy-start.5
  11.1 0.7 copy-done.5
  11.8 0.0 copy-start.2
  11.8 0.0 copy-start.6
  11.8 0.8 local3.1
  12.6 1.4 %collective-permute-done.recv_ref.refs_8_ = bf16[528,128]{1,0:T(8,128)(2,1)S(1)} collective-permute-done((bf16[528,128]{1,0:T(8,128)(2,1)}, bf16[528,128]{1,0:T(8,128)(2,1)S(1)}, u32[]{:S(2)}, u32[]{:S(2)}) %collective-permute-start) | collective-permute-done | bytes 135200 | tf_op jit(solution)/shard_map/ppermute | solution.py:350
  14.0 0.1 merge0.1
  14.1 1.3 %collective-permute-start.1 = (bf16[528,128]{1,0:T(8,128)(2,1)S(1)}, bf16[528,128]{1,0:T(8,128)(2,1)S(1)}, u32[]{:S(2)}, u32[]{:S(2)}) collective-permute-start(bf16[528,128]{1,0:T(8,128)(2,1)S(1)} %get-tuple-element.45), channel_id=1, source_target_pairs={{0,16},{8,24},{16,0},{24,8},{32,48},{40,56},{48,32},{56,40},{64,80... | collective-permute-start | bytes 405512 | tf_op jit(solution)/shard_map/ppermute | solution.py:350
  15.4 0.0 copy-done.2
  15.4 0.0 copy-done.6
  15.4 0.8 local2.1
  16.2 3.8 %collective-permute-done.1.recv_ref.refs_9_ = bf16[528,128]{1,0:T(8,128)(2,1)S(1)} collective-permute-done((bf16[528,128]{1,0:T(8,128)(2,1)S(1)}, bf16[528,128]{1,0:T(8,128)(2,1)S(1)}, u32[]{:S(2)}, u32[]{:S(2)}) %collective-permute-start.1) | collective-permute-done | bytes 135200 | tf_op jit(solution)/shard_map/ppermute | solution.py:350
  20.0 0.1 merge1.1
  20.1 0.1 collective-permute-start.2
  20.2 0.8 local1.1
  21.0 3.0 %collective-permute-done.2.recv_ref.refs_10_ = bf16[528,128]{1,0:T(8,128)(2,1)S(1)} collective-permute-done((bf16[528,128]{1,0:T(8,128)(2,1)S(1)}, bf16[528,128]{1,0:T(8,128)(2,1)S(1)}, u32[]{:S(2)}, u32[]{:S(2)}) %collective-permute-start.2) | collective-permute-done | bytes 135200 | tf_op jit(solution)/shard_map/ppermute | solution.py:350
  24.0 0.1 merge2.1
  24.1 1.5 %collective-permute-start.3 = (bf16[528,128]{1,0:T(8,128)(2,1)S(1)}, bf16[528,128]{1,0:T(8,128)(2,1)S(1)}, u32[]{:S(2)}, u32[]{:S(2)}) collective-permute-start(bf16[528,128]{1,0:T(8,128)(2,1)S(1)} %get-tuple-element.53), channel_id=1, source_target_pairs={{0,64},{8,72},{16,80},{24,88},{32,96},{40,104},{48,112},{56,120},{... | collective-permute-start | bytes 405512 | tf_op jit(solution)/shard_map/ppermute | solution.py:350
  25.6 0.8 local0.1
  26.4 0.0 copy-start.7
  26.4 3.9 %collective-permute-done.3.refs_11_.recv_ref = bf16[528,128]{1,0:T(8,128)(2,1)S(1)} collective-permute-done((bf16[528,128]{1,0:T(8,128)(2,1)S(1)}, bf16[528,128]{1,0:T(8,128)(2,1)S(1)}, u32[]{:S(2)}, u32[]{:S(2)}) %collective-permute-start.3) | collective-permute-done | bytes 135200 | tf_op jit(solution)/shard_map/ppermute | solution.py:350
  30.4 0.8 merge3.1
  31.1 7.1 %collective-permute-start.4 = (bf16[528,128]{1,0:T(8,128)(2,1)S(1)}, bf16[528,128]{1,0:T(8,128)(2,1)S(1)}, u32[]{:S(2)}, u32[]{:S(2)}) collective-permute-start(bf16[528,128]{1,0:T(8,128)(2,1)S(1)} %get-tuple-element.57), channel_id=1, source_target_pairs={{0,128},{8,136},{16,144},{24,152},{32,160},{40,168},{48,176},{56,1... | collective-permute-start | bytes 405512 | tf_op jit(solution)/shard_map/ppermute | solution.py:350
  38.2 0.0 copy-start
  38.2 2.4 %far.1.refs_0_ = f32[512,1024]{1,0:T(8,128)S(1)} custom-call(s32[1]{0:T(128)} %bitcast.pos_ref, f32[128,1024]{1,0:T(8,128)S(1)} %get-tuple-element.34.refs_0_, f32[128,1024]{1,0:T(8,128)S(1)} %get-tuple-element.35.refs_1_, f32[128,1024]{1,0:T(8,128)S(1)} %get-tuple-element.36.refs_2_, f32[128,1024]{1,0:T(8,128)S(1)} %get-tuple-element.37.refs_3_, ...), custom_call_target="tpu_custom_call" | custom-call | flops 2000000000 | bytes 6000000 | tf_op jit(solution)/shard_map/far/pallas_call | solution.py:216
  40.6 0.0 collective-permute-done.4.refs_5_
  40.6 0.0 copy-done.7
  40.6 2.9 %norm.1 = (bf16[512,512]{1,0:T(8,128)(2,1)S(1)}, bf16[512,512]{1,0:T(8,128)(2,1)S(1)}) custom-call(s32[6]{0:T(128)S(1)} %stack.27.pick_ref, f32[512,1024]{1,0:T(8,128)S(1)} %far.1.refs_0_, bf16[128,1024]{1,0:T(8,128)(2,1)S(1)} %get-tuple-element.38.refs_4_.refs_1_, bf16[128,1024]{1,0:T(8,128)(2,1)S(1)} %get-tuple-element.39.refs_5_.refs_2_, ...), custom_call_target="tpu_custom_call" | custom-call | flops 300000000 | bytes 5000000 | tf_op jit(solution)/shard_map/norm/pallas_call | solution.py:255
  43.5 4.5 %collective-permute-start.5 = (bf16[512,512]{1,0:T(8,128)(2,1)S(1)}, bf16[512,512]{1,0:T(8,128)(2,1)S(1)}, u32[]{:S(2)}, u32[]{:S(2)}) collective-permute-start(bf16[512,512]{1,0:T(8,128)(2,1)S(1)} %get-tuple-element.60), channel_id=1, source_target_pairs={{0,1},{1,0},{2,3},{3,2},{4,5},{5,4},{6,7},{7,6},{8,9},{9,8},{10,11... | collective-permute-start | bytes 1572872 | tf_op jit(solution)/shard_map/ppermute | solution.py:361
  48.0 1.5 %collective-permute-done.5.b_ref = bf16[512,512]{1,0:T(8,128)(2,1)S(1)} collective-permute-done((bf16[512,512]{1,0:T(8,128)(2,1)S(1)}, bf16[512,512]{1,0:T(8,128)(2,1)S(1)}, u32[]{:S(2)}, u32[]{:S(2)}) %collective-permute-start.5) | collective-permute-done | bytes 524320 | tf_op jit(solution)/shard_map/ppermute | solution.py:361
  49.5 0.0 collective-permute-done.6.wb_ref
  49.5 0.0 copy-done
  49.5 3.2 %project0.2 = bf16[128,2048]{1,0:T(8,128)(2,1)S(1)} custom-call(bf16[512,512]{1,0:T(8,128)(2,1)S(1)} %get-tuple-element.59.a_ref, bf16[512,512]{1,0:T(8,128)(2,1)S(1)} %collective-permute-done.5.b_ref, bf16[512,4096]{1,0:T(8,128)(2,1)S(1)} %copy-done, bf16[512,4096]{1,0:T(8,128)(2,1)} %collective-permute-done.6.wb_ref), custom_call_target="tpu_custom_call" | custom-call | flops 536870912 | bytes 4194304 | tf_op jit(solution)/shard_map/project0/pallas_call | solution.py:288
  52.8 1.3 %collective-permute-start.8 = (bf16[128,2048]{1,0:T(8,128)(2,1)S(1)}, bf16[128,2048]{1,0:T(8,128)(2,1)S(1)}, u32[]{:S(2)}, u32[]{:S(2)}) collective-permute-start(bf16[128,2048]{1,0:T(8,128)(2,1)S(1)} %project0.2), channel_id=1, source_target_pairs={{0,2},{1,3},{2,4},{3,5},{4,6},{5,7},{6,0},{7,1},{8,10},{9,11},{10,... | collective-permute-start | bytes 1572872 | tf_op jit(solution)/shard_map/ppermute | solution.py:368
  54.1 3.2 %project0.3 = bf16[128,2048]{1,0:T(8,128)(2,1)S(1)} custom-call(bf16[512,512]{1,0:T(8,128)(2,1)S(1)} %get-tuple-element.59.a_ref, bf16[512,512]{1,0:T(8,128)(2,1)S(1)} %collective-permute-done.5.b_ref, bf16[512,4096]{1,0:T(8,128)(2,1)S(1)} %copy-done, bf16[512,4096]{1,0:T(8,128)(2,1)} %collective-permute-done.6.wb_ref), custom_call_target="tpu_custom_call" | custom-call | flops 536870912 | bytes 4194304 | tf_op jit(solution)/shard_map/project0/pallas_call | solution.py:288
  57.3 1.5 %collective-permute-start.11 = (bf16[128,2048]{1,0:T(8,128)(2,1)S(1)}, bf16[128,2048]{1,0:T(8,128)(2,1)S(1)}, u32[]{:S(2)}, u32[]{:S(2)}) collective-permute-start(bf16[128,2048]{1,0:T(8,128)(2,1)S(1)} %project0.3), channel_id=1, source_target_pairs={{0,6},{1,7},{2,0},{3,1},{4,2},{5,3},{6,4},{7,5},{8,14},{9,15},{10,... | collective-permute-start | bytes 1572872 | tf_op jit(solution)/shard_map/ppermute | solution.py:370
  58.8 3.2 %project2.2 = bf16[128,2048]{1,0:T(8,128)(2,1)S(1)} custom-call(bf16[512,512]{1,0:T(8,128)(2,1)S(1)} %get-tuple-element.59.a_ref, bf16[512,512]{1,0:T(8,128)(2,1)S(1)} %collective-permute-done.5.b_ref, bf16[512,4096]{1,0:T(8,128)(2,1)S(1)} %copy-done, bf16[512,4096]{1,0:T(8,128)(2,1)} %collective-permute-done.6.wb_ref), custom_call_target="tpu_custom_call" | custom-call | flops 536870912 | bytes 4194304 | tf_op jit(solution)/shard_map/project2/pallas_call | solution.py:288
  62.1 1.4 %collective-permute-start.7 = (bf16[128,2048]{1,0:T(8,128)(2,1)S(1)}, bf16[128,2048]{1,0:T(8,128)(2,1)S(1)}, u32[]{:S(2)}, u32[]{:S(2)}) collective-permute-start(bf16[128,2048]{1,0:T(8,128)(2,1)S(1)} %project2.2), channel_id=1, source_target_pairs={{0,6},{1,7},{2,0},{3,1},{4,2},{5,3},{6,4},{7,5},{8,14},{9,15},{10,... | collective-permute-start | bytes 1572872 | tf_op jit(solution)/shard_map/ppermute | solution.py:374
  63.5 3.2 %project1.3 = bf16[128,2048]{1,0:T(8,128)(2,1)S(1)} custom-call(bf16[512,512]{1,0:T(8,128)(2,1)S(1)} %get-tuple-element.59.a_ref, bf16[512,512]{1,0:T(8,128)(2,1)S(1)} %collective-permute-done.5.b_ref, bf16[512,4096]{1,0:T(8,128)(2,1)S(1)} %copy-done, bf16[512,4096]{1,0:T(8,128)(2,1)} %collective-permute-done.6.wb_ref), custom_call_target="tpu_custom_call" | custom-call | flops 536870912 | bytes 4194304 | tf_op jit(solution)/shard_map/project1/pallas_call | solution.py:288
  66.7 0.4 collective-permute-start.10
  67.1 0.1 collective-permute-done.8.refs_0_
  67.2 3.5 %project1.2 = bf16[128,2048]{1,0:T(8,128)(2,1)S(1)} custom-call(bf16[512,512]{1,0:T(8,128)(2,1)S(1)} %get-tuple-element.59.a_ref, bf16[512,512]{1,0:T(8,128)(2,1)S(1)} %collective-permute-done.5.b_ref, bf16[512,4096]{1,0:T(8,128)(2,1)} %wa_ref.13, bf16[512,4096]{1,0:T(8,128)(2,1)} %collective-permute-done.6.wb_ref, ...), custom_call_target="tpu_custom_call" | custom-call | flops 536870912 | bytes 4194304 | tf_op jit(solution)/shard_map/project1/pallas_call | solution.py:288
  70.7 0.1 collective-permute-start.9
  70.8 0.0 collective-permute-done.11.refs_0_
  70.8 3.5 %project2.3 = bf16[128,2048]{1,0:T(8,128)(2,1)S(1)} custom-call(bf16[512,512]{1,0:T(8,128)(2,1)S(1)} %get-tuple-element.59.a_ref, bf16[512,512]{1,0:T(8,128)(2,1)S(1)} %collective-permute-done.5.b_ref, bf16[512,4096]{1,0:T(8,128)(2,1)} %wa_ref.13, bf16[512,4096]{1,0:T(8,128)(2,1)} %collective-permute-done.6.wb_ref, ...), custom_call_target="tpu_custom_call" | custom-call | flops 536870912 | bytes 4194304 | tf_op jit(solution)/shard_map/project2/pallas_call | solution.py:288
  74.3 2.7 %collective-permute-start.12 = (bf16[128,2048]{1,0:T(8,128)(2,1)S(1)}, bf16[128,2048]{1,0:T(8,128)(2,1)S(1)}, u32[]{:S(2)}, u32[]{:S(2)}) collective-permute-start(bf16[128,2048]{1,0:T(8,128)(2,1)S(1)} %project2.3), channel_id=1, source_target_pairs={{0,6},{1,7},{2,0},{3,1},{4,2},{5,3},{6,4},{7,5},{8,14},{9,15},{10,... | collective-permute-start | bytes 1572872 | tf_op jit(solution)/shard_map/ppermute | solution.py:379
  77.0 6.7 %project3.1.own_ref = f32[128,4096]{1,0:T(8,128)S(1)} custom-call(bf16[512,512]{1,0:T(8,128)(2,1)S(1)} %get-tuple-element.59.a_ref, bf16[512,512]{1,0:T(8,128)(2,1)S(1)} %collective-permute-done.5.b_ref, bf16[512,4096]{1,0:T(8,128)(2,1)} %wa_ref.13, bf16[512,4096]{1,0:T(8,128)(2,1)} %collective-permute-done.6.wb_ref), custom_call_target="tpu_custom_call" | custom-call | flops 1073741824 | bytes 8388608 | tf_op jit(solution)/shard_map/project3/pallas_call | solution.py:288
  83.7 0.0 collective-permute-done.7.lo1
  83.8 0.0 collective-permute-done.10.hi1
  83.8 7.9 %collective-permute-done.9.lo2 = bf16[128,2048]{1,0:T(8,128)(2,1)S(1)} collective-permute-done((bf16[128,2048]{1,0:T(8,128)(2,1)S(1)}, bf16[128,2048]{1,0:T(8,128)(2,1)S(1)}, u32[]{:S(2)}, u32[]{:S(2)}) %collective-permute-start.9) | collective-permute-done | bytes 524320 | tf_op jit(solution)/shard_map/ppermute | solution.py:377
  91.6 1.1 %collective-permute-done.12.hi2 = bf16[128,2048]{1,0:T(8,128)(2,1)S(1)} collective-permute-done((bf16[128,2048]{1,0:T(8,128)(2,1)S(1)}, bf16[128,2048]{1,0:T(8,128)(2,1)S(1)}, u32[]{:S(2)}, u32[]{:S(2)}) %collective-permute-start.12) | collective-permute-done | bytes 524320 | tf_op jit(solution)/shard_map/ppermute | solution.py:379
  92.7 1.3 %finish.1 = bf16[128,4096]{1,0:T(8,128)(2,1)} custom-call(f32[128,4096]{1,0:T(8,128)S(1)} %project3.1.own_ref, bf16[128,2048]{1,0:T(8,128)(2,1)S(1)} %collective-permute-done.7.lo1, bf16[128,2048]{1,0:T(8,128)(2,1)S(1)} %collective-permute-done.9.lo2, bf16[128,2048]{1,0:T(8,128)(2,1)S(1)} %collective-permute-done.10.hi1, ...), custom_call_target="tpu_custom_call" | custom-call | flops 2000000 | bytes 5000000 | tf_op jit(solution)/shard_map/finish/pallas_call | solution.py:310
  (1 shorter events, 0.0 us)
Async XLA Ops:
  0.0 5.1 %copy-start.3 = (f32[1024,4]{0,1:T(4,128)S(1)}, f32[1024,4]{0,1:T(4,128)}, u32[]{:S(2)}) copy-start(f32[1024,4]{0,1:T(4,128)} %param.10) | copy-start | bytes 49156
  0.0 49.5 %collective-permute-start.6 = (bf16[512,4096]{1,0:T(8,128)(2,1)}, bf16[512,4096]{1,0:T(8,128)(2,1)}, u32[]{:S(2)}, u32[]{:S(2)}) collective-permute-start(bf16[512,4096]{1,0:T(8,128)(2,1)} %wa_ref.13), channel_id=1, source_target_pairs={{0,1},{1,0},{2,3},{3,2},{4,5},{5,4},{6,7},{7,6},{8,9},{9,8},{10,11... | collective-permute-start | bytes 12582920 | tf_op jit(solution)/shard_map/ppermute | solution.py:336
  8.0 0.6 copy-start.4
  8.6 5.4 %collective-permute-start = (bf16[528,128]{1,0:T(8,128)(2,1)}, bf16[528,128]{1,0:T(8,128)(2,1)S(1)}, u32[]{:S(2)}, u32[]{:S(2)}) collective-permute-start(bf16[528,128]{1,0:T(8,128)(2,1)} %get-tuple-element.42), channel_id=1, source_target_pairs={{0,8},{8,0},{16,24},{24,16},{32,40},{40,32},{48,56},{56,48},{64,72... | collective-permute-start | bytes 405512 | tf_op jit(solution)/shard_map/ppermute | solution.py:350
  10.2 0.9 copy-start.1
  11.1 0.7 copy-start.5
  11.8 3.6 %copy-start.2 = (f32[1024,4,10]{0,1,2:T(4,128)S(1)}, f32[1024,4,10]{0,1,2:T(4,128)}, u32[]{:S(2)}) copy-start(f32[1024,4,10]{0,1,2:T(4,128)} %param.11) | copy-start | bytes 491524
  11.8 3.6 %copy-start.6 = (f32[4,1024]{1,0:T(4,128)S(1)}, f32[4,1024]{1,0:T(4,128)}, u32[]{:S(2)}) copy-start(f32[4,1024]{1,0:T(4,128)} %copy-done.4) | copy-start | bytes 49156
  14.1 5.9 %collective-permute-start.1 = (bf16[528,128]{1,0:T(8,128)(2,1)S(1)}, bf16[528,128]{1,0:T(8,128)(2,1)S(1)}, u32[]{:S(2)}, u32[]{:S(2)}) collective-permute-start(bf16[528,128]{1,0:T(8,128)(2,1)S(1)} %get-tuple-element.45), channel_id=1, source_target_pairs={{0,16},{8,24},{16,0},{24,8},{32,48},{40,56},{48,32},{56,40},{64,80... | collective-permute-start | bytes 405512 | tf_op jit(solution)/shard_map/ppermute | solution.py:350
  20.1 3.9 %collective-permute-start.2 = (bf16[528,128]{1,0:T(8,128)(2,1)S(1)}, bf16[528,128]{1,0:T(8,128)(2,1)S(1)}, u32[]{:S(2)}, u32[]{:S(2)}) collective-permute-start(bf16[528,128]{1,0:T(8,128)(2,1)S(1)} %get-tuple-element.49), channel_id=1, source_target_pairs={{0,32},{8,40},{16,48},{24,56},{32,0},{40,8},{48,16},{56,24},{64,96... | collective-permute-start | bytes 405512 | tf_op jit(solution)/shard_map/ppermute | solution.py:350
  24.1 6.3 %collective-permute-start.3 = (bf16[528,128]{1,0:T(8,128)(2,1)S(1)}, bf16[528,128]{1,0:T(8,128)(2,1)S(1)}, u32[]{:S(2)}, u32[]{:S(2)}) collective-permute-start(bf16[528,128]{1,0:T(8,128)(2,1)S(1)} %get-tuple-element.53), channel_id=1, source_target_pairs={{0,64},{8,72},{16,80},{24,88},{32,96},{40,104},{48,112},{56,120},{... | collective-permute-start | bytes 405512 | tf_op jit(solution)/shard_map/ppermute | solution.py:350
  26.4 14.2 %copy-start.7 = (f32[4,128]{1,0:T(4,128)S(1)}, f32[4,128]{1,0:T(4,128)}, u32[]{:S(2)}) copy-start(f32[4,128]{1,0:T(4,128)} %refs_9_.1) | copy-start | bytes 6148
  31.1 9.5 %collective-permute-start.4 = (bf16[528,128]{1,0:T(8,128)(2,1)S(1)}, bf16[528,128]{1,0:T(8,128)(2,1)S(1)}, u32[]{:S(2)}, u32[]{:S(2)}) collective-permute-start(bf16[528,128]{1,0:T(8,128)(2,1)S(1)} %get-tuple-element.57), channel_id=1, source_target_pairs={{0,128},{8,136},{16,144},{24,152},{32,160},{40,168},{48,176},{56,1... | collective-permute-start | bytes 405512 | tf_op jit(solution)/shard_map/ppermute | solution.py:350
  38.2 11.3 %copy-start = (bf16[512,4096]{1,0:T(8,128)(2,1)S(1)}, bf16[512,4096]{1,0:T(8,128)(2,1)}, u32[]{:S(2)}) copy-start(bf16[512,4096]{1,0:T(8,128)(2,1)} %wa_ref.13) | copy-start | bytes 12582916
  43.5 6.0 %collective-permute-start.5 = (bf16[512,512]{1,0:T(8,128)(2,1)S(1)}, bf16[512,512]{1,0:T(8,128)(2,1)S(1)}, u32[]{:S(2)}, u32[]{:S(2)}) collective-permute-start(bf16[512,512]{1,0:T(8,128)(2,1)S(1)} %get-tuple-element.60), channel_id=1, source_target_pairs={{0,1},{1,0},{2,3},{3,2},{4,5},{5,4},{6,7},{7,6},{8,9},{9,8},{10,11... | collective-permute-start | bytes 1572872 | tf_op jit(solution)/shard_map/ppermute | solution.py:361
  52.8 14.4 %collective-permute-start.8 = (bf16[128,2048]{1,0:T(8,128)(2,1)S(1)}, bf16[128,2048]{1,0:T(8,128)(2,1)S(1)}, u32[]{:S(2)}, u32[]{:S(2)}) collective-permute-start(bf16[128,2048]{1,0:T(8,128)(2,1)S(1)} %project0.2), channel_id=1, source_target_pairs={{0,2},{1,3},{2,4},{3,5},{4,6},{5,7},{6,0},{7,1},{8,10},{9,11},{10,... | collective-permute-start | bytes 1572872 | tf_op jit(solution)/shard_map/ppermute | solution.py:368
  57.3 13.5 %collective-permute-start.11 = (bf16[128,2048]{1,0:T(8,128)(2,1)S(1)}, bf16[128,2048]{1,0:T(8,128)(2,1)S(1)}, u32[]{:S(2)}, u32[]{:S(2)}) collective-permute-start(bf16[128,2048]{1,0:T(8,128)(2,1)S(1)} %project0.3), channel_id=1, source_target_pairs={{0,6},{1,7},{2,0},{3,1},{4,2},{5,3},{6,4},{7,5},{8,14},{9,15},{10,... | collective-permute-start | bytes 1572872 | tf_op jit(solution)/shard_map/ppermute | solution.py:370
  62.1 21.7 %collective-permute-start.7 = (bf16[128,2048]{1,0:T(8,128)(2,1)S(1)}, bf16[128,2048]{1,0:T(8,128)(2,1)S(1)}, u32[]{:S(2)}, u32[]{:S(2)}) collective-permute-start(bf16[128,2048]{1,0:T(8,128)(2,1)S(1)} %project2.2), channel_id=1, source_target_pairs={{0,6},{1,7},{2,0},{3,1},{4,2},{5,3},{6,4},{7,5},{8,14},{9,15},{10,... | collective-permute-start | bytes 1572872 | tf_op jit(solution)/shard_map/ppermute | solution.py:374
  66.7 17.1 %collective-permute-start.10 = (bf16[128,2048]{1,0:T(8,128)(2,1)S(1)}, bf16[128,2048]{1,0:T(8,128)(2,1)S(1)}, u32[]{:S(2)}, u32[]{:S(2)}) collective-permute-start(bf16[128,2048]{1,0:T(8,128)(2,1)S(1)} %project1.3), channel_id=1, source_target_pairs={{0,2},{1,3},{2,4},{3,5},{4,6},{5,7},{6,0},{7,1},{8,10},{9,11},{10,... | collective-permute-start | bytes 1572872 | tf_op jit(solution)/shard_map/ppermute | solution.py:372
  70.7 20.9 %collective-permute-start.9 = (bf16[128,2048]{1,0:T(8,128)(2,1)S(1)}, bf16[128,2048]{1,0:T(8,128)(2,1)S(1)}, u32[]{:S(2)}, u32[]{:S(2)}) collective-permute-start(bf16[128,2048]{1,0:T(8,128)(2,1)S(1)} %project1.2), channel_id=1, source_target_pairs={{0,2},{1,3},{2,4},{3,5},{4,6},{5,7},{6,0},{7,1},{8,10},{9,11},{10,... | collective-permute-start | bytes 1572872 | tf_op jit(solution)/shard_map/ppermute | solution.py:377
  74.3 18.4 %collective-permute-start.12 = (bf16[128,2048]{1,0:T(8,128)(2,1)S(1)}, bf16[128,2048]{1,0:T(8,128)(2,1)S(1)}, u32[]{:S(2)}, u32[]{:S(2)}) collective-permute-start(bf16[128,2048]{1,0:T(8,128)(2,1)S(1)} %project2.3), channel_id=1, source_target_pairs={{0,6},{1,7},{2,0},{3,1},{4,2},{5,3},{6,4},{7,5},{8,14},{9,15},{10,... | collective-permute-start | bytes 1572872 | tf_op jit(solution)/shard_map/ppermute | solution.py:379

commit v2 on v0

v2 whole, which is shorter than its diff:
```python
import functools
import jax
import jax.numpy as jnp
from jax import lax
from jax.experimental import pallas as pl
from jax.experimental.pallas import tpu as pltpu
from jax.sharding import PartitionSpec as P

SPAN = 64
HD = 128
BF = jnp.bfloat16
F32 = jnp.float32
VMEM_LIMIT = 16 * 1024 * 1024
VM = pl.BlockSpec(memory_space=pltpu.VMEM)
SM = pl.BlockSpec(memory_space=pltpu.SMEM)


def call(kernel, name, ins, outs, args, scratch=(), flops=0, moved=0, **kw):
    return pl.pallas_call(
        kernel,
        in_specs=ins,
        out_specs=[VM] * len(outs),
        out_shape=[jax.ShapeDtypeStruct(shape, dtype) for shape, dtype in outs],
        scratch_shapes=list(scratch),
        compiler_params=pltpu.CompilerParams(vmem_limit_bytes=VMEM_LIMIT),
        cost_estimate=pl.CostEstimate(flops=flops, bytes_accessed=moved, transcendentals=0),
        name=name,
        **kw,
    )(*args)


def dot(a, b):
    return jnp.dot(a, b, preferred_element_type=F32)


def lane_cumsum(x):
    lanes = lax.broadcasted_iota(jnp.int32, (x.shape[0], 128), 1)
    carry = jnp.zeros((x.shape[0], 1), F32)
    chunks = []
    for i in range(x.shape[1] // 128):
        c = x[:, i * 128 : (i + 1) * 128]
        step = 1
        while step < 128:
            c = c + jnp.where(lanes >= step, pltpu.roll(c, step, 1), 0.0)
            step *= 2
        chunks.append(c)
    out = []
    for c in chunks:
        out.append(c + carry)
        carry = carry + c[:, 127:128]
    return jnp.concatenate(out, axis=1)


def total_rows(total):
    high = total.astype(BF).astype(F32)
    mid = (total - high).astype(BF).astype(F32)
    low = total - high - mid
    rows = jnp.concatenate([high, mid, low, jnp.zeros_like(low)], axis=0)
    return rows.astype(BF)


def total_of(ref, heads):
    rows = ref[heads * HD :, :].astype(F32)
    return rows[:heads] + rows[heads : 2 * heads] + rows[2 * heads : 3 * heads]


def summary_kernel(ld_ref, k_ref, v_ref, pay_ref, cum_ref):
    heads = ld_ref.shape[0]
    cum = lane_cumsum(ld_ref[...])
    total = cum[:, -1:]
    cum_ref[...] = cum
    weight = jnp.exp(total - cum)
    pay_ref[heads * HD :, :] = total_rows(jnp.broadcast_to(total, (heads, 128)))
    for h in range(heads):
        at = slice(h * HD, (h + 1) * HD)
        vt = v_ref[:, at].astype(F32).T * weight[h : h + 1]
        pay_ref[at, :] = dot(vt.astype(BF), k_ref[:, at]).astype(BF)


def summary(ld, k, v):
    heads, rows = ld.shape
    return call(
        summary_kernel,
        "summary",
        [VM, VM, VM],
        [((heads * HD + 16, 128), BF), ((heads, rows), F32)],
        (ld, k, v),
        flops=140_000_000,
        moved=2_000_000,
    )


def merge_kernel(pos_ref, after_ref, recv_ref, self_ref, off_ref, pay_out, off_out, *, bit):
    heads = off_ref.shape[0]
    right = ((pos_ref[0] >> bit) & 1).astype(F32)
    there = total_of(recv_ref, heads)
    here = total_of(self_ref, heads)
    off_out[...] = off_ref[...] + right * there
    pay_out[heads * HD :, :] = total_rows(here + there)
    keep = right + (1.0 - right) * jnp.exp(there)
    take = (1.0 - right) + right * jnp.exp(here)
    for h in range(heads):
        block = slice(h * HD, (h + 1) * HD)
        state = self_ref[block, :].astype(F32) * keep[h : h + 1] + recv_ref[block, :].astype(F32) * take[h : h + 1]
        pay_out[block, :] = state.astype(BF)


def merge(pos, after, recv, pay, off, bit):
    return call(
        functools.partial(merge_kernel, bit=bit),
        f"merge{bit}",
        [SM, VM, VM, VM, VM],
        [(pay.shape, BF), (off.shape, F32)],
        (pos, after, recv, pay, off),
        flops=200_000,
        moved=600_000,
    )


def local_kernel(q_ref, k_ref, v_ref, cum_ref, lw_ref, acc_ref, qt_ref):
    heads, rows = cum_ref.shape
    pair = 2 * SPAN
    s_pos = lax.broadcasted_iota(jnp.int32, (pair, pair), 0)
    t_pos = lax.broadcasted_iota(jnp.int32, (pair, pair), 1)
    same = jnp.logical_and(s_pos <= t_pos, (s_pos >= SPAN) == (t_pos >= SPAN))
    cross = jnp.logical_and(s_pos < SPAN, t_pos >= SPAN)
    for h in range(heads):
        head = slice(h * HD, (h + 1) * HD)
        qt_ref[head, :] = q_ref[:, head].astype(F32).T.astype(BF)
        vt = v_ref[:, head].astype(F32).T
        cum = cum_ref[h : h + 1, :]
        weight = lambda level: lw_ref[level, h : h + 1, :]
        for i in range(rows // pair):
            at = slice(i * pair, (i + 1) * pair)
            middle = cum[:, i * pair + SPAN - 1 : i * pair + SPAN]
            grow = jnp.exp(cum[:, at] - middle)
            scores = dot(k_ref[at, head], qt_ref[head, at])
            probs = scores * jnp.where(same, weight(0)[:, at], jnp.where(cross, weight(1)[:, at], 0.0))
            held = (vt[:, at] * jnp.exp(middle - cum[:, at])).astype(BF)
            acc_ref[head, at] = dot(held, probs.astype(BF)) * grow
        level, half = 2, pair
        while half < rows:
            for i in range(rows // (2 * half)):
                left = slice(2 * i * half, (2 * i + 1) * half)
                right = slice((2 * i + 1) * half, (2 * i + 2) * half)
                end = cum[:, left.stop - 1 : left.stop]
                held = (vt[:, left] * jnp.exp(end - cum[:, left])).astype(BF)
                bucket = dot(held, k_ref[left, head]).astype(BF)
                factor = weight(level)[:, right] * jnp.exp(cum[:, right] - end)
                acc_ref[head, right] += dot(bucket, qt_ref[head, right]) * factor
            level, half = level + 1, half * 2


def local(q, k, v, cum, lw):
    heads, rows = cum.shape
    return call(
        local_kernel,
        "local",
        [VM] * 5,
        [((heads * HD, rows), F32), ((heads * HD, rows), BF)],
        (q, k, v, cum, lw),
        flops=2_000_000_000,
        moved=8_000_000,
    )


def far_factor(pos_ref, off_ref, cum, weight, head, bit):
    flag = ((pos_ref[0] >> bit) & 1).astype(F32)
    return weight * jnp.exp(off_ref[head : head + 1, :1] + cum) * flag


def far_kernel(pos_ref, acc_ref, qt_ref, recv_ref, off_ref, cum_ref, lw_ref, out_ref, *, bit, base):
    heads, rows = cum_ref.shape
    width = min(256, rows)
    for h in range(heads):
        head = slice(h * HD, (h + 1) * HD)
        for i in range(rows // width):
            at = slice(i * width, (i + 1) * width)
            factor = far_factor(pos_ref, off_ref, cum_ref[h : h + 1, at], lw_ref[base + bit, h : h + 1, at], h, bit)
            out_ref[head, at] = acc_ref[head, at] + dot(recv_ref[head, :], qt_ref[head, at]) * factor


def far(pos, acc, qt, recv, off, cum, lw, bit, base):
    return call(
        functools.partial(far_kernel, bit=bit, base=base),
        f"far{bit}",
        [SM] + [VM] * 6,
        [(acc.shape, F32)],
        (pos, acc, qt, recv, off, cum, lw),
        flops=300_000_000,
        moved=3_000_000,
        input_output_aliases={1: 0},
    )[0]


def norm_kernel(pick_ref, acc_ref, qt_ref, recv_ref, off_ref, cum_ref, lw_ref, gain_ref, near_ref, side_ref, own_ref, *, bit, base):
    heads = gain_ref.shape[0]
    core = pick_ref[1]
    size = own_ref.shape[0] // 2
    targets = (((near_ref, 0), (side_ref, 0)), ((near_ref, 1),), ((side_ref, 1),), ((own_ref, 0),))
    for i, outs in enumerate(targets):
        start = pick_ref[3 + i] * (2 * size)
        for part, offset in enumerate((core * size, (1 - core) * size)):
            at = pl.ds(pl.multiple_of(start + offset, size), size)
            for h in range(heads):
                head = slice(h * HD, (h + 1) * HD)
                factor = far_factor(pick_ref, off_ref, cum_ref[h : h + 1, at], lw_ref[base + bit, h : h + 1, at], h, bit)
                att = acc_ref[head, at] + dot(recv_ref[head, :], qt_ref[head, at]) * factor
                mean = jnp.mean(att * att, axis=0, keepdims=True)
                normed = ((att * lax.rsqrt(mean + 1e-6)).T * gain_ref[h : h + 1, :]).astype(BF)
                for out_ref, slot in outs:
                    first = (2 * slot + part) * size
                    out_ref[first : first + size, head] = normed


def norm(pick, acc, qt, recv, off, cum, lw, gain, bit, base, ring):
    heads, rows = cum.shape
    size = rows // ring
    return call(
        functools.partial(norm_kernel, bit=bit, base=base),
        "norm",
        [SM] + [VM] * 7,
        [((2 * size, heads * HD), BF)] * 2 + [((size, heads * HD), BF)],
        (pick, acc, qt, recv, off, cum, lw, gain),
        flops=400_000_000,
        moved=4_000_000,
    )


def start_kernel(a_ref, w_ref, out_ref, *, side, tile):
    rows, half = out_ref.shape
    for j in range(half // tile):
        own = slice(side * half + j * tile, side * half + (j + 1) * tile)
        out_ref[:, j * tile : (j + 1) * tile] = dot(a_ref[rows:, :], w_ref[:, own]).astype(BF)


def start(a, w, side, name, tile=512):
    shape = (a.shape[0] // 2, w.shape[1] // 2)
    kernel = functools.partial(start_kernel, side=side, tile=tile)
    return call(kernel, name, [VM, VM], [(shape, BF)], (a, w), flops=600_000_000, moved=3_000_000)[0]


def across(b_ref, rows, whole_ref, mine_ref, theirs_ref, side, col, parity):
    depth, share = whole_ref.shape[0], mine_ref.shape[0]
    second = b_ref[rows, pl.ds(pl.multiple_of(depth + parity * share, share), share)]
    third = b_ref[rows, pl.ds(pl.multiple_of(depth + (1 - parity) * share, share), share)]
    total = dot(b_ref[rows, :depth], whole_ref[:, col]) + dot(second, mine_ref[:, col])
    return total + dot(third, theirs_ref[side * share : (side + 1) * share, col])


def pass_kernel(pick_ref, begun_ref, b_ref, whole_ref, mine_ref, theirs_ref, kept_ref, sent_ref, *, side, tile):
    size, half = kept_ref.shape
    for j in range(half // tile):
        col = slice(j * tile, (j + 1) * tile)
        more = across(b_ref, slice(0, 2 * size), whole_ref, mine_ref, theirs_ref, side, col, pick_ref[2])
        total = begun_ref[:, col].astype(F32) + more
        kept_ref[:, col] = total[:size]
        sent_ref[:, col] = total[size:].astype(BF)


def pass_on(pick, begun, b, pieces, side, name, tile=512):
    shape = (begun.shape[0] // 2, begun.shape[1])
    return call(
        functools.partial(pass_kernel, side=side, tile=tile),
        name,
        [SM] + [VM] * 5,
        [(shape, F32), (shape, BF)],
        (pick, begun, b, *pieces),
        flops=600_000_000,
        moved=3_000_000,
    )


def own_kernel(pick_ref, a_ref, w_ref, *refs, tile):
    pieces, kept_ref, sent = refs[:8], refs[8], refs[9:]
    size = kept_ref.shape[0]
    half = kept_ref.shape[1] // 2
    for side in range(2):
        b_ref, *weights = pieces[4 * side : 4 * side + 4]
        for j in range(half // tile):
            col = slice(j * tile, (j + 1) * tile)
            at = slice(side * half + j * tile, side * half + (j + 1) * tile)
            total = dot(a_ref[...], w_ref[:, at])
            total = total + across(b_ref, slice(2 * size, 4 * size), *weights, side, col, pick_ref[2])
            kept_ref[:, at] = total[:size]
            first = size
            for out_ref in sent:
                out_ref[:, at] = total[first : first + out_ref.shape[0]].astype(BF)
                first += out_ref.shape[0]


def own_part(pick, a, w, left, right, tile=512):
    size, width = a.shape[0] // 2, w.shape[1]
    sent = (3 * size // 8, 3 * size // 8, size // 4)
    return call(
        functools.partial(own_kernel, tile=tile),
        "own",
        [SM] + [VM] * 10,
        [((size, width), F32)] + [((n, width), BF) for n in sent],
        (pick, a, w, *left, *right),
        flops=2_000_000_000,
        moved=9_000_000,
    )


def join_kernel(a_ref, b_ref, out_ref):
    out_ref[...] = (a_ref[...] + b_ref[...].astype(F32)).astype(BF)


def join(a, b, name):
    return call(join_kernel, name, [VM, VM], [(a.shape, BF)], (a, b), flops=300_000, moved=2_000_000)[0]


def finish_kernel(own_ref, left_ref, right_ref, *refs):
    swaps, out_ref = refs[:-1], refs[-1]
    half = left_ref.shape[1]
    first = 0
    for swap_ref in swaps:
        rows = slice(first, first + swap_ref.shape[0])
        for side, far_ref in enumerate((left_ref, right_ref)):
            at = slice(side * half, (side + 1) * half)
            total = own_ref[rows, at] + swap_ref[:, at].astype(F32) + far_ref[rows, :].astype(F32)
            out_ref[rows, at] = total.astype(BF)
        first = rows.stop


def finish(own, left, right, swaps):
    ins = [VM] * (3 + len(swaps))
    return call(finish_kernel, "finish", ins, [(own.shape, BF)], (own, left, right, *swaps), flops=2_000_000, moved=5_000_000)[0]


def partners(bit, size, inner):
    if 2 << bit == inner:
        flip = inner - 1
    elif 2 << bit == size:
        flip = (size - 1) & ~(inner - 1)
    else:
        flip = 1 << bit
    return [(i, i ^ flip) for i in range(size)]


def body(queries, keys, values, log_decay, level_weight, norm_gain, out_weight):
    rows, heads, _ = queries.shape
    seq_size, head_size = lax.axis_size("seq"), lax.axis_size("head")
    bits = seq_size.bit_length() - 1
    base = (rows // SPAN).bit_length()
    ring = head_size // 2
    pos = lax.axis_index("seq").astype(jnp.int32)
    lane = lax.axis_index("head").astype(jnp.int32)
    x, core = lane // 2, lane % 2
    parity = pos % 2
    near = x ^ 1
    side = (x + ring - 1 + 2 * (x % 2)) % ring
    pick = jnp.stack([pos, core, parity, (x + 2) % ring, near, side, x])
    pos1 = pos[None]
    swap = [(i, i ^ 1) for i in range(head_size)]
    to_near = [(i, i ^ 2) for i in range(head_size)]
    to_side = [(i, (i + (2 if i // 2 % 2 else -2)) % head_size) for i in range(head_size)]
    to_y = [(i, i ^ 1) for i in range(seq_size)]

    flat = lambda a: a.reshape(rows, heads * HD)
    ld = jnp.transpose(log_decay, (1, 0))
    lw = jnp.transpose(level_weight, (2, 1, 0))
    k2, v2 = flat(keys), flat(values)
    pay, cum = summary(ld, k2, v2)

    depth, width = out_weight.shape
    off = jnp.zeros((heads, 128), F32)
    after = cum
    recvs, offs = [], []
    for b in range(bits):
        recv = lax.ppermute(pay, "seq", partners(b, seq_size, 4))
        recvs.append(recv)
        offs.append(off)
        if b == 0:
            weight, _ = lax.optimization_barrier((out_weight, pay))
            mine = lax.dynamic_slice(weight, (depth // 2 + parity * (depth // 4), 0), (depth // 4, width))
            mine_l = lax.ppermute(mine[:, : width // 2], "head", to_near)
            mine_r = lax.ppermute(mine[:, width // 2 :], "head", to_side)
        if b == 1:
            weight, _ = lax.optimization_barrier((out_weight, pay))
            whole_l = lax.ppermute(weight[: depth // 2, : width // 2], "head", to_near)
            whole_r = lax.ppermute(weight[: depth // 2, width // 2 :], "head", to_side)
        if b == 2:
            queries, keys, values, _ = lax.optimization_barrier((queries, keys, values, pay))
            acc, qt = local(flat(queries), flat(keys), flat(values), cum, lw)
            after = acc
        if b == 3:
            mine_l, mine_r, _ = lax.optimization_barrier((mine_l, mine_r, pay))
            theirs = lax.ppermute(jnp.concatenate([mine_l, mine_r], axis=0), "seq", to_y)
        if b >= 3:
            for i in (0, 1, 2) if b == 3 else (3,):
                acc = far(pos1, acc, qt, recvs[i], offs[i], cum, lw, i, base)
            after = acc
        if b < bits - 1:
            pay, off = merge(pos1, after, recv, pay, off, b)
    n_near, n_side, n_own = norm(pick, acc, qt, recv, off, cum, lw, norm_gain, bits - 1, base, ring)
    from_near = lax.ppermute(n_near, "head", to_near)
    from_side = lax.ppermute(n_side, "head", to_side)
    left, right = (whole_l, mine_l, theirs), (whole_r, mine_r, theirs)
    begun_l = start(n_side, out_weight, 0, "start_left")
    begun_r = start(n_near, out_weight, 1, "start_right")
    keep_l, send_l = pass_on(pick, begun_l, from_near, left, 0, "left")
    swap_l = lax.ppermute(send_l, "head", swap)
    keep_r, send_r = pass_on(pick, begun_r, from_side, right, 1, "right")
    swap_r = lax.ppermute(send_r, "head", swap)
    both_l = join(keep_l, swap_l, "join_left")
    both_r = join(keep_r, swap_r, "join_right")
    far_l = lax.ppermute(both_l, "head", to_side)
    far_r = lax.ppermute(both_r, "head", to_near)
    n_own, _, _ = lax.optimization_barrier((n_own, both_l, both_r))
    keep, *sends = own_part(pick, n_own, out_weight, (from_near, *left), (from_side, *right))
    swaps = [lax.ppermute(send, "head", swap) for send in sends]
    return finish(keep, far_l, far_r, swaps)


def solution(mesh):
    return jax.shard_map(
        body,
        mesh=mesh,
        in_specs=(
            P("seq", "head", None),
            P("seq", "head", None),
            P("seq", "head", None),
            P("seq", "head"),
            P("seq", "head", None),
            P("head", None),
            P("head", None),
        ),
        out_specs=P(("seq", "head"), None),
        check_vma=False,
    )
```

time: 215 us -> 81.4 us (0.38)
  local copies, waits for them, and re-layouts: 50.5 us -> 7.79 us
  blocking collectives: 37.4 us -> 0 us
  waiting for transfers between devices: 57.8 us -> 21.1 us
  matrix products: 36.6 us -> 0 us
  starting transfers between devices: 0.04 us -> 28.4 us
  Pallas kernels: 0 us -> 22.3 us
  other arithmetic: 17.7 us -> 1.18 us
  between operations: 13.8 us -> 0.32 us
    reduce_scatter x1 -> x0, waiting for transfers between devices: 57.8 us -> none  [body(): lax.psum_scatter(jnp.dot(normed, out_weight, preferred_element_type=jnp.f...]
    all_gather x1 -> x0, blocking collectives: 37.4 us -> none  [body(): all_totals = lax.all_gather(summary_total[None], 'seq', axis=0, tiled=True)]
    dot_general x9 -> x0, matrix products: 36.6 us -> none  [the longest x4 9.98 us: local_levels(): jnp.einsum('cthd,chde->cthe', query_blocks, picked, preferred_element_typ...]
    ppermute x0 -> x19, starting transfers between devices: none -> 28.4 us  [the longest x5 13.1 us: body(): recv = lax.ppermute(pay, 'seq', partners(b, seq_size, 4))]
    pallas_call x0 -> x19, Pallas kernels: none -> 22.3 us  [call(): pl.pallas_call(kernel, in_specs=ins, out_specs=[VM] * len(outs), out_shap...]
    ppermute x0 -> x19, waiting for transfers between devices: none -> 21.1 us  [the longest x1 6.96 us: body(): from_side = lax.ppermute(n_side, 'head', to_side)]
    gather x13 -> x0, local copies, waits for them, and re-layouts: 15.1 us -> none  [the longest x4 12 us: local_levels(): picked = blocks[source].astype(jnp.bfloat16)]
    mul x7 -> x0, local copies, waits for them, and re-layouts: 9.5 us -> none  [the longest x4 7.01 us: local_levels(): output = output + factor[:, :, :, None] * readout]
  transfers between devices with their start and end apart: 2 -> 19, of which waited for: 1 -> 7; matrix products, arithmetic and copies ran while one was open for 27% -> 8% of each run, Pallas kernels for 0% -> 24%
where the time goes in v2:
time: 81.4 us; the launch traced here: 81.1 us
  starting transfers between devices  28.4 us (35%)
  Pallas kernels  22.3 us (27%)
  waiting for transfers between devices  21.1 us (26%)
  local copies, waits for them, and re-layouts  7.79 us (10%)
  other arithmetic  1.18 us (1%)
    pallas_call x19, Pallas kernels, call(): pl.pallas_call(kernel, in_specs=ins, out_specs=[VM] * len(outs), out_shap...  22.3 us
    ppermute x5, starting transfers between devices, body(): recv = lax.ppermute(pay, 'seq', partners(b, seq_size, 4))  13.1 us
    ppermute x1, waiting for transfers between devices, body(): from_side = lax.ppermute(n_side, 'head', to_side)  6.96 us
    ppermute x1, starting transfers between devices, body(): swap_r = lax.ppermute(send_r, 'head', swap)  5.41 us
    ppermute x5, waiting for transfers between devices, body(): recv = lax.ppermute(pay, 'seq', partners(b, seq_size, 4))  5.28 us
    ppermute x1, waiting for transfers between devices, body(): far_r = lax.ppermute(both_r, 'head', to_near)  3.4 us
    slice x1, local copies, waits for them, and re-layouts, body(): whole_r = lax.ppermute(weight[:depth // 2, width // 2:], 'head', to_side)  3.12 us
    ppermute x1, starting transfers between devices, body(): mine_r = lax.ppermute(mine[:, width // 2:], 'head', to_side)  2.57 us
  transfers between devices with their start and end apart: 19, of which 7 were waited for; matrix products, arithmetic and copies ran while one was open for 8% of the time, Pallas kernels for 24%

profile of v2, /device:TPU:1, one launch (start us, length us, event | category | flops | bytes accessed | tf_op | source)
XLA Modules:
  0.0 81.1 jit_solution(6544597389167985008)
XLA Ops:
  0.0 1.9 %copy_bitcast_fusion.3 = (bf16[1024,512]{1,0:T(8,128)(2,1)S(1)}, bf16[1024,512]{1,0:T(8,128)(2,1)S(1)}) fusion(bf16[128,8,4,128]{3,2,1,0:T(4,128)(2,1)} %bitcast.39, bf16[128,8,4,128]{3,2,1,0:T(4,128)(2,1)} %bitcast.37), kind=kLoop, calls=%fused_computation.3 | loop fusion | bytes 4194304 | tf_op jit(solution)/shard_map/reshape | solution.py:361
  1.9 1.2 %summary.1 = (bf16[528,128]{1,0:T(8,128)(2,1)S(1)}, f32[4,1024]{1,0:T(4,128)S(1)}) custom-call(f32[4,1024]{1,0:T(4,128)S(1)} %bitcast.36, bf16[1024,512]{1,0:T(8,128)(2,1)S(1)} %get-tuple-element.72.k_ref, bf16[1024,512]{1,0:T(8,128)(2,1)S(1)} %get-tuple-element.71.v_ref), custom_call_target="tpu_custom_call" | custom-call | flops 140000000 | bytes 2000000 | tf_op jit(solution)/shard_map/summary/pallas_call | solution.py:19
  3.1 2.2 %collective-permute-start = (bf16[528,128]{1,0:T(8,128)(2,1)S(1)}, bf16[528,128]{1,0:T(8,128)(2,1)S(1)}, u32[]{:S(2)}, u32[]{:S(2)}) collective-permute-start(bf16[528,128]{1,0:T(8,128)(2,1)S(1)} %get-tuple-element.37.self_ref), channel_id=1, source_target_pairs={{0,8},{8,0},{16,24},{24,16},{32,40},{40,32},{48,56},{56,48},{64,72... | collective-permute-start | bytes 405512 | tf_op jit(solution)/shard_map/ppermute | solution.py:372
  5.3 1.3 %fusion.1 = (bf16[128,2048]{1,0:T(8,128)(2,1)S(1)}, bf16[128,2048]{1,0:T(8,128)(2,1)S(1)}) fusion(bf16[512,4096]{1,0:T(8,128)(2,1)} %w_ref.5, s32[]{:T(128)S(6)} %select_n.36, s32[]{:T(128)S(6)} %add.40), kind=kLoop, calls=%fused_computation.8 | loop fusion | bytes 2097160 | tf_op jit(solution)/shard_map/slice | solution.py:379
  6.6 2.6 %collective-permute-start.8 = (bf16[128,2048]{1,0:T(8,128)(2,1)S(1)}, bf16[128,2048]{1,0:T(8,128)(2,1)S(1)}, u32[]{:S(2)}, u32[]{:S(2)}) collective-permute-start(bf16[128,2048]{1,0:T(8,128)(2,1)S(1)} %get-tuple-element.69), channel_id=1, source_target_pairs={{0,6},{1,7},{2,4},{3,5},{4,2},{5,3},{6,0},{7,1},{8,14},{9,15},{10,... | collective-permute-start | bytes 1572872 | tf_op jit(solution)/shard_map/ppermute | solution.py:379
  9.2 0.0 collective-permute-start.7
  9.2 0.0 collective-permute-done.recv_ref
  9.2 0.1 merge0.1
  9.3 0.0 copy-start.10
  9.3 2.1 %collective-permute-start.1 = (bf16[528,128]{1,0:T(8,128)(2,1)S(1)}, bf16[528,128]{1,0:T(8,128)(2,1)S(1)}, u32[]{:S(2)}, u32[]{:S(2)}) collective-permute-start(bf16[528,128]{1,0:T(8,128)(2,1)S(1)} %get-tuple-element.38.self_ref), channel_id=1, source_target_pairs={{0,24},{8,16},{16,8},{24,0},{32,56},{40,48},{48,40},{56,32},{64,88... | collective-permute-start | bytes 405512 | tf_op jit(solution)/shard_map/ppermute | solution.py:372
  11.4 3.1 %fusion = (bf16[256,2048]{1,0:T(8,128)(2,1)}, bf16[256,2048]{1,0:T(8,128)(2,1)}) fusion(bf16[512,4096]{1,0:T(8,128)(2,1)} %w_ref.5), kind=kLoop, calls=%fused_computation.7 | loop fusion | bytes 4194304 | tf_op jit(solution)/shard_map/slice | solution.py:383
  14.5 2.5 %collective-permute-start.12 = (bf16[256,2048]{1,0:T(8,128)(2,1)}, bf16[256,2048]{1,0:T(8,128)(2,1)}, u32[]{:S(2)}, u32[]{:S(2)}) collective-permute-start(bf16[256,2048]{1,0:T(8,128)(2,1)} %get-tuple-element.67), channel_id=1, source_target_pairs={{0,6},{1,7},{2,4},{3,5},{4,2},{5,3},{6,0},{7,1},{8,14},{9,15},{10,... | collective-permute-start | bytes 3145736 | tf_op jit(solution)/shard_map/ppermute | solution.py:383
  17.0 0.0 collective-permute-done.1.recv_ref
  17.0 0.1 merge1.1
  17.1 1.7 %collective-permute-start.2 = (bf16[528,128]{1,0:T(8,128)(2,1)S(1)}, bf16[528,128]{1,0:T(8,128)(2,1)S(1)}, u32[]{:S(2)}, u32[]{:S(2)}) collective-permute-start(bf16[528,128]{1,0:T(8,128)(2,1)S(1)} %get-tuple-element.40.self_ref), channel_id=1, source_target_pairs={{0,32},{8,40},{16,48},{24,56},{32,0},{40,8},{48,16},{56,24},{64,96... | collective-permute-start | bytes 405512 | tf_op jit(solution)/shard_map/ppermute | solution.py:372
  18.8 0.2 copy.23
  19.0 0.0 copy-start.5
  19.0 0.2 copy.24
  19.2 0.8 %copy-done.11 = bf16[1024,4,128]{2,1,0:T(4,128)(2,1)S(1)} copy-done((bf16[1024,4,128]{2,1,0:T(4,128)(2,1)S(1)}, bf16[1024,4,128]{2,1,0:T(4,128)(2,1)}, u32[]{:S(2)}) %copy-start.11) | copy-done | bytes 1048600
  20.0 0.2 copy.22
  20.2 2.6 %local.1 = (f32[512,1024]{1,0:T(8,128)S(1)}, bf16[512,1024]{1,0:T(8,128)(2,1)S(1)}) custom-call(bf16[1024,512]{1,0:T(8,128)(2,1)S(1)} %bitcast.34, bf16[1024,512]{1,0:T(8,128)(2,1)S(1)} %bitcast.33, bf16[1024,512]{1,0:T(8,128)(2,1)S(1)} %bitcast.35, f32[4,1024]{1,0:T(4,128)S(1)} %get-tuple-element.36.after_ref.cum_ref, f32[10,4,1024]{2,1,0:T(4,128)S(1)} %bitcast.27), custom_call_target="tpu_custom_call" | custom-call | flops 2000000000 | bytes 8000000 | tf_op jit(solution)/shard_map/local/pallas_call | solution.py:19
  22.8 0.0 collective-permute-done.2.recv_ref
  22.8 0.1 merge2.1
  22.9 0.0 collective-permute-done.8.mine_ref.refs_6_
  22.9 0.0 collective-permute-done.7.mine_ref.refs_2_
  23.0 1.2 %pad_maximum_fusion = bf16[256,2048]{1,0:T(8,128)(2,1)} fusion(bf16[128,2048]{1,0:T(8,128)(2,1)S(1)} %collective-permute-done.8.mine_ref.refs_6_, bf16[128,2048]{1,0:T(8,128)(2,1)S(1)} %collective-permute-done.7.mine_ref.refs_2_), kind=kLoop, calls=%fused_computation.5 | loop fusion | flops 2097152 | bytes 2097152 | tf_op jit(solution)/shard_map/concatenate | solution.py:390
  24.1 0.0 collective-permute-start.9
  24.1 0.0 collective-permute-start.6
  24.1 3.0 %collective-permute-start.3 = (bf16[528,128]{1,0:T(8,128)(2,1)S(1)}, bf16[528,128]{1,0:T(8,128)(2,1)S(1)}, u32[]{:S(2)}, u32[]{:S(2)}) collective-permute-start(bf16[528,128]{1,0:T(8,128)(2,1)S(1)} %get-tuple-element.47.self_ref), channel_id=1, source_target_pairs={{0,64},{8,72},{16,80},{24,88},{32,96},{40,104},{48,112},{56,120},{... | collective-permute-start | bytes 405512 | tf_op jit(solution)/shard_map/ppermute | solution.py:372
  27.1 0.6 far0.1.acc_ref
  27.8 0.6 far1.1.acc_ref
  28.4 0.6 far2.1.acc_ref.after_ref
  29.0 2.3 %collective-permute-done.3.recv_ref = bf16[528,128]{1,0:T(8,128)(2,1)S(1)} collective-permute-done((bf16[528,128]{1,0:T(8,128)(2,1)S(1)}, bf16[528,128]{1,0:T(8,128)(2,1)S(1)}, u32[]{:S(2)}, u32[]{:S(2)}) %collective-permute-start.3) | collective-permute-done | bytes 135200 | tf_op jit(solution)/shard_map/ppermute | solution.py:372
  31.3 0.7 merge3.1
  32.0 4.1 %collective-permute-start.4 = (bf16[528,128]{1,0:T(8,128)(2,1)}, bf16[528,128]{1,0:T(8,128)(2,1)}, u32[]{:S(2)}, u32[]{:S(2)}) collective-permute-start(bf16[528,128]{1,0:T(8,128)(2,1)} %get-tuple-element.49), channel_id=1, source_target_pairs={{0,224},{8,232},{16,240},{24,248},{32,192},{40,200},{48,208},{56,2... | collective-permute-start | bytes 405512 | tf_op jit(solution)/shard_map/ppermute | solution.py:372
  36.1 0.1 stack.31.pick_ref
  36.2 0.6 far3.1.acc_ref
  36.8 2.9 %collective-permute-done.4.recv_ref = bf16[528,128]{1,0:T(8,128)(2,1)} collective-permute-done((bf16[528,128]{1,0:T(8,128)(2,1)}, bf16[528,128]{1,0:T(8,128)(2,1)}, u32[]{:S(2)}, u32[]{:S(2)}) %collective-permute-start.4) | collective-permute-done | bytes 135200 | tf_op jit(solution)/shard_map/ppermute | solution.py:372
  39.8 2.1 %norm.1 = (bf16[512,512]{1,0:T(8,128)(2,1)S(1)}, bf16[512,512]{1,0:T(8,128)(2,1)S(1)}, bf16[256,512]{1,0:T(8,128)(2,1)S(1)}) custom-call(s32[7]{0:T(128)S(1)} %stack.31.pick_ref, f32[512,1024]{1,0:T(8,128)S(1)} %far3.1.acc_ref, bf16[512,1024]{1,0:T(8,128)(2,1)S(1)} %get-tuple-element.45.qt_ref, bf16[528,128]{1,0:T(8,128)(2,1)} %collective-permute-done.4.recv_ref, ...), custom_call_target="tpu_custom_call" | custom-call | flops 400000000 | bytes 4000000 | tf_op jit(solution)/shard_map/norm/pallas_call | solution.py:19
  41.9 1.4 %collective-permute-start.11 = (bf16[512,512]{1,0:T(8,128)(2,1)S(1)}, bf16[512,512]{1,0:T(8,128)(2,1)S(1)}, u32[]{:S(2)}, u32[]{:S(2)}) collective-permute-start(bf16[512,512]{1,0:T(8,128)(2,1)S(1)} %get-tuple-element.52.a_ref), channel_id=1, source_target_pairs={{0,6},{1,7},{2,4},{3,5},{4,2},{5,3},{6,0},{7,1},{8,14},{9,15},{10,... | collective-permute-start | bytes 1572872 | tf_op jit(solution)/shard_map/ppermute | solution.py:399
  43.3 0.5 collective-permute-start.5
  43.8 0.7 start_left.1.begun_ref
  44.5 0.7 start_right.1.begun_ref
  45.2 0.0 collective-permute-done.12.whole_ref.refs_5_
  45.3 7.0 %collective-permute-done.11.b_ref.refs_4_ = bf16[512,512]{1,0:T(8,128)(2,1)S(1)} collective-permute-done((bf16[512,512]{1,0:T(8,128)(2,1)S(1)}, bf16[512,512]{1,0:T(8,128)(2,1)S(1)}, u32[]{:S(2)}, u32[]{:S(2)}) %collective-permute-start.11) | collective-permute-done | bytes 524320 | tf_op jit(solution)/shard_map/ppermute | solution.py:399
  52.2 2.5 %right.1 = (f32[128,2048]{1,0:T(8,128)S(1)}, bf16[128,2048]{1,0:T(8,128)(2,1)S(1)}) custom-call(s32[7]{0:T(128)S(1)} %stack.31.pick_ref, bf16[256,2048]{1,0:T(8,128)(2,1)S(1)} %start_right.1.begun_ref, bf16[512,512]{1,0:T(8,128)(2,1)S(1)} %collective-permute-done.11.b_ref.refs_4_, bf16[256,2048]{1,0:T(8,128)(2,1)} %collective-permute-done.12.whole_ref.refs_5_, ...), custom_call_target="tpu_custom_call" | custom-call | flops 600000000 | bytes 3000000 | tf_op jit(solution)/shard_map/right/pallas_call | solution.py:19
  54.8 5.4 %collective-permute-start.13 = (bf16[128,2048]{1,0:T(8,128)(2,1)S(1)}, bf16[128,2048]{1,0:T(8,128)(2,1)S(1)}, u32[]{:S(2)}, u32[]{:S(2)}) collective-permute-start(bf16[128,2048]{1,0:T(8,128)(2,1)S(1)} %get-tuple-element.61), channel_id=1, source_target_pairs={{0,1},{1,0},{2,3},{3,2},{4,5},{5,4},{6,7},{7,6},{8,9},{9,8},{10,11... | collective-permute-start | bytes 1572872 | tf_op jit(solution)/shard_map/ppermute | solution.py:406
  60.2 0.0 collective-permute-done.5.b_ref.refs_0_
  60.2 2.5 %left.1 = (f32[128,2048]{1,0:T(8,128)S(1)}, bf16[128,2048]{1,0:T(8,128)(2,1)S(1)}) custom-call(s32[7]{0:T(128)S(1)} %stack.31.pick_ref, bf16[256,2048]{1,0:T(8,128)(2,1)S(1)} %start_left.1.begun_ref, bf16[512,512]{1,0:T(8,128)(2,1)S(1)} %collective-permute-done.5.b_ref.refs_0_, bf16[256,2048]{1,0:T(8,128)(2,1)} %collective-permute-done.6.whole_ref.refs_1_, ...), custom_call_target="tpu_custom_call" | custom-call | flops 600000000 | bytes 3000000 | tf_op jit(solution)/shard_map/left/pallas_call | solution.py:19
  62.7 1.1 %collective-permute-start.10 = (bf16[128,2048]{1,0:T(8,128)(2,1)S(1)}, bf16[128,2048]{1,0:T(8,128)(2,1)S(1)}, u32[]{:S(2)}, u32[]{:S(2)}) collective-permute-start(bf16[128,2048]{1,0:T(8,128)(2,1)S(1)} %get-tuple-element.59), channel_id=1, source_target_pairs={{0,1},{1,0},{2,3},{3,2},{4,5},{5,4},{6,7},{7,6},{8,9},{9,8},{10,11... | collective-permute-start | bytes 1572872 | tf_op jit(solution)/shard_map/ppermute | solution.py:404
  63.8 0.0 collective-permute-done.13.b_ref
  63.8 0.1 join_right.1
  63.9 0.1 collective-permute-start.15
  64.0 1.3 %collective-permute-done.10.b_ref = bf16[128,2048]{1,0:T(8,128)(2,1)S(1)} collective-permute-done((bf16[128,2048]{1,0:T(8,128)(2,1)S(1)}, bf16[128,2048]{1,0:T(8,128)(2,1)S(1)}, u32[]{:S(2)}, u32[]{:S(2)}) %collective-permute-start.10) | collective-permute-done | bytes 524320 | tf_op jit(solution)/shard_map/ppermute | solution.py:404
  65.3 0.1 join_left.1
  65.4 0.8 collective-permute-start.14
  66.2 5.1 %own.1 = (f32[128,4096]{1,0:T(8,128)S(1)}, bf16[48,4096]{1,0:T(8,128)(2,1)S(1)}, bf16[48,4096]{1,0:T(8,128)(2,1)S(1)}, bf16[32,4096]{1,0:T(8,128)(2,1)S(1)}) custom-call(s32[7]{0:T(128)S(1)} %stack.31.pick_ref, bf16[256,512]{1,0:T(8,128)(2,1)S(1)} %get-tuple-element.62.a_ref, bf16[512,4096]{1,0:T(8,128)(2,1)S(1)} %copy-done, ...), custom_call_target="tpu_custom_call" | custom-call | flops 2000000000 | bytes 9000000 | tf_op jit(solution)/shard_map/own/pallas_call | solution.py:19
  71.3 0.5 collective-permute-start.16
  71.8 0.1 collective-permute-start.17
  71.9 0.4 collective-permute-start.18
  72.3 1.8 %collective-permute-done.18.refs_2_ = bf16[32,4096]{1,0:T(8,128)(2,1)S(1)} collective-permute-done((bf16[32,4096]{1,0:T(8,128)(2,1)S(1)}, bf16[32,4096]{1,0:T(8,128)(2,1)S(1)}, u32[]{:S(2)}, u32[]{:S(2)}) %collective-permute-start.18) | collective-permute-done | bytes 262176 | tf_op jit(solution)/shard_map/ppermute | solution.py:413
  74.1 3.4 %collective-permute-done.15.right_ref = bf16[128,2048]{1,0:T(8,128)(2,1)S(1)} collective-permute-done((bf16[128,2048]{1,0:T(8,128)(2,1)S(1)}, bf16[128,2048]{1,0:T(8,128)(2,1)S(1)}, u32[]{:S(2)}, u32[]{:S(2)}) %collective-permute-start.15) | collective-permute-done | bytes 524320 | tf_op jit(solution)/shard_map/ppermute | solution.py:410
  77.5 2.3 %collective-permute-done.14.left_ref = bf16[128,2048]{1,0:T(8,128)(2,1)S(1)} collective-permute-done((bf16[128,2048]{1,0:T(8,128)(2,1)S(1)}, bf16[128,2048]{1,0:T(8,128)(2,1)S(1)}, u32[]{:S(2)}, u32[]{:S(2)}) %collective-permute-start.14) | collective-permute-done | bytes 524320 | tf_op jit(solution)/shard_map/ppermute | solution.py:409
  79.9 1.3 %finish.1 = bf16[128,4096]{1,0:T(8,128)(2,1)} custom-call(f32[128,4096]{1,0:T(8,128)S(1)} %get-tuple-element.63.own_ref, bf16[128,2048]{1,0:T(8,128)(2,1)S(1)} %collective-permute-done.14.left_ref, bf16[128,2048]{1,0:T(8,128)(2,1)S(1)} %collective-permute-done.15.right_ref, bf16[48,4096]{1,0:T(8,128)(2,1)S(1)} %collective-permute-done.16.refs_0_, ...), custom_call_target="tpu_custom_call" | custom-call | flops 2000000 | bytes 5000000 | tf_op jit(solution)/shard_map/finish/pallas_call | solution.py:19
  (28 shorter events, 0.1 us)
Async XLA Ops:
  0.0 1.9 %copy-start.8 = (f32[1024,4]{0,1:T(4,128)S(1)}, f32[1024,4]{0,1:T(4,128)}, u32[]{:S(2)}) copy-start(f32[1024,4]{0,1:T(4,128)} %param.10) | copy-start | bytes 49156
  3.1 6.1 %collective-permute-start = (bf16[528,128]{1,0:T(8,128)(2,1)S(1)}, bf16[528,128]{1,0:T(8,128)(2,1)S(1)}, u32[]{:S(2)}, u32[]{:S(2)}) collective-permute-start(bf16[528,128]{1,0:T(8,128)(2,1)S(1)} %get-tuple-element.37.self_ref), channel_id=1, source_target_pairs={{0,8},{8,0},{16,24},{24,16},{32,40},{40,32},{48,56},{56,48},{64,72... | collective-permute-start | bytes 405512 | tf_op jit(solution)/shard_map/ppermute | solution.py:372
  6.6 16.3 %collective-permute-start.8 = (bf16[128,2048]{1,0:T(8,128)(2,1)S(1)}, bf16[128,2048]{1,0:T(8,128)(2,1)S(1)}, u32[]{:S(2)}, u32[]{:S(2)}) collective-permute-start(bf16[128,2048]{1,0:T(8,128)(2,1)S(1)} %get-tuple-element.69), channel_id=1, source_target_pairs={{0,6},{1,7},{2,4},{3,5},{4,2},{5,3},{6,0},{7,1},{8,14},{9,15},{10,... | collective-permute-start | bytes 1572872 | tf_op jit(solution)/shard_map/ppermute | solution.py:379
  9.2 13.8 %collective-permute-start.7 = (bf16[128,2048]{1,0:T(8,128)(2,1)S(1)}, bf16[128,2048]{1,0:T(8,128)(2,1)S(1)}, u32[]{:S(2)}, u32[]{:S(2)}) collective-permute-start(bf16[128,2048]{1,0:T(8,128)(2,1)S(1)} %get-tuple-element.70), channel_id=1, source_target_pairs={{0,2},{1,3},{2,0},{3,1},{4,6},{5,7},{6,4},{7,5},{8,10},{9,11},{10,... | collective-permute-start | bytes 1572872 | tf_op jit(solution)/shard_map/ppermute | solution.py:378
  9.2 5.3 %copy-start.6 = (bf16[528,128]{1,0:T(8,128)(2,1)}, bf16[528,128]{1,0:T(8,128)(2,1)S(1)}, u32[]{:S(2)}) copy-start(bf16[528,128]{1,0:T(8,128)(2,1)S(1)} %collective-permute-done.recv_ref) | copy-start | bytes 405508
  9.3 9.5 %copy-start.10 = (bf16[1024,4,128]{2,1,0:T(4,128)(2,1)S(1)}, bf16[1024,4,128]{2,1,0:T(4,128)(2,1)}, u32[]{:S(2)}) copy-start(bf16[1024,4,128]{2,1,0:T(4,128)(2,1)} %param.8) | copy-start | bytes 3145732
  9.3 7.7 %collective-permute-start.1 = (bf16[528,128]{1,0:T(8,128)(2,1)S(1)}, bf16[528,128]{1,0:T(8,128)(2,1)S(1)}, u32[]{:S(2)}, u32[]{:S(2)}) collective-permute-start(bf16[528,128]{1,0:T(8,128)(2,1)S(1)} %get-tuple-element.38.self_ref), channel_id=1, source_target_pairs={{0,24},{8,16},{16,8},{24,0},{32,56},{40,48},{48,40},{56,32},{64,88... | collective-permute-start | bytes 405512 | tf_op jit(solution)/shard_map/ppermute | solution.py:372
  14.5 4.5 %copy-start.12 = (bf16[1024,4,128]{2,1,0:T(4,128)(2,1)S(1)}, bf16[1024,4,128]{2,1,0:T(4,128)(2,1)}, u32[]{:S(2)}) copy-start(bf16[1024,4,128]{2,1,0:T(4,128)(2,1)} %param.7) | copy-start | bytes 3145732
  14.5 30.7 %collective-permute-start.12 = (bf16[256,2048]{1,0:T(8,128)(2,1)}, bf16[256,2048]{1,0:T(8,128)(2,1)}, u32[]{:S(2)}, u32[]{:S(2)}) collective-permute-start(bf16[256,2048]{1,0:T(8,128)(2,1)} %get-tuple-element.67), channel_id=1, source_target_pairs={{0,6},{1,7},{2,4},{3,5},{4,2},{5,3},{6,0},{7,1},{8,14},{9,15},{10,... | collective-permute-start | bytes 3145736 | tf_op jit(solution)/shard_map/ppermute | solution.py:383
  17.1 5.7 %collective-permute-start.2 = (bf16[528,128]{1,0:T(8,128)(2,1)S(1)}, bf16[528,128]{1,0:T(8,128)(2,1)S(1)}, u32[]{:S(2)}, u32[]{:S(2)}) collective-permute-start(bf16[528,128]{1,0:T(8,128)(2,1)S(1)} %get-tuple-element.40.self_ref), channel_id=1, source_target_pairs={{0,32},{8,40},{16,48},{24,56},{32,0},{40,8},{48,16},{56,24},{64,96... | collective-permute-start | bytes 405512 | tf_op jit(solution)/shard_map/ppermute | solution.py:372
  18.8 1.2 %copy-start.11 = (bf16[1024,4,128]{2,1,0:T(4,128)(2,1)S(1)}, bf16[1024,4,128]{2,1,0:T(4,128)(2,1)}, u32[]{:S(2)}) copy-start(bf16[1024,4,128]{2,1,0:T(4,128)(2,1)} %param.9) | copy-start | bytes 3145732
  19.0 1.2 %copy-start.5 = (f32[1024,4,10]{0,1,2:T(4,128)S(1)}, f32[1024,4,10]{0,1,2:T(4,128)}, u32[]{:S(2)}) copy-start(f32[1024,4,10]{0,1,2:T(4,128)} %param.11) | copy-start | bytes 491524
  22.8 4.3 %copy-start.7 = (bf16[528,128]{1,0:T(8,128)(2,1)S(1)}, bf16[528,128]{1,0:T(8,128)(2,1)}, u32[]{:S(2)}) copy-start(bf16[528,128]{1,0:T(8,128)(2,1)} %copy-done.6) | copy-start | bytes 405508
  22.9 4.8 %copy-start.1 = (bf16[128,2048]{1,0:T(8,128)(2,1)}, bf16[128,2048]{1,0:T(8,128)(2,1)S(1)}, u32[]{:S(2)}) copy-start(bf16[128,2048]{1,0:T(8,128)(2,1)S(1)} %collective-permute-done.8.mine_ref.refs_6_) | copy-start | bytes 1572868
  22.9 4.8 %copy-start.3 = (bf16[128,2048]{1,0:T(8,128)(2,1)}, bf16[128,2048]{1,0:T(8,128)(2,1)S(1)}, u32[]{:S(2)}) copy-start(bf16[128,2048]{1,0:T(8,128)(2,1)S(1)} %collective-permute-done.7.mine_ref.refs_2_) | copy-start | bytes 1572868
  24.1 28.1 %collective-permute-start.9 = (bf16[256,2048]{1,0:T(8,128)(2,1)}, bf16[256,2048]{1,0:T(8,128)(2,1)}, u32[]{:S(2)}, u32[]{:S(2)}) collective-permute-start(bf16[256,2048]{1,0:T(8,128)(2,1)} %pad_maximum_fusion), channel_id=1, source_target_pairs={{0,8},{8,0},{16,24},{24,16},{32,40},{40,32},{48,56},{56,48},{64,72... | collective-permute-start | bytes 3145736 | tf_op jit(solution)/shard_map/ppermute | solution.py:390
  24.1 36.0 %collective-permute-start.6 = (bf16[256,2048]{1,0:T(8,128)(2,1)}, bf16[256,2048]{1,0:T(8,128)(2,1)}, u32[]{:S(2)}, u32[]{:S(2)}) collective-permute-start(bf16[256,2048]{1,0:T(8,128)(2,1)} %get-tuple-element.68), channel_id=1, source_target_pairs={{0,2},{1,3},{2,0},{3,1},{4,6},{5,7},{6,4},{7,5},{8,10},{9,11},{10,... | collective-permute-start | bytes 3145736 | tf_op jit(solution)/shard_map/ppermute | solution.py:382
  24.1 7.2 %collective-permute-start.3 = (bf16[528,128]{1,0:T(8,128)(2,1)S(1)}, bf16[528,128]{1,0:T(8,128)(2,1)S(1)}, u32[]{:S(2)}, u32[]{:S(2)}) collective-permute-start(bf16[528,128]{1,0:T(8,128)(2,1)S(1)} %get-tuple-element.47.self_ref), channel_id=1, source_target_pairs={{0,64},{8,72},{16,80},{24,88},{32,96},{40,104},{48,112},{56,120},{... | collective-permute-start | bytes 405512 | tf_op jit(solution)/shard_map/ppermute | solution.py:372
  32.0 7.8 %collective-permute-start.4 = (bf16[528,128]{1,0:T(8,128)(2,1)}, bf16[528,128]{1,0:T(8,128)(2,1)}, u32[]{:S(2)}, u32[]{:S(2)}) collective-permute-start(bf16[528,128]{1,0:T(8,128)(2,1)} %get-tuple-element.49), channel_id=1, source_target_pairs={{0,224},{8,232},{16,240},{24,248},{32,192},{40,200},{48,208},{56,2... | collective-permute-start | bytes 405512 | tf_op jit(solution)/shard_map/ppermute | solution.py:372
  36.2 3.6 %copy-start.9 = (f32[4,128]{1,0:T(4,128)S(1)}, f32[4,128]{1,0:T(4,128)}, u32[]{:S(2)}) copy-start(f32[4,128]{1,0:T(4,128)} %gain_ref.1) | copy-start | bytes 6148
  36.2 7.5 %copy-start = (bf16[512,4096]{1,0:T(8,128)(2,1)S(1)}, bf16[512,4096]{1,0:T(8,128)(2,1)}, u32[]{:S(2)}) copy-start(bf16[512,4096]{1,0:T(8,128)(2,1)} %w_ref.5) | copy-start | bytes 12582916
  41.9 10.3 %collective-permute-start.11 = (bf16[512,512]{1,0:T(8,128)(2,1)S(1)}, bf16[512,512]{1,0:T(8,128)(2,1)S(1)}, u32[]{:S(2)}, u32[]{:S(2)}) collective-permute-start(bf16[512,512]{1,0:T(8,128)(2,1)S(1)} %get-tuple-element.52.a_ref), channel_id=1, source_target_pairs={{0,6},{1,7},{2,4},{3,5},{4,2},{5,3},{6,0},{7,1},{8,14},{9,15},{10,... | collective-permute-start | bytes 1572872 | tf_op jit(solution)/shard_map/ppermute | solution.py:399
  43.3 16.9 %collective-permute-start.5 = (bf16[512,512]{1,0:T(8,128)(2,1)S(1)}, bf16[512,512]{1,0:T(8,128)(2,1)S(1)}, u32[]{:S(2)}, u32[]{:S(2)}) collective-permute-start(bf16[512,512]{1,0:T(8,128)(2,1)S(1)} %get-tuple-element.53.a_ref), channel_id=1, source_target_pairs={{0,2},{1,3},{2,0},{3,1},{4,6},{5,7},{6,4},{7,5},{8,10},{9,11},{10,... | collective-permute-start | bytes 1572872 | tf_op jit(solution)/shard_map/ppermute | solution.py:398
  44.5 7.7 %copy-start.2 = (bf16[128,2048]{1,0:T(8,128)(2,1)S(1)}, bf16[128,2048]{1,0:T(8,128)(2,1)}, u32[]{:S(2)}) copy-start(bf16[128,2048]{1,0:T(8,128)(2,1)} %copy-done.1) | copy-start | bytes 1572868
  45.2 14.9 %copy-start.4 = (bf16[128,2048]{1,0:T(8,128)(2,1)S(1)}, bf16[128,2048]{1,0:T(8,128)(2,1)}, u32[]{:S(2)}) copy-start(bf16[128,2048]{1,0:T(8,128)(2,1)} %copy-done.3) | copy-start | bytes 1572868
  54.8 9.0 %collective-permute-start.13 = (bf16[128,2048]{1,0:T(8,128)(2,1)S(1)}, bf16[128,2048]{1,0:T(8,128)(2,1)S(1)}, u32[]{:S(2)}, u32[]{:S(2)}) collective-permute-start(bf16[128,2048]{1,0:T(8,128)(2,1)S(1)} %get-tuple-element.61), channel_id=1, source_target_pairs={{0,1},{1,0},{2,3},{3,2},{4,5},{5,4},{6,7},{7,6},{8,9},{9,8},{10,11... | collective-permute-start | bytes 1572872 | tf_op jit(solution)/shard_map/ppermute | solution.py:406
  62.7 2.6 %collective-permute-start.10 = (bf16[128,2048]{1,0:T(8,128)(2,1)S(1)}, bf16[128,2048]{1,0:T(8,128)(2,1)S(1)}, u32[]{:S(2)}, u32[]{:S(2)}) collective-permute-start(bf16[128,2048]{1,0:T(8,128)(2,1)S(1)} %get-tuple-element.59), channel_id=1, source_target_pairs={{0,1},{1,0},{2,3},{3,2},{4,5},{5,4},{6,7},{7,6},{8,9},{9,8},{10,11... | collective-permute-start | bytes 1572872 | tf_op jit(solution)/shard_map/ppermute | solution.py:404
  63.9 13.6 %collective-permute-start.15 = (bf16[128,2048]{1,0:T(8,128)(2,1)S(1)}, bf16[128,2048]{1,0:T(8,128)(2,1)S(1)}, u32[]{:S(2)}, u32[]{:S(2)}) collective-permute-start(bf16[128,2048]{1,0:T(8,128)(2,1)S(1)} %join_right.1), channel_id=1, source_target_pairs={{0,2},{1,3},{2,0},{3,1},{4,6},{5,7},{6,4},{7,5},{8,10},{9,11},{10,... | collective-permute-start | bytes 1572872 | tf_op jit(solution)/shard_map/ppermute | solution.py:410
  65.4 14.4 %collective-permute-start.14 = (bf16[128,2048]{1,0:T(8,128)(2,1)S(1)}, bf16[128,2048]{1,0:T(8,128)(2,1)S(1)}, u32[]{:S(2)}, u32[]{:S(2)}) collective-permute-start(bf16[128,2048]{1,0:T(8,128)(2,1)S(1)} %join_left.1), channel_id=1, source_target_pairs={{0,6},{1,7},{2,4},{3,5},{4,2},{5,3},{6,0},{7,1},{8,14},{9,15},{10,... | collective-permute-start | bytes 1572872 | tf_op jit(solution)/shard_map/ppermute | solution.py:409
  71.3 2.8 %collective-permute-start.16 = (bf16[48,4096]{1,0:T(8,128)(2,1)S(1)}, bf16[48,4096]{1,0:T(8,128)(2,1)S(1)}, u32[]{:S(2)}, u32[]{:S(2)}) collective-permute-start(bf16[48,4096]{1,0:T(8,128)(2,1)S(1)} %get-tuple-element.64), channel_id=1, source_target_pairs={{0,1},{1,0},{2,3},{3,2},{4,5},{5,4},{6,7},{7,6},{8,9},{9,8},{10,11... | collective-permute-start | bytes 1179656 | tf_op jit(solution)/shard_map/ppermute | solution.py:413
  71.8 2.3 %collective-permute-start.17 = (bf16[48,4096]{1,0:T(8,128)(2,1)S(1)}, bf16[48,4096]{1,0:T(8,128)(2,1)S(1)}, u32[]{:S(2)}, u32[]{:S(2)}) collective-permute-start(bf16[48,4096]{1,0:T(8,128)(2,1)S(1)} %get-tuple-element.65), channel_id=1, source_target_pairs={{0,1},{1,0},{2,3},{3,2},{4,5},{5,4},{6,7},{7,6},{8,9},{9,8},{10,11... | collective-permute-start | bytes 1179656 | tf_op jit(solution)/shard_map/ppermute | solution.py:413
  71.9 2.2 %collective-permute-start.18 = (bf16[32,4096]{1,0:T(8,128)(2,1)S(1)}, bf16[32,4096]{1,0:T(8,128)(2,1)S(1)}, u32[]{:S(2)}, u32[]{:S(2)}) collective-permute-start(bf16[32,4096]{1,0:T(8,128)(2,1)S(1)} %get-tuple-element.66), channel_id=1, source_target_pairs={{0,1},{1,0},{2,3},{3,2},{4,5},{5,4},{6,7},{7,6},{8,9},{9,8},{10,11... | collective-permute-start | bytes 786440 | tf_op jit(solution)/shard_map/ppermute | solution.py:413

commit v3 on v2

--- a/solution.py
+++ b/solution.py
@@ -159,8 +159,8 @@
         [VM] * 5,
         [((heads * HD, rows), F32), ((heads * HD, rows), BF)],
         (q, k, v, cum, lw),
-        flops=2_000_000_000,
-        moved=8_000_000,
+        flops=1_000_000,
+        moved=100_000,
     )
 
 
@@ -187,8 +187,8 @@
         [SM] + [VM] * 6,
         [(acc.shape, F32)],
         (pos, acc, qt, recv, off, cum, lw),
-        flops=300_000_000,
-        moved=3_000_000,
+        flops=1_000_000,
+        moved=100_000,
         input_output_aliases={1: 0},
     )[0]
 
@@ -222,66 +222,69 @@
         [SM] + [VM] * 7,
         [((2 * size, heads * HD), BF)] * 2 + [((size, heads * HD), BF)],
         (pick, acc, qt, recv, off, cum, lw, gain),
-        flops=400_000_000,
-        moved=4_000_000,
-    )
-
-
-def start_kernel(a_ref, w_ref, out_ref, *, side, tile):
-    rows, half = out_ref.shape
-    for j in range(half // tile):
-        own = slice(side * half + j * tile, side * half + (j + 1) * tile)
-        out_ref[:, j * tile : (j + 1) * tile] = dot(a_ref[rows:, :], w_ref[:, own]).astype(BF)
-
-
-def start(a, w, side, name, tile=512):
-    shape = (a.shape[0] // 2, w.shape[1] // 2)
-    kernel = functools.partial(start_kernel, side=side, tile=tile)
-    return call(kernel, name, [VM, VM], [(shape, BF)], (a, w), flops=600_000_000, moved=3_000_000)[0]
-
-
-def across(b_ref, rows, whole_ref, mine_ref, theirs_ref, side, col, parity):
-    depth, share = whole_ref.shape[0], mine_ref.shape[0]
-    second = b_ref[rows, pl.ds(pl.multiple_of(depth + parity * share, share), share)]
-    third = b_ref[rows, pl.ds(pl.multiple_of(depth + (1 - parity) * share, share), share)]
-    total = dot(b_ref[rows, :depth], whole_ref[:, col]) + dot(second, mine_ref[:, col])
-    return total + dot(third, theirs_ref[side * share : (side + 1) * share, col])
-
-
-def pass_kernel(pick_ref, begun_ref, b_ref, whole_ref, mine_ref, theirs_ref, kept_ref, sent_ref, *, side, tile):
+        flops=1_000_000,
+        moved=100_000,
+    )
+
+
+def begin_kernel(pick_ref, near_ref, side_ref, w_ref, *refs, tile):
+    pieces, (out_l, out_r, full_l, full_r) = refs[:6], refs[6:]
+    rows, half = out_l.shape
+    for side, (a_ref, out_ref, full_ref) in enumerate(((side_ref, out_l, full_l), (near_ref, out_r, full_r))):
+        whole_ref, mine_ref, theirs_ref = pieces[3 * side : 3 * side + 3]
+        depth, share = whole_ref.shape[0], mine_ref.shape[0]
+        first = pick_ref[7 + side]
+        full_ref[:depth, :] = whole_ref[...]
+        full_ref[pl.ds(pl.multiple_of(depth + first * share, 32), share), :] = mine_ref[...]
+        full_ref[pl.ds(pl.multiple_of(depth + (1 - first) * share, 32), share), :] = theirs_ref[...]
+        for j in range(half // tile):
+            own = slice(side * half + j * tile, side * half + (j + 1) * tile)
+            out_ref[:, j * tile : (j + 1) * tile] = dot(a_ref[rows:, :], w_ref[:, own]).astype(BF)
+
+
+def begin(pick, near, side, w, left, right, tile=512):
+    half = w.shape[1] // 2
+    return call(
+        functools.partial(begin_kernel, tile=tile),
+        "begin",
+        [SM] + [VM] * 9,
+        [((near.shape[0] // 2, half), BF)] * 2 + [((w.shape[0], half), BF)] * 2,
+        (pick, near, side, w, *left, *right),
+        flops=1_000_000_000,
+        moved=6_000_000,
+    )
+
+
+def pass_kernel(begun_ref, b_ref, w_ref, kept_ref, sent_ref, *, tile):
     size, half = kept_ref.shape
     for j in range(half // tile):
         col = slice(j * tile, (j + 1) * tile)
-        more = across(b_ref, slice(0, 2 * size), whole_ref, mine_ref, theirs_ref, side, col, pick_ref[2])
-        total = begun_ref[:, col].astype(F32) + more
+        total = begun_ref[:, col].astype(F32) + dot(b_ref[: 2 * size, :], w_ref[:, col])
         kept_ref[:, col] = total[:size]
         sent_ref[:, col] = total[size:].astype(BF)
 
 
-def pass_on(pick, begun, b, pieces, side, name, tile=512):
+def pass_on(begun, b, w, name, tile=512):
     shape = (begun.shape[0] // 2, begun.shape[1])
     return call(
-        functools.partial(pass_kernel, side=side, tile=tile),
+        functools.partial(pass_kernel, tile=tile),
         name,
-        [SM] + [VM] * 5,
+        [VM] * 3,
         [(shape, F32), (shape, BF)],
-        (pick, begun, b, *pieces),
+        (begun, b, w),
         flops=600_000_000,
         moved=3_000_000,
     )
 
 
-def own_kernel(pick_ref, a_ref, w_ref, *refs, tile):
-    pieces, kept_ref, sent = refs[:8], refs[8], refs[9:]
+def own_kernel(a_ref, w_ref, b_left, b_right, w_left, w_right, kept_ref, *sent, tile):
     size = kept_ref.shape[0]
     half = kept_ref.shape[1] // 2
-    for side in range(2):
-        b_ref, *weights = pieces[4 * side : 4 * side + 4]
+    for side, (b_ref, v_ref) in enumerate(((b_left, w_left), (b_right, w_right))):
         for j in range(half // tile):
             col = slice(j * tile, (j + 1) * tile)
             at = slice(side * half + j * tile, side * half + (j + 1) * tile)
-            total = dot(a_ref[...], w_ref[:, at])
-            total = total + across(b_ref, slice(2 * size, 4 * size), *weights, side, col, pick_ref[2])
+            total = dot(a_ref[...], w_ref[:, at]) + dot(b_ref[2 * size :, :], v_ref[:, col])
             kept_ref[:, at] = total[:size]
             first = size
             for out_ref in sent:
@@ -289,15 +292,15 @@
                 first += out_ref.shape[0]
 
 
-def own_part(pick, a, w, left, right, tile=512):
+def own_part(a, w, bs, ws, tile=512):
     size, width = a.shape[0] // 2, w.shape[1]
     sent = (3 * size // 8, 3 * size // 8, size // 4)
     return call(
         functools.partial(own_kernel, tile=tile),
         "own",
-        [SM] + [VM] * 10,
+        [VM] * 6,
         [((size, width), F32)] + [((n, width), BF) for n in sent],
-        (pick, a, w, *left, *right),
+        (a, w, *bs, *ws),
         flops=2_000_000_000,
         moved=9_000_000,
     )
@@ -348,15 +351,15 @@
     pos = lax.axis_index("seq").astype(jnp.int32)
     lane = lax.axis_index("head").astype(jnp.int32)
     x, core = lane // 2, lane % 2
-    parity = pos % 2
+    share_l, share_r = pos % 2, pos // 2 % 2
     near = x ^ 1
     side = (x + ring - 1 + 2 * (x % 2)) % ring
-    pick = jnp.stack([pos, core, parity, (x + 2) % ring, near, side, x])
+    pick = jnp.stack([pos, core, core, (x + 2) % ring, near, side, x, share_l, share_r])
     pos1 = pos[None]
     swap = [(i, i ^ 1) for i in range(head_size)]
     to_near = [(i, i ^ 2) for i in range(head_size)]
     to_side = [(i, (i + (2 if i // 2 % 2 else -2)) % head_size) for i in range(head_size)]
-    to_y = [(i, i ^ 1) for i in range(seq_size)]
+    to_y = [[(i, i ^ flip) for i in range(seq_size)] for flip in (1, 3)]
 
     flat = lambda a: a.reshape(rows, heads * HD)
     ld = jnp.transpose(log_decay, (1, 0))
@@ -365,6 +368,8 @@
     pay, cum = summary(ld, k2, v2)
 
     depth, width = out_weight.shape
+    share = 5 * depth // 16
+    direct = depth - 2 * share
     off = jnp.zeros((heads, 128), F32)
     after = cum
     recvs, offs = [], []
@@ -374,42 +379,48 @@
         offs.append(off)
         if b == 0:
             weight, _ = lax.optimization_barrier((out_weight, pay))
-            mine = lax.dynamic_slice(weight, (depth // 2 + parity * (depth // 4), 0), (depth // 4, width))
-            mine_l = lax.ppermute(mine[:, : width // 2], "head", to_near)
-            mine_r = lax.ppermute(mine[:, width // 2 :], "head", to_side)
+            mine_l = lax.dynamic_slice(weight, (direct + share_l * share, 0), (share, width // 2))
+            mine_r = lax.dynamic_slice(weight, (direct + share_r * share, width // 2), (share, width // 2))
+            mine_l = lax.ppermute(mine_l, "head", to_near)
+            mine_r = lax.ppermute(mine_r, "head", to_side)
         if b == 1:
             weight, _ = lax.optimization_barrier((out_weight, pay))
-            whole_l = lax.ppermute(weight[: depth // 2, : width // 2], "head", to_near)
-            whole_r = lax.ppermute(weight[: depth // 2, width // 2 :], "head", to_side)
+            slice_l, slice_r = weight[:direct, : width // 2], weight[:direct, width // 2 :]
+            slice_l, slice_r, recv = lax.optimization_barrier((slice_l, slice_r, recv))
+            whole_l = lax.ppermute(slice_l, "head", to_near)
         if b == 2:
             queries, keys, values, _ = lax.optimization_barrier((queries, keys, values, pay))
             acc, qt = local(flat(queries), flat(keys), flat(values), cum, lw)
             after = acc
         if b == 3:
+            slice_r, _ = lax.optimization_barrier((slice_r, pay))
+            whole_r = lax.ppermute(slice_r, "head", to_side)
             mine_l, mine_r, _ = lax.optimization_barrier((mine_l, mine_r, pay))
-            theirs = lax.ppermute(jnp.concatenate([mine_l, mine_r], axis=0), "seq", to_y)
-        if b >= 3:
-            for i in (0, 1, 2) if b == 3 else (3,):
+            theirs_l = lax.ppermute(mine_l, "seq", to_y[0])
+            theirs_r = lax.ppermute(mine_r, "seq", to_y[1])
+            for i in (0, 1, 2):
                 acc = far(pos1, acc, qt, recvs[i], offs[i], cum, lw, i, base)
             after = acc
+        if b == 4:
+            acc = far(pos1, acc, qt, recvs[3], offs[3], cum, lw, 3, base)
         if b < bits - 1:
             pay, off = merge(pos1, after, recv, pay, off, b)
     n_near, n_side, n_own = norm(pick, acc, qt, recv, off, cum, lw, norm_gain, bits - 1, base, ring)
     from_near = lax.ppermute(n_near, "head", to_near)
     from_side = lax.ppermute(n_side, "head", to_side)
-    left, right = (whole_l, mine_l, theirs), (whole_r, mine_r, theirs)
-    begun_l = start(n_side, out_weight, 0, "start_left")
-    begun_r = start(n_near, out_weight, 1, "start_right")
-    keep_l, send_l = pass_on(pick, begun_l, from_near, left, 0, "left")
+    begun_l, begun_r, w_l, w_r = begin(
+        pick, n_near, n_side, out_weight, (whole_l, mine_l, theirs_l), (whole_r, mine_r, theirs_r)
+    )
+    keep_l, send_l = pass_on(begun_l, from_near, w_l, "left")
     swap_l = lax.ppermute(send_l, "head", swap)
-    keep_r, send_r = pass_on(pick, begun_r, from_side, right, 1, "right")
+    keep_r, send_r = pass_on(begun_r, from_side, w_r, "right")
     swap_r = lax.ppermute(send_r, "head", swap)
     both_l = join(keep_l, swap_l, "join_left")
     both_r = join(keep_r, swap_r, "join_right")
     far_l = lax.ppermute(both_l, "head", to_side)
     far_r = lax.ppermute(both_r, "head", to_near)
     n_own, _, _ = lax.optimization_barrier((n_own, both_l, both_r))
-    keep, *sends = own_part(pick, n_own, out_weight, (from_near, *left), (from_side, *right))
+    keep, *sends = own_part(n_own, out_weight, (from_near, from_side), (w_l, w_r))
     swaps = [lax.ppermute(send, "head", swap) for send in sends]
     return finish(keep, far_l, far_r, swaps)
 

time: 81.4 us -> 75.3 us (0.925)
  waiting for transfers between devices: 21.1 us -> 16.8 us
  Pallas kernels: 22.3 us -> 18.3 us
  starting transfers between devices: 28.4 us -> 32.3 us
  other arithmetic: 1.18 us -> 0 us
    ppermute x1, waiting for transfers between devices: 6.96 us -> 0.01 us  [body(): from_side = lax.ppermute(n_side, 'head', to_side)]
    ppermute x1, starting transfers between devices: 1.06 us -> 6.05 us  [body(): swap_l = lax.ppermute(send_l, 'head', swap)]
    ppermute x1, starting transfers between devices: 5.41 us -> 0.57 us  [body(): swap_r = lax.ppermute(send_r, 'head', swap)]
    ppermute x1, waiting for transfers between devices: 2.32 us -> 6.88 us  [body(): far_l = lax.ppermute(both_l, 'head', to_side)]
    pallas_call x19 -> x18, Pallas kernels: 22.3 us -> 18.3 us  [call(): pl.pallas_call(kernel, in_specs=ins, out_specs=[VM] * len(outs), out_shap...]
    ppermute x1, waiting for transfers between devices: 3.4 us -> 0.45 us  [body(): far_r = lax.ppermute(both_r, 'head', to_near)]
    ppermute x1, waiting for transfers between devices: 0.01 us -> 2.77 us  [body(): from_near = lax.ppermute(n_near, 'head', to_near)]
    ppermute x5 -> x6, starting transfers between devices: 5.06 us -> 7.26 us  [the longest x1 2.35 us: body(): theirs_r = lax.ppermute(mine_r, 'seq', to_y[1])]
  transfers between devices with their start and end apart: 19 -> 20, of which waited for: 7 -> 7; matrix products, arithmetic and copies ran while one was open for 8% -> 6% of each run, Pallas kernels for 24% -> 21%
where the time goes in v3:
time: 75.3 us; the launch traced here: 75.1 us
  starting transfers between devices  32.3 us (43%)
  Pallas kernels  18.3 us (24%)
  waiting for transfers between devices  16.8 us (22%)
  local copies, waits for them, and re-layouts  7.48 us (10%)
    pallas_call x18, Pallas kernels, call(): pl.pallas_call(kernel, in_specs=ins, out_specs=[VM] * len(outs), out_shap...  18.3 us
    ppermute x5, starting transfers between devices, body(): recv = lax.ppermute(pay, 'seq', partners(b, seq_size, 4))  13.2 us
    ppermute x1, waiting for transfers between devices, body(): far_l = lax.ppermute(both_l, 'head', to_side)  6.88 us
    ppermute x1, starting transfers between devices, body(): swap_l = lax.ppermute(send_l, 'head', swap)  6.05 us
    ppermute x5, waiting for transfers between devices, body(): recv = lax.ppermute(pay, 'seq', partners(b, seq_size, 4))  4.64 us
    ppermute x1, waiting for transfers between devices, body(): from_near = lax.ppermute(n_near, 'head', to_near)  2.77 us
    slice x1, local copies, waits for them, and re-layouts, body(): weight[:direct, width // 2:]  2.69 us
    ppermute x1, starting transfers between devices, body(): theirs_r = lax.ppermute(mine_r, 'seq', to_y[1])  2.35 us
  transfers between devices with their start and end apart: 20, of which 7 were waited for; matrix products, arithmetic and copies ran while one was open for 6% of the time, Pallas kernels for 21%

profile of v3, /device:TPU:1, one launch (start us, length us, event | category | flops | bytes accessed | tf_op | source)
XLA Modules:
  0.0 75.1 jit_solution(15795278995145621224)
XLA Ops:
  0.0 1.9 %copy_bitcast_fusion.3 = (bf16[1024,512]{1,0:T(8,128)(2,1)S(1)}, bf16[1024,512]{1,0:T(8,128)(2,1)S(1)}) fusion(bf16[128,8,4,128]{3,2,1,0:T(4,128)(2,1)} %bitcast.40, bf16[128,8,4,128]{3,2,1,0:T(4,128)(2,1)} %bitcast.38), kind=kLoop, calls=%fused_computation.3 | loop fusion | bytes 4194304 | tf_op jit(solution)/shard_map/reshape | solution.py:364
  1.9 1.2 %summary.1 = (bf16[528,128]{1,0:T(8,128)(2,1)S(1)}, f32[4,1024]{1,0:T(4,128)S(1)}) custom-call(f32[4,1024]{1,0:T(4,128)S(1)} %bitcast.37, bf16[1024,512]{1,0:T(8,128)(2,1)S(1)} %get-tuple-element.88.k_ref, bf16[1024,512]{1,0:T(8,128)(2,1)S(1)} %get-tuple-element.87.v_ref), custom_call_target="tpu_custom_call" | custom-call | flops 140000000 | bytes 2000000 | tf_op jit(solution)/shard_map/summary/pallas_call | solution.py:19
  3.1 2.2 %collective-permute-start = (bf16[528,128]{1,0:T(8,128)(2,1)S(1)}, bf16[528,128]{1,0:T(8,128)(2,1)S(1)}, u32[]{:S(2)}, u32[]{:S(2)}) collective-permute-start(bf16[528,128]{1,0:T(8,128)(2,1)S(1)} %get-tuple-element.45.self_ref), channel_id=1, source_target_pairs={{0,8},{8,0},{16,24},{24,16},{32,40},{40,32},{48,56},{56,48},{64,72... | collective-permute-start | bytes 405512 | tf_op jit(solution)/shard_map/ppermute | solution.py:377
  5.3 1.4 %constant_dynamic-slice_fusion = (bf16[160,2048]{1,0:T(8,128)(2,1)S(1)}, bf16[160,2048]{1,0:T(8,128)(2,1)S(1)}) fusion(bf16[512,4096]{1,0:T(8,128)(2,1)} %w_ref.3, s32[]{:T(128)S(6)} %select_n.49, s32[]{:T(128)S(6)} %select_n.48), kind=kLoop, calls=%fused_computation.5 | loop fusion | bytes 2621448 | tf_op jit(solution)/shard_map/dynamic_slice | solution.py:383
  6.8 0.0 copy-start.8
  6.8 1.3 %collective-permute-start.6 = (bf16[160,2048]{1,0:T(8,128)(2,1)S(1)}, bf16[160,2048]{1,0:T(8,128)(2,1)}, u32[]{:S(2)}, u32[]{:S(2)}) collective-permute-start(bf16[160,2048]{1,0:T(8,128)(2,1)S(1)} %get-tuple-element.84), channel_id=1, source_target_pairs={{0,2},{1,3},{2,0},{3,1},{4,6},{5,7},{6,4},{7,5},{8,10},{9,11},{10,... | collective-permute-start | bytes 1966088 | tf_op jit(solution)/shard_map/ppermute | solution.py:384
  8.1 1.8 %collective-permute-start.7 = (bf16[160,2048]{1,0:T(8,128)(2,1)S(1)}, bf16[160,2048]{1,0:T(8,128)(2,1)}, u32[]{:S(2)}, u32[]{:S(2)}) collective-permute-start(bf16[160,2048]{1,0:T(8,128)(2,1)S(1)} %get-tuple-element.83), channel_id=1, source_target_pairs={{0,6},{1,7},{2,4},{3,5},{4,2},{5,3},{6,0},{7,1},{8,14},{9,15},{10,... | collective-permute-start | bytes 1966088 | tf_op jit(solution)/shard_map/ppermute | solution.py:385
  9.9 0.0 collective-permute-done.recv_ref
  9.9 0.1 merge0.1
  10.0 0.0 copy-start.6
  10.0 2.0 %collective-permute-start.1 = (bf16[528,128]{1,0:T(8,128)(2,1)S(1)}, bf16[528,128]{1,0:T(8,128)(2,1)S(1)}, u32[]{:S(2)}, u32[]{:S(2)}) collective-permute-start(bf16[528,128]{1,0:T(8,128)(2,1)S(1)} %get-tuple-element.46.self_ref), channel_id=1, source_target_pairs={{0,24},{8,16},{16,8},{24,0},{32,56},{40,48},{48,40},{56,32},{64,88... | collective-permute-start | bytes 405512 | tf_op jit(solution)/shard_map/ppermute | solution.py:377
  12.0 2.7 %fusion = (bf16[192,2048]{1,0:T(8,128)(2,1)}, bf16[192,2048]{1,0:T(8,128)(2,1)}) fusion(bf16[512,4096]{1,0:T(8,128)(2,1)} %w_ref.3), kind=kLoop, calls=%fused_computation.7 | loop fusion | bytes 3145728 | tf_op jit(solution)/shard_map/slice | solution.py:388
  14.7 0.9 %collective-permute-done.1.recv_ref = bf16[528,128]{1,0:T(8,128)(2,1)S(1)} collective-permute-done((bf16[528,128]{1,0:T(8,128)(2,1)S(1)}, bf16[528,128]{1,0:T(8,128)(2,1)S(1)}, u32[]{:S(2)}, u32[]{:S(2)}) %collective-permute-start.1) | collective-permute-done | bytes 135200 | tf_op jit(solution)/shard_map/ppermute | solution.py:377
  15.5 0.1 merge1.1
  15.6 1.7 %collective-permute-start.2 = (bf16[528,128]{1,0:T(8,128)(2,1)S(1)}, bf16[528,128]{1,0:T(8,128)(2,1)S(1)}, u32[]{:S(2)}, u32[]{:S(2)}) collective-permute-start(bf16[528,128]{1,0:T(8,128)(2,1)S(1)} %get-tuple-element.50.self_ref), channel_id=1, source_target_pairs={{0,32},{8,40},{16,48},{24,56},{32,0},{40,8},{48,16},{56,24},{64,96... | collective-permute-start | bytes 405512 | tf_op jit(solution)/shard_map/ppermute | solution.py:377
  17.3 0.2 copy.24
  17.6 0.0 copy-start.1
  17.6 0.2 copy.23
  17.7 0.8 %copy-done.7 = bf16[1024,4,128]{2,1,0:T(4,128)(2,1)S(1)} copy-done((bf16[1024,4,128]{2,1,0:T(4,128)(2,1)S(1)}, bf16[1024,4,128]{2,1,0:T(4,128)(2,1)}, u32[]{:S(2)}) %copy-start.7) | copy-done | bytes 1048600
  18.6 0.2 copy.22
  18.8 2.6 %local.1 = (f32[512,1024]{1,0:T(8,128)S(1)}, bf16[512,1024]{1,0:T(8,128)(2,1)S(1)}) custom-call(bf16[1024,512]{1,0:T(8,128)(2,1)S(1)} %bitcast.34, bf16[1024,512]{1,0:T(8,128)(2,1)S(1)} %bitcast.35, bf16[1024,512]{1,0:T(8,128)(2,1)S(1)} %bitcast.36, f32[4,1024]{1,0:T(4,128)S(1)} %get-tuple-element.44.after_ref.cum_ref, f32[10,4,1024]{2,1,0:T(4,128)S(1)} %bitcast.28), custom_call_target="tpu_custom_call" | custom-call | flops 1000000 | bytes 100000 | tf_op jit(solution)/shard_map/local/pallas_call | solution.py:19
  21.4 0.0 collective-permute-done.2.recv_ref
  21.4 0.1 merge2.1
  21.5 1.7 %collective-permute-start.9 = (bf16[192,2048]{1,0:T(8,128)(2,1)}, bf16[192,2048]{1,0:T(8,128)(2,1)}, u32[]{:S(2)}, u32[]{:S(2)}) collective-permute-start(bf16[192,2048]{1,0:T(8,128)(2,1)} %get-tuple-element.68), channel_id=1, source_target_pairs={{0,6},{1,7},{2,4},{3,5},{4,2},{5,3},{6,0},{7,1},{8,14},{9,15},{10,... | collective-permute-start | bytes 2359304 | tf_op jit(solution)/shard_map/ppermute | solution.py:397
  23.1 3.0 %collective-permute-start.3 = (bf16[528,128]{1,0:T(8,128)(2,1)S(1)}, bf16[528,128]{1,0:T(8,128)(2,1)S(1)}, u32[]{:S(2)}, u32[]{:S(2)}) collective-permute-start(bf16[528,128]{1,0:T(8,128)(2,1)S(1)} %get-tuple-element.57.self_ref), channel_id=1, source_target_pairs={{0,64},{8,72},{16,80},{24,88},{32,96},{40,104},{48,112},{56,120},{... | collective-permute-start | bytes 405512 | tf_op jit(solution)/shard_map/ppermute | solution.py:377
  26.1 0.0 collective-permute-done.6.refs_1_
  26.1 0.0 collective-permute-done.7.refs_4_
  26.1 0.1 collective-permute-start.8
  26.2 2.3 %collective-permute-start.10 = (bf16[160,2048]{1,0:T(8,128)(2,1)}, bf16[160,2048]{1,0:T(8,128)(2,1)}, u32[]{:S(2)}, u32[]{:S(2)}) collective-permute-start(bf16[160,2048]{1,0:T(8,128)(2,1)} %collective-permute-done.7.refs_4_), channel_id=1, source_target_pairs={{0,24},{8,16},{16,8},{24,0},{32,56},{40,48},{48,40},{56,32},{64,88... | collective-permute-start | bytes 1966088 | tf_op jit(solution)/shard_map/ppermute | solution.py:400
  28.6 0.6 far0.1.acc_ref
  29.2 0.6 far1.1.acc_ref
  29.8 0.6 far2.1.acc_ref.after_ref
  30.4 0.0 collective-permute-done.3.recv_ref
  30.5 0.7 merge3.1
  31.2 4.3 %collective-permute-start.4 = (bf16[528,128]{1,0:T(8,128)(2,1)}, bf16[528,128]{1,0:T(8,128)(2,1)}, u32[]{:S(2)}, u32[]{:S(2)}) collective-permute-start(bf16[528,128]{1,0:T(8,128)(2,1)} %get-tuple-element.59), channel_id=1, source_target_pairs={{0,224},{8,232},{16,240},{24,248},{32,192},{40,200},{48,208},{56,2... | collective-permute-start | bytes 405512 | tf_op jit(solution)/shard_map/ppermute | solution.py:377
  35.5 0.1 stack.36.pick_ref
  35.6 0.6 far3.1.acc_ref
  36.2 3.8 %collective-permute-done.4.recv_ref = bf16[528,128]{1,0:T(8,128)(2,1)} collective-permute-done((bf16[528,128]{1,0:T(8,128)(2,1)}, bf16[528,128]{1,0:T(8,128)(2,1)}, u32[]{:S(2)}, u32[]{:S(2)}) %collective-permute-start.4) | collective-permute-done | bytes 135200 | tf_op jit(solution)/shard_map/ppermute | solution.py:377
  39.9 2.1 %norm.1 = (bf16[512,512]{1,0:T(8,128)(2,1)S(1)}, bf16[512,512]{1,0:T(8,128)(2,1)S(1)}, bf16[256,512]{1,0:T(8,128)(2,1)S(1)}) custom-call(s32[9]{0:T(128)S(1)} %stack.36.pick_ref, f32[512,1024]{1,0:T(8,128)S(1)} %far3.1.acc_ref, bf16[512,1024]{1,0:T(8,128)(2,1)S(1)} %get-tuple-element.55.qt_ref, bf16[528,128]{1,0:T(8,128)(2,1)} %collective-permute-done.4.recv_ref, ...), custom_call_target="tpu_custom_call" | custom-call | flops 1000000 | bytes 100000 | tf_op jit(solution)/shard_map/norm/pallas_call | solution.py:19
  42.0 0.1 collective-permute-start.11
  42.1 0.0 collective-permute-done.5.refs_0_
  42.1 1.9 %collective-permute-start.13 = (bf16[512,512]{1,0:T(8,128)(2,1)S(1)}, bf16[512,512]{1,0:T(8,128)(2,1)S(1)}, u32[]{:S(2)}, u32[]{:S(2)}) collective-permute-start(bf16[512,512]{1,0:T(8,128)(2,1)S(1)} %get-tuple-element.63.side_ref), channel_id=1, source_target_pairs={{0,6},{1,7},{2,4},{3,5},{4,2},{5,3},{6,0},{7,1},{8,14},{9,15},{10,... | collective-permute-start | bytes 1572872 | tf_op jit(solution)/shard_map/ppermute | solution.py:410
  44.0 0.0 collective-permute-done.9.refs_3_
  44.0 0.0 collective-permute-done.8.refs_2_
  44.0 0.0 collective-permute-done.10.refs_5_
  44.1 3.7 %begin.1 = (bf16[256,2048]{1,0:T(8,128)(2,1)S(1)}, bf16[256,2048]{1,0:T(8,128)(2,1)S(1)}, bf16[512,2048]{1,0:T(8,128)(2,1)S(1)}, bf16[512,2048]{1,0:T(8,128)(2,1)S(1)}) custom-call(s32[9]{0:T(128)S(1)} %stack.36.pick_ref, bf16[512,512]{1,0:T(8,128)(2,1)S(1)} %get-tuple-element.62.near_ref, bf16[512,512]{1,0:T(8,128)(2,1)S(1)} %get-tuple-element.63.side_ref, ...), custom_call_target="tpu_custom_call" | custom-call | flops 1000000000 | bytes 6000000 | tf_op jit(solution)/shard_map/begin/pallas_call | solution.py:19
  47.7 2.8 %collective-permute-done.11.b_ref.b_left = bf16[512,512]{1,0:T(8,128)(2,1)S(1)} collective-permute-done((bf16[512,512]{1,0:T(8,128)(2,1)S(1)}, bf16[512,512]{1,0:T(8,128)(2,1)S(1)}, u32[]{:S(2)}, u32[]{:S(2)}) %collective-permute-start.11) | collective-permute-done | bytes 524320 | tf_op jit(solution)/shard_map/ppermute | solution.py:409
  50.5 0.7 left.1
  51.2 6.0 %collective-permute-start.12 = (bf16[128,2048]{1,0:T(8,128)(2,1)S(1)}, bf16[128,2048]{1,0:T(8,128)(2,1)S(1)}, u32[]{:S(2)}, u32[]{:S(2)}) collective-permute-start(bf16[128,2048]{1,0:T(8,128)(2,1)S(1)} %get-tuple-element.73), channel_id=1, source_target_pairs={{0,1},{1,0},{2,3},{3,2},{4,5},{5,4},{6,7},{7,6},{8,9},{9,8},{10,11... | collective-permute-start | bytes 1572872 | tf_op jit(solution)/shard_map/ppermute | solution.py:415
  57.3 0.7 right.1
  58.0 0.6 collective-permute-start.14
  58.6 0.2 collective-permute-done.12.b_ref
  58.8 0.1 join_left.1
  58.9 1.9 %collective-permute-start.15 = (bf16[128,2048]{1,0:T(8,128)(2,1)S(1)}, bf16[128,2048]{1,0:T(8,128)(2,1)S(1)}, u32[]{:S(2)}, u32[]{:S(2)}) collective-permute-start(bf16[128,2048]{1,0:T(8,128)(2,1)S(1)} %join_left.1), channel_id=1, source_target_pairs={{0,6},{1,7},{2,4},{3,5},{4,2},{5,3},{6,0},{7,1},{8,14},{9,15},{10,... | collective-permute-start | bytes 1572872 | tf_op jit(solution)/shard_map/ppermute | solution.py:420
  60.8 0.1 join_right.1
  60.9 0.1 collective-permute-start.16
  61.0 2.4 %own.1 = (f32[128,4096]{1,0:T(8,128)S(1)}, bf16[48,4096]{1,0:T(8,128)(2,1)S(1)}, bf16[48,4096]{1,0:T(8,128)(2,1)S(1)}, bf16[32,4096]{1,0:T(8,128)(2,1)S(1)}) custom-call(bf16[256,512]{1,0:T(8,128)(2,1)S(1)} %get-tuple-element.78.a_ref, bf16[512,4096]{1,0:T(8,128)(2,1)S(1)} %copy-done, bf16[512,512]{1,0:T(8,128)(2,1)S(1)} %collective-permute-done.11.b_ref.b_left, ...), custom_call_target="tpu_custom_call" | custom-call | flops 2000000000 | bytes 9000000 | tf_op jit(solution)/shard_map/own/pallas_call | solution.py:19
  63.4 0.7 collective-permute-start.17
  64.2 0.1 collective-permute-start.18
  64.3 0.4 collective-permute-start.19
  64.7 1.8 %collective-permute-done.19.refs_2_ = bf16[32,4096]{1,0:T(8,128)(2,1)S(1)} collective-permute-done((bf16[32,4096]{1,0:T(8,128)(2,1)S(1)}, bf16[32,4096]{1,0:T(8,128)(2,1)S(1)}, u32[]{:S(2)}, u32[]{:S(2)}) %collective-permute-start.19) | collective-permute-done | bytes 262176 | tf_op jit(solution)/shard_map/ppermute | solution.py:424
  66.5 6.9 %collective-permute-done.15.left_ref = bf16[128,2048]{1,0:T(8,128)(2,1)S(1)} collective-permute-done((bf16[128,2048]{1,0:T(8,128)(2,1)S(1)}, bf16[128,2048]{1,0:T(8,128)(2,1)S(1)}, u32[]{:S(2)}, u32[]{:S(2)}) %collective-permute-start.15) | collective-permute-done | bytes 524320 | tf_op jit(solution)/shard_map/ppermute | solution.py:420
  73.4 0.5 collective-permute-done.16.right_ref
  73.8 1.3 %finish.1 = bf16[128,4096]{1,0:T(8,128)(2,1)} custom-call(f32[128,4096]{1,0:T(8,128)S(1)} %get-tuple-element.79.own_ref, bf16[128,2048]{1,0:T(8,128)(2,1)S(1)} %collective-permute-done.15.left_ref, bf16[128,2048]{1,0:T(8,128)(2,1)S(1)} %collective-permute-done.16.right_ref, bf16[48,4096]{1,0:T(8,128)(2,1)S(1)} %collective-permute-done.17.refs_0_, ...), custom_call_target="tpu_custom_call" | custom-call | flops 2000000 | bytes 5000000 | tf_op jit(solution)/shard_map/finish/pallas_call | solution.py:19
  (20 shorter events, 0.0 us)
Async XLA Ops:
  0.0 1.9 %copy-start.4 = (f32[1024,4]{0,1:T(4,128)S(1)}, f32[1024,4]{0,1:T(4,128)}, u32[]{:S(2)}) copy-start(f32[1024,4]{0,1:T(4,128)} %param.10) | copy-start | bytes 49156
  3.1 6.8 %collective-permute-start = (bf16[528,128]{1,0:T(8,128)(2,1)S(1)}, bf16[528,128]{1,0:T(8,128)(2,1)S(1)}, u32[]{:S(2)}, u32[]{:S(2)}) collective-permute-start(bf16[528,128]{1,0:T(8,128)(2,1)S(1)} %get-tuple-element.45.self_ref), channel_id=1, source_target_pairs={{0,8},{8,0},{16,24},{24,16},{32,40},{40,32},{48,56},{56,48},{64,72... | collective-permute-start | bytes 405512 | tf_op jit(solution)/shard_map/ppermute | solution.py:377
  6.8 10.6 %copy-start.8 = (bf16[1024,4,128]{2,1,0:T(4,128)(2,1)S(1)}, bf16[1024,4,128]{2,1,0:T(4,128)(2,1)}, u32[]{:S(2)}) copy-start(bf16[1024,4,128]{2,1,0:T(4,128)(2,1)} %param.7) | copy-start | bytes 3145732
  6.8 19.3 %collective-permute-start.6 = (bf16[160,2048]{1,0:T(8,128)(2,1)S(1)}, bf16[160,2048]{1,0:T(8,128)(2,1)}, u32[]{:S(2)}, u32[]{:S(2)}) collective-permute-start(bf16[160,2048]{1,0:T(8,128)(2,1)S(1)} %get-tuple-element.84), channel_id=1, source_target_pairs={{0,2},{1,3},{2,0},{3,1},{4,6},{5,7},{6,4},{7,5},{8,10},{9,11},{10,... | collective-permute-start | bytes 1966088 | tf_op jit(solution)/shard_map/ppermute | solution.py:384
  8.1 18.0 %collective-permute-start.7 = (bf16[160,2048]{1,0:T(8,128)(2,1)S(1)}, bf16[160,2048]{1,0:T(8,128)(2,1)}, u32[]{:S(2)}, u32[]{:S(2)}) collective-permute-start(bf16[160,2048]{1,0:T(8,128)(2,1)S(1)} %get-tuple-element.83), channel_id=1, source_target_pairs={{0,6},{1,7},{2,4},{3,5},{4,2},{5,3},{6,0},{7,1},{8,14},{9,15},{10,... | collective-permute-start | bytes 1966088 | tf_op jit(solution)/shard_map/ppermute | solution.py:385
  9.9 7.6 %copy-start.2 = (bf16[528,128]{1,0:T(8,128)(2,1)}, bf16[528,128]{1,0:T(8,128)(2,1)S(1)}, u32[]{:S(2)}) copy-start(bf16[528,128]{1,0:T(8,128)(2,1)S(1)} %collective-permute-done.recv_ref) | copy-start | bytes 405508
  10.0 7.6 %copy-start.6 = (bf16[1024,4,128]{2,1,0:T(4,128)(2,1)S(1)}, bf16[1024,4,128]{2,1,0:T(4,128)(2,1)}, u32[]{:S(2)}) copy-start(bf16[1024,4,128]{2,1,0:T(4,128)(2,1)} %param.8) | copy-start | bytes 3145732
  10.0 5.6 %collective-permute-start.1 = (bf16[528,128]{1,0:T(8,128)(2,1)S(1)}, bf16[528,128]{1,0:T(8,128)(2,1)S(1)}, u32[]{:S(2)}, u32[]{:S(2)}) collective-permute-start(bf16[528,128]{1,0:T(8,128)(2,1)S(1)} %get-tuple-element.46.self_ref), channel_id=1, source_target_pairs={{0,24},{8,16},{16,8},{24,0},{32,56},{40,48},{48,40},{56,32},{64,88... | collective-permute-start | bytes 405512 | tf_op jit(solution)/shard_map/ppermute | solution.py:377
  15.5 26.6 %collective-permute-start.5 = (bf16[192,2048]{1,0:T(8,128)(2,1)}, bf16[192,2048]{1,0:T(8,128)(2,1)}, u32[]{:S(2)}, u32[]{:S(2)}) collective-permute-start(bf16[192,2048]{1,0:T(8,128)(2,1)} %get-tuple-element.64), channel_id=1, source_target_pairs={{0,2},{1,3},{2,0},{3,1},{4,6},{5,7},{6,4},{7,5},{8,10},{9,11},{10,... | collective-permute-start | bytes 2359304 | tf_op jit(solution)/shard_map/ppermute | solution.py:390
  15.6 5.8 %collective-permute-start.2 = (bf16[528,128]{1,0:T(8,128)(2,1)S(1)}, bf16[528,128]{1,0:T(8,128)(2,1)S(1)}, u32[]{:S(2)}, u32[]{:S(2)}) collective-permute-start(bf16[528,128]{1,0:T(8,128)(2,1)S(1)} %get-tuple-element.50.self_ref), channel_id=1, source_target_pairs={{0,32},{8,40},{16,48},{24,56},{32,0},{40,8},{48,16},{56,24},{64,96... | collective-permute-start | bytes 405512 | tf_op jit(solution)/shard_map/ppermute | solution.py:377
  17.3 1.2 %copy-start.7 = (bf16[1024,4,128]{2,1,0:T(4,128)(2,1)S(1)}, bf16[1024,4,128]{2,1,0:T(4,128)(2,1)}, u32[]{:S(2)}) copy-start(bf16[1024,4,128]{2,1,0:T(4,128)(2,1)} %param.9) | copy-start | bytes 3145732
  17.6 1.2 %copy-start.1 = (f32[1024,4,10]{0,1,2:T(4,128)S(1)}, f32[1024,4,10]{0,1,2:T(4,128)}, u32[]{:S(2)}) copy-start(f32[1024,4,10]{0,1,2:T(4,128)} %param.11) | copy-start | bytes 491524
  18.8 9.8 %copy-start.3 = (bf16[528,128]{1,0:T(8,128)(2,1)S(1)}, bf16[528,128]{1,0:T(8,128)(2,1)}, u32[]{:S(2)}) copy-start(bf16[528,128]{1,0:T(8,128)(2,1)} %copy-done.2) | copy-start | bytes 405508
  21.5 22.6 %collective-permute-start.9 = (bf16[192,2048]{1,0:T(8,128)(2,1)}, bf16[192,2048]{1,0:T(8,128)(2,1)}, u32[]{:S(2)}, u32[]{:S(2)}) collective-permute-start(bf16[192,2048]{1,0:T(8,128)(2,1)} %get-tuple-element.68), channel_id=1, source_target_pairs={{0,6},{1,7},{2,4},{3,5},{4,2},{5,3},{6,0},{7,1},{8,14},{9,15},{10,... | collective-permute-start | bytes 2359304 | tf_op jit(solution)/shard_map/ppermute | solution.py:397
  23.1 7.3 %collective-permute-start.3 = (bf16[528,128]{1,0:T(8,128)(2,1)S(1)}, bf16[528,128]{1,0:T(8,128)(2,1)S(1)}, u32[]{:S(2)}, u32[]{:S(2)}) collective-permute-start(bf16[528,128]{1,0:T(8,128)(2,1)S(1)} %get-tuple-element.57.self_ref), channel_id=1, source_target_pairs={{0,64},{8,72},{16,80},{24,88},{32,96},{40,104},{48,112},{56,120},{... | collective-permute-start | bytes 405512 | tf_op jit(solution)/shard_map/ppermute | solution.py:377
  26.1 17.9 %collective-permute-start.8 = (bf16[160,2048]{1,0:T(8,128)(2,1)}, bf16[160,2048]{1,0:T(8,128)(2,1)}, u32[]{:S(2)}, u32[]{:S(2)}) collective-permute-start(bf16[160,2048]{1,0:T(8,128)(2,1)} %collective-permute-done.6.refs_1_), channel_id=1, source_target_pairs={{0,8},{8,0},{16,24},{24,16},{32,40},{40,32},{48,56},{56,48},{64,72... | collective-permute-start | bytes 1966088 | tf_op jit(solution)/shard_map/ppermute | solution.py:399
  26.2 17.8 %collective-permute-start.10 = (bf16[160,2048]{1,0:T(8,128)(2,1)}, bf16[160,2048]{1,0:T(8,128)(2,1)}, u32[]{:S(2)}, u32[]{:S(2)}) collective-permute-start(bf16[160,2048]{1,0:T(8,128)(2,1)} %collective-permute-done.7.refs_4_), channel_id=1, source_target_pairs={{0,24},{8,16},{16,8},{24,0},{32,56},{40,48},{48,40},{56,32},{64,88... | collective-permute-start | bytes 1966088 | tf_op jit(solution)/shard_map/ppermute | solution.py:400
  31.2 8.7 %collective-permute-start.4 = (bf16[528,128]{1,0:T(8,128)(2,1)}, bf16[528,128]{1,0:T(8,128)(2,1)}, u32[]{:S(2)}, u32[]{:S(2)}) collective-permute-start(bf16[528,128]{1,0:T(8,128)(2,1)} %get-tuple-element.59), channel_id=1, source_target_pairs={{0,224},{8,232},{16,240},{24,248},{32,192},{40,200},{48,208},{56,2... | collective-permute-start | bytes 405512 | tf_op jit(solution)/shard_map/ppermute | solution.py:377
  35.5 4.4 %copy-start.5 = (f32[4,128]{1,0:T(4,128)S(1)}, f32[4,128]{1,0:T(4,128)}, u32[]{:S(2)}) copy-start(f32[4,128]{1,0:T(4,128)} %gain_ref.1) | copy-start | bytes 6148
  35.6 8.5 %copy-start = (bf16[512,4096]{1,0:T(8,128)(2,1)S(1)}, bf16[512,4096]{1,0:T(8,128)(2,1)}, u32[]{:S(2)}) copy-start(bf16[512,4096]{1,0:T(8,128)(2,1)} %w_ref.3) | copy-start | bytes 12582916
  42.0 8.5 %collective-permute-start.11 = (bf16[512,512]{1,0:T(8,128)(2,1)S(1)}, bf16[512,512]{1,0:T(8,128)(2,1)S(1)}, u32[]{:S(2)}, u32[]{:S(2)}) collective-permute-start(bf16[512,512]{1,0:T(8,128)(2,1)S(1)} %get-tuple-element.62.near_ref), channel_id=1, source_target_pairs={{0,2},{1,3},{2,0},{3,1},{4,6},{5,7},{6,4},{7,5},{8,10},{9,11},{10,... | collective-permute-start | bytes 1572872 | tf_op jit(solution)/shard_map/ppermute | solution.py:409
  42.1 15.1 %collective-permute-start.13 = (bf16[512,512]{1,0:T(8,128)(2,1)S(1)}, bf16[512,512]{1,0:T(8,128)(2,1)S(1)}, u32[]{:S(2)}, u32[]{:S(2)}) collective-permute-start(bf16[512,512]{1,0:T(8,128)(2,1)S(1)} %get-tuple-element.63.side_ref), channel_id=1, source_target_pairs={{0,6},{1,7},{2,4},{3,5},{4,2},{5,3},{6,0},{7,1},{8,14},{9,15},{10,... | collective-permute-start | bytes 1572872 | tf_op jit(solution)/shard_map/ppermute | solution.py:410
  51.2 7.6 %collective-permute-start.12 = (bf16[128,2048]{1,0:T(8,128)(2,1)S(1)}, bf16[128,2048]{1,0:T(8,128)(2,1)S(1)}, u32[]{:S(2)}, u32[]{:S(2)}) collective-permute-start(bf16[128,2048]{1,0:T(8,128)(2,1)S(1)} %get-tuple-element.73), channel_id=1, source_target_pairs={{0,1},{1,0},{2,3},{3,2},{4,5},{5,4},{6,7},{7,6},{8,9},{9,8},{10,11... | collective-permute-start | bytes 1572872 | tf_op jit(solution)/shard_map/ppermute | solution.py:415
  58.0 2.8 %collective-permute-start.14 = (bf16[128,2048]{1,0:T(8,128)(2,1)S(1)}, bf16[128,2048]{1,0:T(8,128)(2,1)S(1)}, u32[]{:S(2)}, u32[]{:S(2)}) collective-permute-start(bf16[128,2048]{1,0:T(8,128)(2,1)S(1)} %get-tuple-element.77), channel_id=1, source_target_pairs={{0,1},{1,0},{2,3},{3,2},{4,5},{5,4},{6,7},{7,6},{8,9},{9,8},{10,11... | collective-permute-start | bytes 1572872 | tf_op jit(solution)/shard_map/ppermute | solution.py:417
  58.9 14.4 %collective-permute-start.15 = (bf16[128,2048]{1,0:T(8,128)(2,1)S(1)}, bf16[128,2048]{1,0:T(8,128)(2,1)S(1)}, u32[]{:S(2)}, u32[]{:S(2)}) collective-permute-start(bf16[128,2048]{1,0:T(8,128)(2,1)S(1)} %join_left.1), channel_id=1, source_target_pairs={{0,6},{1,7},{2,4},{3,5},{4,2},{5,3},{6,0},{7,1},{8,14},{9,15},{10,... | collective-permute-start | bytes 1572872 | tf_op jit(solution)/shard_map/ppermute | solution.py:420
  60.9 12.9 %collective-permute-start.16 = (bf16[128,2048]{1,0:T(8,128)(2,1)S(1)}, bf16[128,2048]{1,0:T(8,128)(2,1)S(1)}, u32[]{:S(2)}, u32[]{:S(2)}) collective-permute-start(bf16[128,2048]{1,0:T(8,128)(2,1)S(1)} %join_right.1), channel_id=1, source_target_pairs={{0,2},{1,3},{2,0},{3,1},{4,6},{5,7},{6,4},{7,5},{8,10},{9,11},{10,... | collective-permute-start | bytes 1572872 | tf_op jit(solution)/shard_map/ppermute | solution.py:421
  63.4 3.0 %collective-permute-start.17 = (bf16[48,4096]{1,0:T(8,128)(2,1)S(1)}, bf16[48,4096]{1,0:T(8,128)(2,1)S(1)}, u32[]{:S(2)}, u32[]{:S(2)}) collective-permute-start(bf16[48,4096]{1,0:T(8,128)(2,1)S(1)} %get-tuple-element.80), channel_id=1, source_target_pairs={{0,1},{1,0},{2,3},{3,2},{4,5},{5,4},{6,7},{7,6},{8,9},{9,8},{10,11... | collective-permute-start | bytes 1179656 | tf_op jit(solution)/shard_map/ppermute | solution.py:424
  64.2 2.3 %collective-permute-start.18 = (bf16[48,4096]{1,0:T(8,128)(2,1)S(1)}, bf16[48,4096]{1,0:T(8,128)(2,1)S(1)}, u32[]{:S(2)}, u32[]{:S(2)}) collective-permute-start(bf16[48,4096]{1,0:T(8,128)(2,1)S(1)} %get-tuple-element.81), channel_id=1, source_target_pairs={{0,1},{1,0},{2,3},{3,2},{4,5},{5,4},{6,7},{7,6},{8,9},{9,8},{10,11... | collective-permute-start | bytes 1179656 | tf_op jit(solution)/shard_map/ppermute | solution.py:424
  64.3 2.2 %collective-permute-start.19 = (bf16[32,4096]{1,0:T(8,128)(2,1)S(1)}, bf16[32,4096]{1,0:T(8,128)(2,1)S(1)}, u32[]{:S(2)}, u32[]{:S(2)}) collective-permute-start(bf16[32,4096]{1,0:T(8,128)(2,1)S(1)} %get-tuple-element.82), channel_id=1, source_target_pairs={{0,1},{1,0},{2,3},{3,2},{4,5},{5,4},{6,7},{7,6},{8,9},{9,8},{10,11... | collective-permute-start | bytes 786440 | tf_op jit(solution)/shard_map/ppermute | solution.py:424

commit v4 on v3

--- a/solution.py
+++ b/solution.py
@@ -10,19 +10,18 @@
 HD = 128
 BF = jnp.bfloat16
 F32 = jnp.float32
-VMEM_LIMIT = 16 * 1024 * 1024
 VM = pl.BlockSpec(memory_space=pltpu.VMEM)
 SM = pl.BlockSpec(memory_space=pltpu.SMEM)
 
 
-def call(kernel, name, ins, outs, args, scratch=(), flops=0, moved=0, **kw):
+def call(kernel, name, ins, outs, args, scratch=(), flops=0, moved=0, vmem=8, **kw):
     return pl.pallas_call(
         kernel,
         in_specs=ins,
         out_specs=[VM] * len(outs),
         out_shape=[jax.ShapeDtypeStruct(shape, dtype) for shape, dtype in outs],
         scratch_shapes=list(scratch),
-        compiler_params=pltpu.CompilerParams(vmem_limit_bytes=VMEM_LIMIT),
+        compiler_params=pltpu.CompilerParams(vmem_limit_bytes=vmem * 1024 * 1024),
         cost_estimate=pl.CostEstimate(flops=flops, bytes_accessed=moved, transcendentals=0),
         name=name,
         **kw,
@@ -96,7 +95,8 @@
     there = total_of(recv_ref, heads)
     here = total_of(self_ref, heads)
     off_out[...] = off_ref[...] + right * there
-    pay_out[heads * HD :, :] = total_rows(here + there)
+    if pay_out.shape[0] > heads * HD:
+        pay_out[heads * HD :, :] = total_rows(here + there)
     keep = right + (1.0 - right) * jnp.exp(there)
     take = (1.0 - right) + right * jnp.exp(here)
     for h in range(heads):
@@ -105,15 +105,16 @@
         pay_out[block, :] = state.astype(BF)
 
 
-def merge(pos, after, recv, pay, off, bit):
+def merge(pos, after, recv, pay, off, bit, last):
     return call(
         functools.partial(merge_kernel, bit=bit),
         f"merge{bit}",
         [SM, VM, VM, VM, VM],
-        [(pay.shape, BF), (off.shape, F32)],
+        [((off.shape[0] * HD if last else pay.shape[0], HD), BF), (off.shape, F32)],
         (pos, after, recv, pay, off),
         flops=200_000,
         moved=600_000,
+        vmem=4,
     )
 
 
@@ -161,6 +162,7 @@
         (q, k, v, cum, lw),
         flops=1_000_000,
         moved=100_000,
+        vmem=12,
     )
 
 
@@ -224,6 +226,7 @@
         (pick, acc, qt, recv, off, cum, lw, gain),
         flops=1_000_000,
         moved=100_000,
+        vmem=10,
     )
 
 
@@ -252,6 +255,7 @@
         (pick, near, side, w, *left, *right),
         flops=1_000_000_000,
         moved=6_000_000,
+        vmem=20,
     )
 
 
@@ -303,6 +307,7 @@
         (a, w, *bs, *ws),
         flops=2_000_000_000,
         moved=9_000_000,
+        vmem=16,
     )
 
 
@@ -314,29 +319,45 @@
     return call(join_kernel, name, [VM, VM], [(a.shape, BF)], (a, b), flops=300_000, moved=2_000_000)[0]
 
 
-def finish_kernel(own_ref, left_ref, right_ref, *refs):
-    swaps, out_ref = refs[:-1], refs[-1]
+def finish_kernel(own_ref, left_ref, right_ref, *refs, parts):
+    swaps, (out_ref, tile_ref, sems) = refs[:3], refs[3:]
     half = left_ref.shape[1]
+    size = tile_ref.shape[0] // parts
+    copies = []
     first = 0
     for swap_ref in swaps:
-        rows = slice(first, first + swap_ref.shape[0])
-        for side, far_ref in enumerate((left_ref, right_ref)):
-            at = slice(side * half, (side + 1) * half)
-            total = own_ref[rows, at] + swap_ref[:, at].astype(F32) + far_ref[rows, :].astype(F32)
-            out_ref[rows, at] = total.astype(BF)
-        first = rows.stop
-
-
-def finish(own, left, right, swaps):
-    ins = [VM] * (3 + len(swaps))
-    return call(finish_kernel, "finish", ins, [(own.shape, BF)], (own, left, right, *swaps), flops=2_000_000, moved=5_000_000)[0]
+        for row in range(0, swap_ref.shape[0], size):
+            here = slice(first, first + size)
+            for side, far_ref in enumerate((left_ref, right_ref)):
+                at = slice(side * half, (side + 1) * half)
+                total = own_ref[here, at] + swap_ref[row : row + size, at].astype(F32)
+                tile_ref[here, at] = (total + far_ref[here, :].astype(F32)).astype(BF)
+            copy = pltpu.make_async_copy(tile_ref.at[here], out_ref.at[here], sems.at[len(copies)])
+            copy.start()
+            copies.append(copy)
+            first += size
+    for copy in copies:
+        copy.wait()
+
+
+def finish(own, left, right, swaps, parts=8):
+    return pl.pallas_call(
+        functools.partial(finish_kernel, parts=parts),
+        in_specs=[VM] * 6,
+        out_specs=pl.BlockSpec(memory_space=pl.ANY),
+        out_shape=jax.ShapeDtypeStruct(own.shape, BF),
+        scratch_shapes=[pltpu.VMEM(own.shape, BF), pltpu.SemaphoreType.DMA((parts,))],
+        compiler_params=pltpu.CompilerParams(vmem_limit_bytes=8 * 1024 * 1024),
+        name="finish",
+        cost_estimate=pl.CostEstimate(flops=2_000_000, bytes_accessed=5_000_000, transcendentals=0),
+    )(own, left, right, *swaps)
 
 
 def partners(bit, size, inner):
     if 2 << bit == inner:
         flip = inner - 1
     elif 2 << bit == size:
-        flip = (size - 1) & ~(inner - 1)
+        flip = 3 * size // 4
     else:
         flip = 1 << bit
     return [(i, i ^ flip) for i in range(size)]
@@ -404,7 +425,7 @@
         if b == 4:
             acc = far(pos1, acc, qt, recvs[3], offs[3], cum, lw, 3, base)
         if b < bits - 1:
-            pay, off = merge(pos1, after, recv, pay, off, b)
+            pay, off = merge(pos1, after, recv, pay, off, b, b == bits - 2)
     n_near, n_side, n_own = norm(pick, acc, qt, recv, off, cum, lw, norm_gain, bits - 1, base, ring)
     from_near = lax.ppermute(n_near, "head", to_near)
     from_side = lax.ppermute(n_side, "head", to_side)

time: 75.3 us -> 75.1 us (level)
  waiting for transfers between devices: 16.8 us -> 15.7 us
  starting transfers between devices: 32.3 us -> 33.3 us
    pallas_call x18 -> x17, Pallas kernels: 18.3 us -> 16.9 us  [call(): pl.pallas_call(kernel, in_specs=ins, out_specs=[VM] * len(outs), out_shap...]
    pallas_call x0 -> x1, Pallas kernels: none -> 1.07 us  [finish(): pl.pallas_call(functools.partial(finish_kernel, parts=parts), in_specs=[V...]
    ppermute x5, waiting for transfers between devices: 4.64 us -> 3.85 us  [body(): recv = lax.ppermute(pay, 'seq', partners(b, seq_size, 4))]
where the time goes in v4:
time: 75.1 us; the launch traced here: 74.9 us
  starting transfers between devices  33.3 us (44%)
  Pallas kernels  18 us (24%)
  waiting for transfers between devices  15.7 us (21%)
  local copies, waits for them, and re-layouts  7.48 us (10%)
    pallas_call x17, Pallas kernels, call(): pl.pallas_call(kernel, in_specs=ins, out_specs=[VM] * len(outs), out_shap...  16.9 us
    ppermute x5, starting transfers between devices, body(): recv = lax.ppermute(pay, 'seq', partners(b, seq_size, 4))  13.6 us
    ppermute x1, waiting for transfers between devices, body(): far_l = lax.ppermute(both_l, 'head', to_side)  6.9 us
    ppermute x1, starting transfers between devices, body(): swap_l = lax.ppermute(send_l, 'head', swap)  6.59 us
    ppermute x5, waiting for transfers between devices, body(): recv = lax.ppermute(pay, 'seq', partners(b, seq_size, 4))  3.85 us
    slice x1, local copies, waits for them, and re-layouts, body(): weight[:direct, width // 2:]  2.69 us
    ppermute x1, waiting for transfers between devices, body(): from_near = lax.ppermute(n_near, 'head', to_near)  2.42 us
    ppermute x1, starting transfers between devices, body(): theirs_r = lax.ppermute(mine_r, 'seq', to_y[1])  2.35 us
  transfers between devices with their start and end apart: 20, of which 7 were waited for; matrix products, arithmetic and copies ran while one was open for 6% of the time, Pallas kernels for 21%

profile of v4, /device:TPU:1, one launch (start us, length us, event | category | flops | bytes accessed | tf_op | source)
XLA Modules:
  0.0 74.9 jit_solution(8367034261205594625)
XLA Ops:
  0.0 1.9 %copy_bitcast_fusion.3 = (bf16[1024,512]{1,0:T(8,128)(2,1)S(1)}, bf16[1024,512]{1,0:T(8,128)(2,1)S(1)}) fusion(bf16[128,8,4,128]{3,2,1,0:T(4,128)(2,1)} %bitcast.40, bf16[128,8,4,128]{3,2,1,0:T(4,128)(2,1)} %bitcast.38), kind=kLoop, calls=%fused_computation.3 | loop fusion | bytes 4194304 | tf_op jit(solution)/shard_map/reshape | solution.py:385
  1.9 1.2 %summary.1 = (bf16[528,128]{1,0:T(8,128)(2,1)S(1)}, f32[4,1024]{1,0:T(4,128)S(1)}) custom-call(f32[4,1024]{1,0:T(4,128)S(1)} %bitcast.37, bf16[1024,512]{1,0:T(8,128)(2,1)S(1)} %get-tuple-element.88.k_ref, bf16[1024,512]{1,0:T(8,128)(2,1)S(1)} %get-tuple-element.87.v_ref), custom_call_target="tpu_custom_call" | custom-call | flops 140000000 | bytes 2000000 | tf_op jit(solution)/shard_map/summary/pallas_call | solution.py:18
  3.1 2.2 %collective-permute-start = (bf16[528,128]{1,0:T(8,128)(2,1)S(1)}, bf16[528,128]{1,0:T(8,128)(2,1)S(1)}, u32[]{:S(2)}, u32[]{:S(2)}) collective-permute-start(bf16[528,128]{1,0:T(8,128)(2,1)S(1)} %get-tuple-element.45.self_ref), channel_id=1, source_target_pairs={{0,8},{8,0},{16,24},{24,16},{32,40},{40,32},{48,56},{56,48},{64,72... | collective-permute-start | bytes 405512 | tf_op jit(solution)/shard_map/ppermute | solution.py:398
  5.3 1.4 %constant_dynamic-slice_fusion = (bf16[160,2048]{1,0:T(8,128)(2,1)S(1)}, bf16[160,2048]{1,0:T(8,128)(2,1)S(1)}) fusion(bf16[512,4096]{1,0:T(8,128)(2,1)} %w_ref.3, s32[]{:T(128)S(6)} %select_n.49, s32[]{:T(128)S(6)} %select_n.48), kind=kLoop, calls=%fused_computation.5 | loop fusion | bytes 2621448 | tf_op jit(solution)/shard_map/dynamic_slice | solution.py:404
  6.8 0.0 copy-start.8
  6.8 1.3 %collective-permute-start.6 = (bf16[160,2048]{1,0:T(8,128)(2,1)S(1)}, bf16[160,2048]{1,0:T(8,128)(2,1)}, u32[]{:S(2)}, u32[]{:S(2)}) collective-permute-start(bf16[160,2048]{1,0:T(8,128)(2,1)S(1)} %get-tuple-element.84), channel_id=1, source_target_pairs={{0,2},{1,3},{2,0},{3,1},{4,6},{5,7},{6,4},{7,5},{8,10},{9,11},{10,... | collective-permute-start | bytes 1966088 | tf_op jit(solution)/shard_map/ppermute | solution.py:405
  8.1 1.8 %collective-permute-start.7 = (bf16[160,2048]{1,0:T(8,128)(2,1)S(1)}, bf16[160,2048]{1,0:T(8,128)(2,1)}, u32[]{:S(2)}, u32[]{:S(2)}) collective-permute-start(bf16[160,2048]{1,0:T(8,128)(2,1)S(1)} %get-tuple-element.83), channel_id=1, source_target_pairs={{0,6},{1,7},{2,4},{3,5},{4,2},{5,3},{6,0},{7,1},{8,14},{9,15},{10,... | collective-permute-start | bytes 1966088 | tf_op jit(solution)/shard_map/ppermute | solution.py:406
  9.9 0.0 collective-permute-done.recv_ref
  9.9 0.1 merge0.1
  10.0 0.0 copy-start.6
  10.0 2.0 %collective-permute-start.1 = (bf16[528,128]{1,0:T(8,128)(2,1)S(1)}, bf16[528,128]{1,0:T(8,128)(2,1)S(1)}, u32[]{:S(2)}, u32[]{:S(2)}) collective-permute-start(bf16[528,128]{1,0:T(8,128)(2,1)S(1)} %get-tuple-element.46.self_ref), channel_id=1, source_target_pairs={{0,24},{8,16},{16,8},{24,0},{32,56},{40,48},{48,40},{56,32},{64,88... | collective-permute-start | bytes 405512 | tf_op jit(solution)/shard_map/ppermute | solution.py:398
  12.0 2.7 %fusion = (bf16[192,2048]{1,0:T(8,128)(2,1)}, bf16[192,2048]{1,0:T(8,128)(2,1)}) fusion(bf16[512,4096]{1,0:T(8,128)(2,1)} %w_ref.3), kind=kLoop, calls=%fused_computation.7 | loop fusion | bytes 3145728 | tf_op jit(solution)/shard_map/slice | solution.py:409
  14.7 0.9 %collective-permute-done.1.recv_ref = bf16[528,128]{1,0:T(8,128)(2,1)S(1)} collective-permute-done((bf16[528,128]{1,0:T(8,128)(2,1)S(1)}, bf16[528,128]{1,0:T(8,128)(2,1)S(1)}, u32[]{:S(2)}, u32[]{:S(2)}) %collective-permute-start.1) | collective-permute-done | bytes 135200 | tf_op jit(solution)/shard_map/ppermute | solution.py:398
  15.5 0.0 collective-permute-start.5
  15.5 0.1 merge1.1
  15.6 1.7 %collective-permute-start.2 = (bf16[528,128]{1,0:T(8,128)(2,1)S(1)}, bf16[528,128]{1,0:T(8,128)(2,1)S(1)}, u32[]{:S(2)}, u32[]{:S(2)}) collective-permute-start(bf16[528,128]{1,0:T(8,128)(2,1)S(1)} %get-tuple-element.50.self_ref), channel_id=1, source_target_pairs={{0,32},{8,40},{16,48},{24,56},{32,0},{40,8},{48,16},{56,24},{64,96... | collective-permute-start | bytes 405512 | tf_op jit(solution)/shard_map/ppermute | solution.py:398
  17.3 0.2 copy.24
  17.6 0.0 copy-start.1
  17.6 0.2 copy.23
  17.8 0.8 %copy-done.7 = bf16[1024,4,128]{2,1,0:T(4,128)(2,1)S(1)} copy-done((bf16[1024,4,128]{2,1,0:T(4,128)(2,1)S(1)}, bf16[1024,4,128]{2,1,0:T(4,128)(2,1)}, u32[]{:S(2)}) %copy-start.7) | copy-done | bytes 1048600
  18.6 0.2 copy.22
  18.8 2.6 %local.1 = (f32[512,1024]{1,0:T(8,128)S(1)}, bf16[512,1024]{1,0:T(8,128)(2,1)S(1)}) custom-call(bf16[1024,512]{1,0:T(8,128)(2,1)S(1)} %bitcast.34, bf16[1024,512]{1,0:T(8,128)(2,1)S(1)} %bitcast.35, bf16[1024,512]{1,0:T(8,128)(2,1)S(1)} %bitcast.36, f32[4,1024]{1,0:T(4,128)S(1)} %get-tuple-element.44.after_ref.cum_ref, f32[10,4,1024]{2,1,0:T(4,128)S(1)} %bitcast.28), custom_call_target="tpu_custom_call" | custom-call | flops 1000000 | bytes 100000 | tf_op jit(solution)/shard_map/local/pallas_call | solution.py:18
  21.4 0.0 collective-permute-done.2.recv_ref
  21.4 0.1 merge2.1
  21.5 1.7 %collective-permute-start.9 = (bf16[192,2048]{1,0:T(8,128)(2,1)}, bf16[192,2048]{1,0:T(8,128)(2,1)}, u32[]{:S(2)}, u32[]{:S(2)}) collective-permute-start(bf16[192,2048]{1,0:T(8,128)(2,1)} %get-tuple-element.68), channel_id=1, source_target_pairs={{0,6},{1,7},{2,4},{3,5},{4,2},{5,3},{6,0},{7,1},{8,14},{9,15},{10,... | collective-permute-start | bytes 2359304 | tf_op jit(solution)/shard_map/ppermute | solution.py:418
  23.1 3.0 %collective-permute-start.3 = (bf16[528,128]{1,0:T(8,128)(2,1)S(1)}, bf16[528,128]{1,0:T(8,128)(2,1)S(1)}, u32[]{:S(2)}, u32[]{:S(2)}) collective-permute-start(bf16[528,128]{1,0:T(8,128)(2,1)S(1)} %get-tuple-element.57.self_ref), channel_id=1, source_target_pairs={{0,64},{8,72},{16,80},{24,88},{32,96},{40,104},{48,112},{56,120},{... | collective-permute-start | bytes 405512 | tf_op jit(solution)/shard_map/ppermute | solution.py:398
  26.1 0.0 collective-permute-done.6.refs_1_
  26.1 0.1 collective-permute-start.8
  26.2 2.3 %collective-permute-start.10 = (bf16[160,2048]{1,0:T(8,128)(2,1)}, bf16[160,2048]{1,0:T(8,128)(2,1)}, u32[]{:S(2)}, u32[]{:S(2)}) collective-permute-start(bf16[160,2048]{1,0:T(8,128)(2,1)} %collective-permute-done.7.refs_4_), channel_id=1, source_target_pairs={{0,24},{8,16},{16,8},{24,0},{32,56},{40,48},{48,40},{56,32},{64,88... | collective-permute-start | bytes 1966088 | tf_op jit(solution)/shard_map/ppermute | solution.py:421
  28.6 0.6 far0.1.acc_ref
  29.2 0.6 far1.1.acc_ref
  29.8 0.6 far2.1.acc_ref.after_ref
  30.4 0.7 merge3.1
  31.2 4.7 %collective-permute-start.4 = (bf16[512,128]{1,0:T(8,128)(2,1)}, bf16[512,128]{1,0:T(8,128)(2,1)}, u32[]{:S(2)}, u32[]{:S(2)}) collective-permute-start(bf16[512,128]{1,0:T(8,128)(2,1)} %get-tuple-element.59), channel_id=1, source_target_pairs={{0,192},{8,200},{16,208},{24,216},{32,224},{40,232},{48,240},{56,2... | collective-permute-start | bytes 393224 | tf_op jit(solution)/shard_map/ppermute | solution.py:398
  35.9 0.1 stack.36.pick_ref
  36.0 0.6 far3.1.acc_ref
  36.6 3.0 %collective-permute-done.4.recv_ref = bf16[512,128]{1,0:T(8,128)(2,1)} collective-permute-done((bf16[512,128]{1,0:T(8,128)(2,1)}, bf16[512,128]{1,0:T(8,128)(2,1)}, u32[]{:S(2)}, u32[]{:S(2)}) %collective-permute-start.4) | collective-permute-done | bytes 131104 | tf_op jit(solution)/shard_map/ppermute | solution.py:398
  39.6 2.1 %norm.1 = (bf16[512,512]{1,0:T(8,128)(2,1)S(1)}, bf16[512,512]{1,0:T(8,128)(2,1)S(1)}, bf16[256,512]{1,0:T(8,128)(2,1)S(1)}) custom-call(s32[9]{0:T(128)S(1)} %stack.36.pick_ref, f32[512,1024]{1,0:T(8,128)S(1)} %far3.1.acc_ref, bf16[512,1024]{1,0:T(8,128)(2,1)S(1)} %get-tuple-element.55.qt_ref, bf16[512,128]{1,0:T(8,128)(2,1)} %collective-permute-done.4.recv_ref, ...), custom_call_target="tpu_custom_call" | custom-call | flops 1000000 | bytes 100000 | tf_op jit(solution)/shard_map/norm/pallas_call | solution.py:18
  41.7 0.1 collective-permute-start.11
  41.8 0.0 collective-permute-done.5.refs_0_
  41.8 1.9 %collective-permute-start.13 = (bf16[512,512]{1,0:T(8,128)(2,1)S(1)}, bf16[512,512]{1,0:T(8,128)(2,1)S(1)}, u32[]{:S(2)}, u32[]{:S(2)}) collective-permute-start(bf16[512,512]{1,0:T(8,128)(2,1)S(1)} %get-tuple-element.63.side_ref), channel_id=1, source_target_pairs={{0,6},{1,7},{2,4},{3,5},{4,2},{5,3},{6,0},{7,1},{8,14},{9,15},{10,... | collective-permute-start | bytes 1572872 | tf_op jit(solution)/shard_map/ppermute | solution.py:431
  43.7 0.0 collective-permute-done.9.refs_3_
  43.7 3.7 %begin.1 = (bf16[256,2048]{1,0:T(8,128)(2,1)S(1)}, bf16[256,2048]{1,0:T(8,128)(2,1)S(1)}, bf16[512,2048]{1,0:T(8,128)(2,1)S(1)}, bf16[512,2048]{1,0:T(8,128)(2,1)S(1)}) custom-call(s32[9]{0:T(128)S(1)} %stack.36.pick_ref, bf16[512,512]{1,0:T(8,128)(2,1)S(1)} %get-tuple-element.62.near_ref, bf16[512,512]{1,0:T(8,128)(2,1)S(1)} %get-tuple-element.63.side_ref, ...), custom_call_target="tpu_custom_call" | custom-call | flops 1000000000 | bytes 6000000 | tf_op jit(solution)/shard_map/begin/pallas_call | solution.py:18
  47.4 2.4 %collective-permute-done.11.b_ref.b_left = bf16[512,512]{1,0:T(8,128)(2,1)S(1)} collective-permute-done((bf16[512,512]{1,0:T(8,128)(2,1)S(1)}, bf16[512,512]{1,0:T(8,128)(2,1)S(1)}, u32[]{:S(2)}, u32[]{:S(2)}) %collective-permute-start.11) | collective-permute-done | bytes 524320 | tf_op jit(solution)/shard_map/ppermute | solution.py:430
  49.8 0.7 left.1
  50.5 6.6 %collective-permute-start.12 = (bf16[128,2048]{1,0:T(8,128)(2,1)S(1)}, bf16[128,2048]{1,0:T(8,128)(2,1)S(1)}, u32[]{:S(2)}, u32[]{:S(2)}) collective-permute-start(bf16[128,2048]{1,0:T(8,128)(2,1)S(1)} %get-tuple-element.73), channel_id=1, source_target_pairs={{0,1},{1,0},{2,3},{3,2},{4,5},{5,4},{6,7},{7,6},{8,9},{9,8},{10,11... | collective-permute-start | bytes 1572872 | tf_op jit(solution)/shard_map/ppermute | solution.py:436
  57.1 0.0 collective-permute-done.13.b_ref.b_right
  57.1 0.7 right.1
  57.8 0.6 collective-permute-start.14
  58.4 0.2 collective-permute-done.12.b_ref
  58.7 0.1 join_left.1
  58.7 1.9 %collective-permute-start.15 = (bf16[128,2048]{1,0:T(8,128)(2,1)S(1)}, bf16[128,2048]{1,0:T(8,128)(2,1)S(1)}, u32[]{:S(2)}, u32[]{:S(2)}) collective-permute-start(bf16[128,2048]{1,0:T(8,128)(2,1)S(1)} %join_left.1), channel_id=1, source_target_pairs={{0,6},{1,7},{2,4},{3,5},{4,2},{5,3},{6,0},{7,1},{8,14},{9,15},{10,... | collective-permute-start | bytes 1572872 | tf_op jit(solution)/shard_map/ppermute | solution.py:441
  60.6 0.1 join_right.1
  60.7 0.1 collective-permute-start.16
  60.8 2.4 %own.1 = (f32[128,4096]{1,0:T(8,128)S(1)}, bf16[48,4096]{1,0:T(8,128)(2,1)S(1)}, bf16[48,4096]{1,0:T(8,128)(2,1)S(1)}, bf16[32,4096]{1,0:T(8,128)(2,1)S(1)}) custom-call(bf16[256,512]{1,0:T(8,128)(2,1)S(1)} %get-tuple-element.78.a_ref, bf16[512,4096]{1,0:T(8,128)(2,1)S(1)} %copy-done, bf16[512,512]{1,0:T(8,128)(2,1)S(1)} %collective-permute-done.11.b_ref.b_left, ...), custom_call_target="tpu_custom_call" | custom-call | flops 2000000000 | bytes 9000000 | tf_op jit(solution)/shard_map/own/pallas_call | solution.py:18
  63.2 0.7 collective-permute-start.17
  64.0 0.1 collective-permute-start.18
  64.1 0.4 collective-permute-start.19
  64.5 1.8 %collective-permute-done.19.refs_2_ = bf16[32,4096]{1,0:T(8,128)(2,1)S(1)} collective-permute-done((bf16[32,4096]{1,0:T(8,128)(2,1)S(1)}, bf16[32,4096]{1,0:T(8,128)(2,1)S(1)}, u32[]{:S(2)}, u32[]{:S(2)}) %collective-permute-start.19) | collective-permute-done | bytes 262176 | tf_op jit(solution)/shard_map/ppermute | solution.py:445
  66.3 0.0 collective-permute-done.17.refs_0_
  66.3 0.0 collective-permute-done.18.refs_1_
  66.3 6.9 %collective-permute-done.15.left_ref = bf16[128,2048]{1,0:T(8,128)(2,1)S(1)} collective-permute-done((bf16[128,2048]{1,0:T(8,128)(2,1)S(1)}, bf16[128,2048]{1,0:T(8,128)(2,1)S(1)}, u32[]{:S(2)}, u32[]{:S(2)}) %collective-permute-start.15) | collective-permute-done | bytes 524320 | tf_op jit(solution)/shard_map/ppermute | solution.py:441
  73.2 0.4 collective-permute-done.16.right_ref
  73.6 1.1 %finish.1 = bf16[128,4096]{1,0:T(8,128)(2,1)} custom-call(f32[128,4096]{1,0:T(8,128)S(1)} %get-tuple-element.79.own_ref, bf16[128,2048]{1,0:T(8,128)(2,1)S(1)} %collective-permute-done.15.left_ref, bf16[128,2048]{1,0:T(8,128)(2,1)S(1)} %collective-permute-done.16.right_ref, bf16[48,4096]{1,0:T(8,128)(2,1)S(1)} %collective-permute-done.17.refs_0_, ...), custom_call_target="tpu_custom_call" | custom-call | flops 2000000 | bytes 5000000 | tf_op jit(solution)/shard_map/finish/pallas_call | solution.py:344
  (20 shorter events, 0.0 us)
Async XLA Ops:
  0.0 1.9 %copy-start.4 = (f32[1024,4]{0,1:T(4,128)S(1)}, f32[1024,4]{0,1:T(4,128)}, u32[]{:S(2)}) copy-start(f32[1024,4]{0,1:T(4,128)} %param.10) | copy-start | bytes 49156
  3.1 6.8 %collective-permute-start = (bf16[528,128]{1,0:T(8,128)(2,1)S(1)}, bf16[528,128]{1,0:T(8,128)(2,1)S(1)}, u32[]{:S(2)}, u32[]{:S(2)}) collective-permute-start(bf16[528,128]{1,0:T(8,128)(2,1)S(1)} %get-tuple-element.45.self_ref), channel_id=1, source_target_pairs={{0,8},{8,0},{16,24},{24,16},{32,40},{40,32},{48,56},{56,48},{64,72... | collective-permute-start | bytes 405512 | tf_op jit(solution)/shard_map/ppermute | solution.py:398
  6.8 10.6 %copy-start.8 = (bf16[1024,4,128]{2,1,0:T(4,128)(2,1)S(1)}, bf16[1024,4,128]{2,1,0:T(4,128)(2,1)}, u32[]{:S(2)}) copy-start(bf16[1024,4,128]{2,1,0:T(4,128)(2,1)} %param.7) | copy-start | bytes 3145732
  6.8 19.3 %collective-permute-start.6 = (bf16[160,2048]{1,0:T(8,128)(2,1)S(1)}, bf16[160,2048]{1,0:T(8,128)(2,1)}, u32[]{:S(2)}, u32[]{:S(2)}) collective-permute-start(bf16[160,2048]{1,0:T(8,128)(2,1)S(1)} %get-tuple-element.84), channel_id=1, source_target_pairs={{0,2},{1,3},{2,0},{3,1},{4,6},{5,7},{6,4},{7,5},{8,10},{9,11},{10,... | collective-permute-start | bytes 1966088 | tf_op jit(solution)/shard_map/ppermute | solution.py:405
  8.1 18.0 %collective-permute-start.7 = (bf16[160,2048]{1,0:T(8,128)(2,1)S(1)}, bf16[160,2048]{1,0:T(8,128)(2,1)}, u32[]{:S(2)}, u32[]{:S(2)}) collective-permute-start(bf16[160,2048]{1,0:T(8,128)(2,1)S(1)} %get-tuple-element.83), channel_id=1, source_target_pairs={{0,6},{1,7},{2,4},{3,5},{4,2},{5,3},{6,0},{7,1},{8,14},{9,15},{10,... | collective-permute-start | bytes 1966088 | tf_op jit(solution)/shard_map/ppermute | solution.py:406
  9.9 7.6 %copy-start.2 = (bf16[528,128]{1,0:T(8,128)(2,1)}, bf16[528,128]{1,0:T(8,128)(2,1)S(1)}, u32[]{:S(2)}) copy-start(bf16[528,128]{1,0:T(8,128)(2,1)S(1)} %collective-permute-done.recv_ref) | copy-start | bytes 405508
  10.0 7.6 %copy-start.6 = (bf16[1024,4,128]{2,1,0:T(4,128)(2,1)S(1)}, bf16[1024,4,128]{2,1,0:T(4,128)(2,1)}, u32[]{:S(2)}) copy-start(bf16[1024,4,128]{2,1,0:T(4,128)(2,1)} %param.8) | copy-start | bytes 3145732
  10.0 5.6 %collective-permute-start.1 = (bf16[528,128]{1,0:T(8,128)(2,1)S(1)}, bf16[528,128]{1,0:T(8,128)(2,1)S(1)}, u32[]{:S(2)}, u32[]{:S(2)}) collective-permute-start(bf16[528,128]{1,0:T(8,128)(2,1)S(1)} %get-tuple-element.46.self_ref), channel_id=1, source_target_pairs={{0,24},{8,16},{16,8},{24,0},{32,56},{40,48},{48,40},{56,32},{64,88... | collective-permute-start | bytes 405512 | tf_op jit(solution)/shard_map/ppermute | solution.py:398
  15.5 26.2 %collective-permute-start.5 = (bf16[192,2048]{1,0:T(8,128)(2,1)}, bf16[192,2048]{1,0:T(8,128)(2,1)}, u32[]{:S(2)}, u32[]{:S(2)}) collective-permute-start(bf16[192,2048]{1,0:T(8,128)(2,1)} %get-tuple-element.64), channel_id=1, source_target_pairs={{0,2},{1,3},{2,0},{3,1},{4,6},{5,7},{6,4},{7,5},{8,10},{9,11},{10,... | collective-permute-start | bytes 2359304 | tf_op jit(solution)/shard_map/ppermute | solution.py:411
  15.6 5.8 %collective-permute-start.2 = (bf16[528,128]{1,0:T(8,128)(2,1)S(1)}, bf16[528,128]{1,0:T(8,128)(2,1)S(1)}, u32[]{:S(2)}, u32[]{:S(2)}) collective-permute-start(bf16[528,128]{1,0:T(8,128)(2,1)S(1)} %get-tuple-element.50.self_ref), channel_id=1, source_target_pairs={{0,32},{8,40},{16,48},{24,56},{32,0},{40,8},{48,16},{56,24},{64,96... | collective-permute-start | bytes 405512 | tf_op jit(solution)/shard_map/ppermute | solution.py:398
  17.3 1.2 %copy-start.7 = (bf16[1024,4,128]{2,1,0:T(4,128)(2,1)S(1)}, bf16[1024,4,128]{2,1,0:T(4,128)(2,1)}, u32[]{:S(2)}) copy-start(bf16[1024,4,128]{2,1,0:T(4,128)(2,1)} %param.9) | copy-start | bytes 3145732
  17.6 1.2 %copy-start.1 = (f32[1024,4,10]{0,1,2:T(4,128)S(1)}, f32[1024,4,10]{0,1,2:T(4,128)}, u32[]{:S(2)}) copy-start(f32[1024,4,10]{0,1,2:T(4,128)} %param.11) | copy-start | bytes 491524
  18.8 9.8 %copy-start.3 = (bf16[528,128]{1,0:T(8,128)(2,1)S(1)}, bf16[528,128]{1,0:T(8,128)(2,1)}, u32[]{:S(2)}) copy-start(bf16[528,128]{1,0:T(8,128)(2,1)} %copy-done.2) | copy-start | bytes 405508
  21.5 22.2 %collective-permute-start.9 = (bf16[192,2048]{1,0:T(8,128)(2,1)}, bf16[192,2048]{1,0:T(8,128)(2,1)}, u32[]{:S(2)}, u32[]{:S(2)}) collective-permute-start(bf16[192,2048]{1,0:T(8,128)(2,1)} %get-tuple-element.68), channel_id=1, source_target_pairs={{0,6},{1,7},{2,4},{3,5},{4,2},{5,3},{6,0},{7,1},{8,14},{9,15},{10,... | collective-permute-start | bytes 2359304 | tf_op jit(solution)/shard_map/ppermute | solution.py:418
  23.1 7.3 %collective-permute-start.3 = (bf16[528,128]{1,0:T(8,128)(2,1)S(1)}, bf16[528,128]{1,0:T(8,128)(2,1)S(1)}, u32[]{:S(2)}, u32[]{:S(2)}) collective-permute-start(bf16[528,128]{1,0:T(8,128)(2,1)S(1)} %get-tuple-element.57.self_ref), channel_id=1, source_target_pairs={{0,64},{8,72},{16,80},{24,88},{32,96},{40,104},{48,112},{56,120},{... | collective-permute-start | bytes 405512 | tf_op jit(solution)/shard_map/ppermute | solution.py:398
  26.1 17.6 %collective-permute-start.8 = (bf16[160,2048]{1,0:T(8,128)(2,1)}, bf16[160,2048]{1,0:T(8,128)(2,1)}, u32[]{:S(2)}, u32[]{:S(2)}) collective-permute-start(bf16[160,2048]{1,0:T(8,128)(2,1)} %collective-permute-done.6.refs_1_), channel_id=1, source_target_pairs={{0,8},{8,0},{16,24},{24,16},{32,40},{40,32},{48,56},{56,48},{64,72... | collective-permute-start | bytes 1966088 | tf_op jit(solution)/shard_map/ppermute | solution.py:420
  26.2 17.4 %collective-permute-start.10 = (bf16[160,2048]{1,0:T(8,128)(2,1)}, bf16[160,2048]{1,0:T(8,128)(2,1)}, u32[]{:S(2)}, u32[]{:S(2)}) collective-permute-start(bf16[160,2048]{1,0:T(8,128)(2,1)} %collective-permute-done.7.refs_4_), channel_id=1, source_target_pairs={{0,24},{8,16},{16,8},{24,0},{32,56},{40,48},{48,40},{56,32},{64,88... | collective-permute-start | bytes 1966088 | tf_op jit(solution)/shard_map/ppermute | solution.py:421
  31.2 8.4 %collective-permute-start.4 = (bf16[512,128]{1,0:T(8,128)(2,1)}, bf16[512,128]{1,0:T(8,128)(2,1)}, u32[]{:S(2)}, u32[]{:S(2)}) collective-permute-start(bf16[512,128]{1,0:T(8,128)(2,1)} %get-tuple-element.59), channel_id=1, source_target_pairs={{0,192},{8,200},{16,208},{24,216},{32,224},{40,232},{48,240},{56,2... | collective-permute-start | bytes 393224 | tf_op jit(solution)/shard_map/ppermute | solution.py:398
  36.0 3.6 %copy-start.5 = (f32[4,128]{1,0:T(4,128)S(1)}, f32[4,128]{1,0:T(4,128)}, u32[]{:S(2)}) copy-start(f32[4,128]{1,0:T(4,128)} %gain_ref.1) | copy-start | bytes 6148
  36.0 7.7 %copy-start = (bf16[512,4096]{1,0:T(8,128)(2,1)S(1)}, bf16[512,4096]{1,0:T(8,128)(2,1)}, u32[]{:S(2)}) copy-start(bf16[512,4096]{1,0:T(8,128)(2,1)} %w_ref.3) | copy-start | bytes 12582916
  41.7 8.1 %collective-permute-start.11 = (bf16[512,512]{1,0:T(8,128)(2,1)S(1)}, bf16[512,512]{1,0:T(8,128)(2,1)S(1)}, u32[]{:S(2)}, u32[]{:S(2)}) collective-permute-start(bf16[512,512]{1,0:T(8,128)(2,1)S(1)} %get-tuple-element.62.near_ref), channel_id=1, source_target_pairs={{0,2},{1,3},{2,0},{3,1},{4,6},{5,7},{6,4},{7,5},{8,10},{9,11},{10,... | collective-permute-start | bytes 1572872 | tf_op jit(solution)/shard_map/ppermute | solution.py:430
  41.8 15.3 %collective-permute-start.13 = (bf16[512,512]{1,0:T(8,128)(2,1)S(1)}, bf16[512,512]{1,0:T(8,128)(2,1)S(1)}, u32[]{:S(2)}, u32[]{:S(2)}) collective-permute-start(bf16[512,512]{1,0:T(8,128)(2,1)S(1)} %get-tuple-element.63.side_ref), channel_id=1, source_target_pairs={{0,6},{1,7},{2,4},{3,5},{4,2},{5,3},{6,0},{7,1},{8,14},{9,15},{10,... | collective-permute-start | bytes 1572872 | tf_op jit(solution)/shard_map/ppermute | solution.py:431
  50.5 8.1 %collective-permute-start.12 = (bf16[128,2048]{1,0:T(8,128)(2,1)S(1)}, bf16[128,2048]{1,0:T(8,128)(2,1)S(1)}, u32[]{:S(2)}, u32[]{:S(2)}) collective-permute-start(bf16[128,2048]{1,0:T(8,128)(2,1)S(1)} %get-tuple-element.73), channel_id=1, source_target_pairs={{0,1},{1,0},{2,3},{3,2},{4,5},{5,4},{6,7},{7,6},{8,9},{9,8},{10,11... | collective-permute-start | bytes 1572872 | tf_op jit(solution)/shard_map/ppermute | solution.py:436
  57.8 2.8 %collective-permute-start.14 = (bf16[128,2048]{1,0:T(8,128)(2,1)S(1)}, bf16[128,2048]{1,0:T(8,128)(2,1)S(1)}, u32[]{:S(2)}, u32[]{:S(2)}) collective-permute-start(bf16[128,2048]{1,0:T(8,128)(2,1)S(1)} %get-tuple-element.77), channel_id=1, source_target_pairs={{0,1},{1,0},{2,3},{3,2},{4,5},{5,4},{6,7},{7,6},{8,9},{9,8},{10,11... | collective-permute-start | bytes 1572872 | tf_op jit(solution)/shard_map/ppermute | solution.py:438
  58.7 14.4 %collective-permute-start.15 = (bf16[128,2048]{1,0:T(8,128)(2,1)S(1)}, bf16[128,2048]{1,0:T(8,128)(2,1)S(1)}, u32[]{:S(2)}, u32[]{:S(2)}) collective-permute-start(bf16[128,2048]{1,0:T(8,128)(2,1)S(1)} %join_left.1), channel_id=1, source_target_pairs={{0,6},{1,7},{2,4},{3,5},{4,2},{5,3},{6,0},{7,1},{8,14},{9,15},{10,... | collective-permute-start | bytes 1572872 | tf_op jit(solution)/shard_map/ppermute | solution.py:441
  60.7 12.9 %collective-permute-start.16 = (bf16[128,2048]{1,0:T(8,128)(2,1)S(1)}, bf16[128,2048]{1,0:T(8,128)(2,1)S(1)}, u32[]{:S(2)}, u32[]{:S(2)}) collective-permute-start(bf16[128,2048]{1,0:T(8,128)(2,1)S(1)} %join_right.1), channel_id=1, source_target_pairs={{0,2},{1,3},{2,0},{3,1},{4,6},{5,7},{6,4},{7,5},{8,10},{9,11},{10,... | collective-permute-start | bytes 1572872 | tf_op jit(solution)/shard_map/ppermute | solution.py:442
  63.2 3.0 %collective-permute-start.17 = (bf16[48,4096]{1,0:T(8,128)(2,1)S(1)}, bf16[48,4096]{1,0:T(8,128)(2,1)S(1)}, u32[]{:S(2)}, u32[]{:S(2)}) collective-permute-start(bf16[48,4096]{1,0:T(8,128)(2,1)S(1)} %get-tuple-element.80), channel_id=1, source_target_pairs={{0,1},{1,0},{2,3},{3,2},{4,5},{5,4},{6,7},{7,6},{8,9},{9,8},{10,11... | collective-permute-start | bytes 1179656 | tf_op jit(solution)/shard_map/ppermute | solution.py:445
  64.0 2.3 %collective-permute-start.18 = (bf16[48,4096]{1,0:T(8,128)(2,1)S(1)}, bf16[48,4096]{1,0:T(8,128)(2,1)S(1)}, u32[]{:S(2)}, u32[]{:S(2)}) collective-permute-start(bf16[48,4096]{1,0:T(8,128)(2,1)S(1)} %get-tuple-element.81), channel_id=1, source_target_pairs={{0,1},{1,0},{2,3},{3,2},{4,5},{5,4},{6,7},{7,6},{8,9},{9,8},{10,11... | collective-permute-start | bytes 1179656 | tf_op jit(solution)/shard_map/ppermute | solution.py:445
  64.1 2.2 %collective-permute-start.19 = (bf16[32,4096]{1,0:T(8,128)(2,1)S(1)}, bf16[32,4096]{1,0:T(8,128)(2,1)S(1)}, u32[]{:S(2)}, u32[]{:S(2)}) collective-permute-start(bf16[32,4096]{1,0:T(8,128)(2,1)S(1)} %get-tuple-element.82), channel_id=1, source_target_pairs={{0,1},{1,0},{2,3},{3,2},{4,5},{5,4},{6,7},{7,6},{8,9},{9,8},{10,11... | collective-permute-start | bytes 786440 | tf_op jit(solution)/shard_map/ppermute | solution.py:445

commit v5 on v4

--- a/solution.py
+++ b/solution.py
@@ -224,38 +224,54 @@
         [SM] + [VM] * 7,
         [((2 * size, heads * HD), BF)] * 2 + [((size, heads * HD), BF)],
         (pick, acc, qt, recv, off, cum, lw, gain),
+        flops=1000000000,
+        moved=100_000,
+        vmem=10,
+    )
+
+
+def begin_kernel(near_ref, side_ref, w_ref, out_l, out_r, *, tile):
+    rows, half = out_l.shape
+    for side, (a_ref, out_ref) in enumerate(((side_ref, out_l), (near_ref, out_r))):
+        for j in range(half // tile):
+            own = slice(side * half + j * tile, side * half + (j + 1) * tile)
+            out_ref[:, j * tile : (j + 1) * tile] = dot(a_ref[rows:, :], w_ref[:, own]).astype(BF)
+
+
+def begin(near, side, w, tile=512):
+    return call(
+        functools.partial(begin_kernel, tile=tile),
+        "begin",
+        [VM] * 3,
+        [((near.shape[0] // 2, w.shape[1] // 2), BF)] * 2,
+        (near, side, w),
         flops=1_000_000,
         moved=100_000,
-        vmem=10,
-    )
-
-
-def begin_kernel(pick_ref, near_ref, side_ref, w_ref, *refs, tile):
-    pieces, (out_l, out_r, full_l, full_r) = refs[:6], refs[6:]
-    rows, half = out_l.shape
-    for side, (a_ref, out_ref, full_ref) in enumerate(((side_ref, out_l, full_l), (near_ref, out_r, full_r))):
-        whole_ref, mine_ref, theirs_ref = pieces[3 * side : 3 * side + 3]
+        vmem=16,
+    )
+
+
+def gather_kernel(pick_ref, *refs):
+    for side, full_ref in enumerate(refs[6:]):
+        whole_ref, mine_ref, theirs_ref = refs[3 * side : 3 * side + 3]
         depth, share = whole_ref.shape[0], mine_ref.shape[0]
         first = pick_ref[7 + side]
         full_ref[:depth, :] = whole_ref[...]
-        full_ref[pl.ds(pl.multiple_of(depth + first * share, 32), share), :] = mine_ref[...]
-        full_ref[pl.ds(pl.multiple_of(depth + (1 - first) * share, 32), share), :] = theirs_ref[...]
-        for j in range(half // tile):
-            own = slice(side * half + j * tile, side * half + (j + 1) * tile)
-            out_ref[:, j * tile : (j + 1) * tile] = dot(a_ref[rows:, :], w_ref[:, own]).astype(BF)
-
-
-def begin(pick, near, side, w, left, right, tile=512):
-    half = w.shape[1] // 2
-    return call(
-        functools.partial(begin_kernel, tile=tile),
-        "begin",
-        [SM] + [VM] * 9,
-        [((near.shape[0] // 2, half), BF)] * 2 + [((w.shape[0], half), BF)] * 2,
-        (pick, near, side, w, *left, *right),
-        flops=1_000_000_000,
-        moved=6_000_000,
-        vmem=20,
+        full_ref[pl.ds(pl.multiple_of(depth + first * share, 16), share), :] = mine_ref[...]
+        full_ref[pl.ds(pl.multiple_of(depth + (1 - first) * share, 16), share), :] = theirs_ref[...]
+
+
+def gather(pick, left, right):
+    depth = left[0].shape[0] + 2 * left[1].shape[0]
+    return call(
+        gather_kernel,
+        "gather",
+        [SM] + [VM] * 6,
+        [((depth, left[0].shape[1]), BF)] * 2,
+        (pick, *left, *right),
+        flops=1_000_000,
+        moved=100_000,
+        vmem=16,
     )
 
 
@@ -416,22 +432,21 @@
         if b == 3:
             slice_r, _ = lax.optimization_barrier((slice_r, pay))
             whole_r = lax.ppermute(slice_r, "head", to_side)
-            mine_l, mine_r, _ = lax.optimization_barrier((mine_l, mine_r, pay))
-            theirs_l = lax.ppermute(mine_l, "seq", to_y[0])
-            theirs_r = lax.ppermute(mine_r, "seq", to_y[1])
             for i in (0, 1, 2):
                 acc = far(pos1, acc, qt, recvs[i], offs[i], cum, lw, i, base)
             after = acc
         if b == 4:
+            mine_l, mine_r, _ = lax.optimization_barrier((mine_l, mine_r, pay))
+            theirs_l = lax.ppermute(mine_l, "seq", to_y[0])
+            theirs_r = lax.ppermute(mine_r, "seq", to_y[1])
             acc = far(pos1, acc, qt, recvs[3], offs[3], cum, lw, 3, base)
         if b < bits - 1:
             pay, off = merge(pos1, after, recv, pay, off, b, b == bits - 2)
     n_near, n_side, n_own = norm(pick, acc, qt, recv, off, cum, lw, norm_gain, bits - 1, base, ring)
     from_near = lax.ppermute(n_near, "head", to_near)
     from_side = lax.ppermute(n_side, "head", to_side)
-    begun_l, begun_r, w_l, w_r = begin(
-        pick, n_near, n_side, out_weight, (whole_l, mine_l, theirs_l), (whole_r, mine_r, theirs_r)
-    )
+    begun_l, begun_r = begin(n_near, n_side, out_weight)
+    w_l, w_r = gather(pick, (whole_l, mine_l, theirs_l), (whole_r, mine_r, theirs_r))
     keep_l, send_l = pass_on(begun_l, from_near, w_l, "left")
     swap_l = lax.ppermute(send_l, "head", swap)
     keep_r, send_r = pass_on(begun_r, from_side, w_r, "right")

time: 75.1 us -> 74.8 us (level)
  starting transfers between devices: 33.3 us -> 28.2 us
  waiting for transfers between devices: 15.7 us -> 20.5 us
    ppermute x1, starting transfers between devices: 6.59 us -> 4.09 us  [body(): swap_l = lax.ppermute(send_l, 'head', swap)]
    ppermute x1, waiting for transfers between devices: 0.01 us -> 2.02 us  [body(): theirs_l = lax.ppermute(mine_l, 'seq', to_y[0])]
    ppermute x1, waiting for transfers between devices: 0.01 us -> 2.01 us  [body(): whole_l = lax.ppermute(slice_l, 'head', to_near)]
    ppermute x1, starting transfers between devices: 1.89 us -> 0.06 us  [body(): from_side = lax.ppermute(n_side, 'head', to_side)]
    ppermute x1, starting transfers between devices: 0.57 us -> 2.33 us  [body(): swap_r = lax.ppermute(send_r, 'head', swap)]
    ppermute x1, waiting for transfers between devices: 0.01 us -> 1.49 us  [body(): theirs_r = lax.ppermute(mine_r, 'seq', to_y[1])]
    ppermute x5, starting transfers between devices: 13.6 us -> 12.2 us  [body(): recv = lax.ppermute(pay, 'seq', partners(b, seq_size, 4))]
    ppermute x1, starting transfers between devices: 1.3 us -> 0.01 us  [body(): mine_l = lax.ppermute(mine_l, 'head', to_near)]
  transfers between devices with their start and end apart: 20 -> 20, of which waited for: 7 -> 10; matrix products, arithmetic and copies ran while one was open for 6% -> 6% of each run, Pallas kernels for 21% -> 21%
where the time goes in v5:
time: 74.8 us; the launch traced here: 74.6 us
  starting transfers between devices  28.2 us (38%)
  waiting for transfers between devices  20.5 us (27%)
  Pallas kernels  18 us (24%)
  local copies, waits for them, and re-layouts  7.48 us (10%)
    pallas_call x18, Pallas kernels, call(): pl.pallas_call(kernel, in_specs=ins, out_specs=[VM] * len(outs), out_shap...  17 us
    ppermute x5, starting transfers between devices, body(): recv = lax.ppermute(pay, 'seq', partners(b, seq_size, 4))  12.2 us
    ppermute x1, waiting for transfers between devices, body(): far_l = lax.ppermute(both_l, 'head', to_side)  8.03 us
    ppermute x1, starting transfers between devices, body(): swap_l = lax.ppermute(send_l, 'head', swap)  4.09 us
    ppermute x5, waiting for transfers between devices, body(): recv = lax.ppermute(pay, 'seq', partners(b, seq_size, 4))  2.86 us
    slice x1, local copies, waits for them, and re-layouts, body(): weight[:direct, width // 2:]  2.69 us
    ppermute x1, starting transfers between devices, body(): mine_r = lax.ppermute(mine_r, 'head', to_side)  2.57 us
    ppermute x1, starting transfers between devices, body(): swap_r = lax.ppermute(send_r, 'head', swap)  2.33 us
  transfers between devices with their start and end apart: 20, of which 10 were waited for; matrix products, arithmetic and copies ran while one was open for 6% of the time, Pallas kernels for 21%

profile of v5, /device:TPU:1, one launch (start us, length us, event | category | flops | bytes accessed | tf_op | source)
XLA Modules:
  0.0 74.6 jit_solution(8749325982204785742)
XLA Ops:
  0.0 1.9 %copy_bitcast_fusion.3 = (bf16[1024,512]{1,0:T(8,128)(2,1)S(1)}, bf16[1024,512]{1,0:T(8,128)(2,1)S(1)}) fusion(bf16[128,8,4,128]{3,2,1,0:T(4,128)(2,1)} %bitcast.40, bf16[128,8,4,128]{3,2,1,0:T(4,128)(2,1)} %bitcast.38), kind=kLoop, calls=%fused_computation.3 | loop fusion | bytes 4194304 | tf_op jit(solution)/shard_map/reshape | solution.py:401
  1.9 1.2 %summary.1 = (bf16[528,128]{1,0:T(8,128)(2,1)S(1)}, f32[4,1024]{1,0:T(4,128)S(1)}) custom-call(f32[4,1024]{1,0:T(4,128)S(1)} %bitcast.37, bf16[1024,512]{1,0:T(8,128)(2,1)S(1)} %get-tuple-element.88.k_ref, bf16[1024,512]{1,0:T(8,128)(2,1)S(1)} %get-tuple-element.87.v_ref), custom_call_target="tpu_custom_call" | custom-call | flops 140000000 | bytes 2000000 | tf_op jit(solution)/shard_map/summary/pallas_call | solution.py:18
  3.1 2.2 %collective-permute-start = (bf16[528,128]{1,0:T(8,128)(2,1)S(1)}, bf16[528,128]{1,0:T(8,128)(2,1)S(1)}, u32[]{:S(2)}, u32[]{:S(2)}) collective-permute-start(bf16[528,128]{1,0:T(8,128)(2,1)S(1)} %get-tuple-element.45.self_ref), channel_id=1, source_target_pairs={{0,8},{8,0},{16,24},{24,16},{32,40},{40,32},{48,56},{56,48},{64,72... | collective-permute-start | bytes 405512 | tf_op jit(solution)/shard_map/ppermute | solution.py:414
  5.3 1.4 %constant_dynamic-slice_fusion = (bf16[160,2048]{1,0:T(8,128)(2,1)S(1)}, bf16[160,2048]{1,0:T(8,128)(2,1)S(1)}) fusion(bf16[512,4096]{1,0:T(8,128)(2,1)} %w_ref.3, s32[]{:T(128)S(6)} %select_n.49, s32[]{:T(128)S(6)} %select_n.48), kind=kLoop, calls=%fused_computation.5 | loop fusion | bytes 2621448 | tf_op jit(solution)/shard_map/dynamic_slice | solution.py:420
  6.8 0.0 copy-start.6
  6.8 2.6 %collective-permute-start.8 = (bf16[160,2048]{1,0:T(8,128)(2,1)S(1)}, bf16[160,2048]{1,0:T(8,128)(2,1)}, u32[]{:S(2)}, u32[]{:S(2)}) collective-permute-start(bf16[160,2048]{1,0:T(8,128)(2,1)S(1)} %get-tuple-element.83), channel_id=1, source_target_pairs={{0,6},{1,7},{2,4},{3,5},{4,2},{5,3},{6,0},{7,1},{8,14},{9,15},{10,... | collective-permute-start | bytes 1966088 | tf_op jit(solution)/shard_map/ppermute | solution.py:422
  9.3 0.0 collective-permute-start.7
  9.3 0.0 collective-permute-done.recv_ref
  9.4 0.1 merge0.1
  9.4 0.0 copy-start.8
  9.5 2.0 %collective-permute-start.1 = (bf16[528,128]{1,0:T(8,128)(2,1)S(1)}, bf16[528,128]{1,0:T(8,128)(2,1)S(1)}, u32[]{:S(2)}, u32[]{:S(2)}) collective-permute-start(bf16[528,128]{1,0:T(8,128)(2,1)S(1)} %get-tuple-element.46.self_ref), channel_id=1, source_target_pairs={{0,24},{8,16},{16,8},{24,0},{32,56},{40,48},{48,40},{56,32},{64,88... | collective-permute-start | bytes 405512 | tf_op jit(solution)/shard_map/ppermute | solution.py:414
  11.4 2.7 %fusion = (bf16[192,2048]{1,0:T(8,128)(2,1)}, bf16[192,2048]{1,0:T(8,128)(2,1)}) fusion(bf16[512,4096]{1,0:T(8,128)(2,1)} %w_ref.3), kind=kLoop, calls=%fused_computation.7 | loop fusion | bytes 3145728 | tf_op jit(solution)/shard_map/slice | solution.py:425
  14.1 0.9 %collective-permute-done.1.recv_ref = bf16[528,128]{1,0:T(8,128)(2,1)S(1)} collective-permute-done((bf16[528,128]{1,0:T(8,128)(2,1)S(1)}, bf16[528,128]{1,0:T(8,128)(2,1)S(1)}, u32[]{:S(2)}, u32[]{:S(2)}) %collective-permute-start.1) | collective-permute-done | bytes 135200 | tf_op jit(solution)/shard_map/ppermute | solution.py:414
  15.0 1.0 %collective-permute-start.6 = (bf16[192,2048]{1,0:T(8,128)(2,1)}, bf16[192,2048]{1,0:T(8,128)(2,1)}, u32[]{:S(2)}, u32[]{:S(2)}) collective-permute-start(bf16[192,2048]{1,0:T(8,128)(2,1)} %get-tuple-element.65), channel_id=1, source_target_pairs={{0,2},{1,3},{2,0},{3,1},{4,6},{5,7},{6,4},{7,5},{8,10},{9,11},{10,... | collective-permute-start | bytes 2359304 | tf_op jit(solution)/shard_map/ppermute | solution.py:427
  16.1 0.1 merge1.1
  16.1 1.7 %collective-permute-start.2 = (bf16[528,128]{1,0:T(8,128)(2,1)S(1)}, bf16[528,128]{1,0:T(8,128)(2,1)S(1)}, u32[]{:S(2)}, u32[]{:S(2)}) collective-permute-start(bf16[528,128]{1,0:T(8,128)(2,1)S(1)} %get-tuple-element.50.self_ref), channel_id=1, source_target_pairs={{0,32},{8,40},{16,48},{24,56},{32,0},{40,8},{48,16},{56,24},{64,96... | collective-permute-start | bytes 405512 | tf_op jit(solution)/shard_map/ppermute | solution.py:414
  17.9 0.2 copy.23
  18.1 0.0 copy-start.1
  18.1 0.2 copy.24
  18.3 0.8 %copy-done.7 = bf16[1024,4,128]{2,1,0:T(4,128)(2,1)S(1)} copy-done((bf16[1024,4,128]{2,1,0:T(4,128)(2,1)S(1)}, bf16[1024,4,128]{2,1,0:T(4,128)(2,1)}, u32[]{:S(2)}) %copy-start.7) | copy-done | bytes 1048600
  19.1 0.2 copy.22
  19.3 2.6 %local.1 = (f32[512,1024]{1,0:T(8,128)S(1)}, bf16[512,1024]{1,0:T(8,128)(2,1)S(1)}) custom-call(bf16[1024,512]{1,0:T(8,128)(2,1)S(1)} %bitcast.29, bf16[1024,512]{1,0:T(8,128)(2,1)S(1)} %bitcast.28, bf16[1024,512]{1,0:T(8,128)(2,1)S(1)} %bitcast.30, f32[4,1024]{1,0:T(4,128)S(1)} %get-tuple-element.44.after_ref.cum_ref, f32[10,4,1024]{2,1,0:T(4,128)S(1)} %bitcast.31), custom_call_target="tpu_custom_call" | custom-call | flops 1000000 | bytes 100000 | tf_op jit(solution)/shard_map/local/pallas_call | solution.py:18
  21.9 0.0 collective-permute-done.2.recv_ref
  21.9 0.1 merge2.1
  22.0 3.1 %collective-permute-start.3 = (bf16[528,128]{1,0:T(8,128)(2,1)S(1)}, bf16[528,128]{1,0:T(8,128)(2,1)S(1)}, u32[]{:S(2)}, u32[]{:S(2)}) collective-permute-start(bf16[528,128]{1,0:T(8,128)(2,1)S(1)} %get-tuple-element.57.self_ref), channel_id=1, source_target_pairs={{0,64},{8,72},{16,80},{24,88},{32,96},{40,104},{48,112},{56,120},{... | collective-permute-start | bytes 405512 | tf_op jit(solution)/shard_map/ppermute | solution.py:414
  25.0 1.1 %collective-permute-start.10 = (bf16[192,2048]{1,0:T(8,128)(2,1)}, bf16[192,2048]{1,0:T(8,128)(2,1)}, u32[]{:S(2)}, u32[]{:S(2)}) collective-permute-start(bf16[192,2048]{1,0:T(8,128)(2,1)} %get-tuple-element.69), channel_id=1, source_target_pairs={{0,6},{1,7},{2,4},{3,5},{4,2},{5,3},{6,0},{7,1},{8,14},{9,15},{10,... | collective-permute-start | bytes 2359304 | tf_op jit(solution)/shard_map/ppermute | solution.py:434
  26.1 0.6 far0.1.acc_ref
  26.7 0.6 far1.1.acc_ref
  27.4 0.6 far2.1.acc_ref.after_ref
  28.0 0.9 %collective-permute-done.3.recv_ref = bf16[528,128]{1,0:T(8,128)(2,1)S(1)} collective-permute-done((bf16[528,128]{1,0:T(8,128)(2,1)S(1)}, bf16[528,128]{1,0:T(8,128)(2,1)S(1)}, u32[]{:S(2)}, u32[]{:S(2)}) %collective-permute-start.3) | collective-permute-done | bytes 135200 | tf_op jit(solution)/shard_map/ppermute | solution.py:414
  28.9 0.7 merge3.1
  29.6 3.2 %collective-permute-start.4 = (bf16[512,128]{1,0:T(8,128)(2,1)}, bf16[512,128]{1,0:T(8,128)(2,1)}, u32[]{:S(2)}, u32[]{:S(2)}) collective-permute-start(bf16[512,128]{1,0:T(8,128)(2,1)} %get-tuple-element.59), channel_id=1, source_target_pairs={{0,192},{8,200},{16,208},{24,216},{32,224},{40,232},{48,240},{56,2... | collective-permute-start | bytes 393224 | tf_op jit(solution)/shard_map/ppermute | solution.py:414
  32.8 0.0 collective-permute-done.8.refs_4_
  32.8 0.0 collective-permute-done.7.refs_1_
  32.8 0.0 collective-permute-start.9
  32.8 2.1 %collective-permute-start.11 = (bf16[160,2048]{1,0:T(8,128)(2,1)}, bf16[160,2048]{1,0:T(8,128)(2,1)}, u32[]{:S(2)}, u32[]{:S(2)}) collective-permute-start(bf16[160,2048]{1,0:T(8,128)(2,1)} %collective-permute-done.8.refs_4_), channel_id=1, source_target_pairs={{0,24},{8,16},{16,8},{24,0},{32,56},{40,48},{48,40},{56,32},{64,88... | collective-permute-start | bytes 1966088 | tf_op jit(solution)/shard_map/ppermute | solution.py:441
  34.9 0.1 stack.36.pick_ref
  35.0 0.6 far3.1.acc_ref
  35.6 1.1 %collective-permute-done.4.recv_ref = bf16[512,128]{1,0:T(8,128)(2,1)} collective-permute-done((bf16[512,128]{1,0:T(8,128)(2,1)}, bf16[512,128]{1,0:T(8,128)(2,1)}, u32[]{:S(2)}, u32[]{:S(2)}) %collective-permute-start.4) | collective-permute-done | bytes 131104 | tf_op jit(solution)/shard_map/ppermute | solution.py:414
  36.7 2.1 %norm.1 = (bf16[512,512]{1,0:T(8,128)(2,1)S(1)}, bf16[512,512]{1,0:T(8,128)(2,1)S(1)}, bf16[256,512]{1,0:T(8,128)(2,1)S(1)}) custom-call(s32[9]{0:T(128)S(1)} %stack.36.pick_ref, f32[512,1024]{1,0:T(8,128)S(1)} %far3.1.acc_ref, bf16[512,1024]{1,0:T(8,128)(2,1)S(1)} %get-tuple-element.55.qt_ref, bf16[512,128]{1,0:T(8,128)(2,1)} %collective-permute-done.4.recv_ref, ...), custom_call_target="tpu_custom_call" | custom-call | flops 1000000000 | bytes 100000 | tf_op jit(solution)/shard_map/norm/pallas_call | solution.py:18
  38.8 0.5 collective-permute-start.5
  39.3 2.0 %collective-permute-done.6.refs_0_ = bf16[192,2048]{1,0:T(8,128)(2,1)} collective-permute-done((bf16[192,2048]{1,0:T(8,128)(2,1)}, bf16[192,2048]{1,0:T(8,128)(2,1)}, u32[]{:S(2)}, u32[]{:S(2)}) %collective-permute-start.6) | collective-permute-done | bytes 786464 | tf_op jit(solution)/shard_map/ppermute | solution.py:427
  41.3 0.1 collective-permute-start.13
  41.4 1.3 %begin.1 = (bf16[256,2048]{1,0:T(8,128)(2,1)S(1)}, bf16[256,2048]{1,0:T(8,128)(2,1)S(1)}) custom-call(bf16[512,512]{1,0:T(8,128)(2,1)S(1)} %get-tuple-element.62.near_ref, bf16[512,512]{1,0:T(8,128)(2,1)S(1)} %get-tuple-element.63.side_ref, bf16[512,4096]{1,0:T(8,128)(2,1)S(1)} %copy-done), custom_call_target="tpu_custom_call" | custom-call | flops 1000000 | bytes 100000 | tf_op jit(solution)/shard_map/begin/pallas_call | solution.py:18
  42.6 2.0 %collective-permute-done.9.refs_2_ = bf16[160,2048]{1,0:T(8,128)(2,1)} collective-permute-done((bf16[160,2048]{1,0:T(8,128)(2,1)}, bf16[160,2048]{1,0:T(8,128)(2,1)}, u32[]{:S(2)}, u32[]{:S(2)}) %collective-permute-start.9) | collective-permute-done | bytes 655392 | tf_op jit(solution)/shard_map/ppermute | solution.py:440
  44.6 1.5 %collective-permute-done.11.refs_5_ = bf16[160,2048]{1,0:T(8,128)(2,1)} collective-permute-done((bf16[160,2048]{1,0:T(8,128)(2,1)}, bf16[160,2048]{1,0:T(8,128)(2,1)}, u32[]{:S(2)}, u32[]{:S(2)}) %collective-permute-start.11) | collective-permute-done | bytes 655392 | tf_op jit(solution)/shard_map/ppermute | solution.py:441
  46.1 2.4 %gather.1 = (bf16[512,2048]{1,0:T(8,128)(2,1)S(1)}, bf16[512,2048]{1,0:T(8,128)(2,1)S(1)}) custom-call(s32[9]{0:T(128)S(1)} %stack.36.pick_ref, bf16[192,2048]{1,0:T(8,128)(2,1)} %collective-permute-done.6.refs_0_, bf16[160,2048]{1,0:T(8,128)(2,1)} %collective-permute-done.7.refs_1_, bf16[160,2048]{1,0:T(8,128)(2,1)} %collective-permute-done.9.refs_2_, ...), custom_call_target="tpu_custom_call" | custom-call | flops 1000000 | bytes 100000 | tf_op jit(solution)/shard_map/gather/pallas_call | solution.py:18
  48.6 2.0 %collective-permute-done.5.b_ref.b_left = bf16[512,512]{1,0:T(8,128)(2,1)S(1)} collective-permute-done((bf16[512,512]{1,0:T(8,128)(2,1)S(1)}, bf16[512,512]{1,0:T(8,128)(2,1)S(1)}, u32[]{:S(2)}, u32[]{:S(2)}) %collective-permute-start.5) | collective-permute-done | bytes 524320 | tf_op jit(solution)/shard_map/ppermute | solution.py:446
  50.6 0.7 left.1
  51.3 4.1 %collective-permute-start.12 = (bf16[128,2048]{1,0:T(8,128)(2,1)S(1)}, bf16[128,2048]{1,0:T(8,128)(2,1)S(1)}, u32[]{:S(2)}, u32[]{:S(2)}) collective-permute-start(bf16[128,2048]{1,0:T(8,128)(2,1)S(1)} %get-tuple-element.73), channel_id=1, source_target_pairs={{0,1},{1,0},{2,3},{3,2},{4,5},{5,4},{6,7},{7,6},{8,9},{9,8},{10,11... | collective-permute-start | bytes 1572872 | tf_op jit(solution)/shard_map/ppermute | solution.py:451
  55.4 0.7 right.1
  56.1 2.3 %collective-permute-start.14 = (bf16[128,2048]{1,0:T(8,128)(2,1)S(1)}, bf16[128,2048]{1,0:T(8,128)(2,1)S(1)}, u32[]{:S(2)}, u32[]{:S(2)}) collective-permute-start(bf16[128,2048]{1,0:T(8,128)(2,1)S(1)} %get-tuple-element.77), channel_id=1, source_target_pairs={{0,1},{1,0},{2,3},{3,2},{4,5},{5,4},{6,7},{7,6},{8,9},{9,8},{10,11... | collective-permute-start | bytes 1572872 | tf_op jit(solution)/shard_map/ppermute | solution.py:453
  58.5 0.1 join_left.1
  58.6 1.2 %collective-permute-start.15 = (bf16[128,2048]{1,0:T(8,128)(2,1)S(1)}, bf16[128,2048]{1,0:T(8,128)(2,1)S(1)}, u32[]{:S(2)}, u32[]{:S(2)}) collective-permute-start(bf16[128,2048]{1,0:T(8,128)(2,1)S(1)} %join_left.1), channel_id=1, source_target_pairs={{0,6},{1,7},{2,4},{3,5},{4,2},{5,3},{6,0},{7,1},{8,14},{9,15},{10,... | collective-permute-start | bytes 1572872 | tf_op jit(solution)/shard_map/ppermute | solution.py:456
  59.7 0.3 collective-permute-done.14.b_ref
  60.0 0.1 join_right.1
  60.1 0.1 collective-permute-start.16
  60.2 2.4 %own.1 = (f32[128,4096]{1,0:T(8,128)S(1)}, bf16[48,4096]{1,0:T(8,128)(2,1)S(1)}, bf16[48,4096]{1,0:T(8,128)(2,1)S(1)}, bf16[32,4096]{1,0:T(8,128)(2,1)S(1)}) custom-call(bf16[256,512]{1,0:T(8,128)(2,1)S(1)} %get-tuple-element.78.a_ref, bf16[512,4096]{1,0:T(8,128)(2,1)S(1)} %copy-done, bf16[512,512]{1,0:T(8,128)(2,1)S(1)} %collective-permute-done.5.b_ref.b_left, ...), custom_call_target="tpu_custom_call" | custom-call | flops 2000000000 | bytes 9000000 | tf_op jit(solution)/shard_map/own/pallas_call | solution.py:18
  62.6 0.5 collective-permute-start.17
  63.1 0.1 collective-permute-start.18
  63.2 0.4 collective-permute-start.19
  63.6 1.8 %collective-permute-done.19.refs_2_ = bf16[32,4096]{1,0:T(8,128)(2,1)S(1)} collective-permute-done((bf16[32,4096]{1,0:T(8,128)(2,1)S(1)}, bf16[32,4096]{1,0:T(8,128)(2,1)S(1)}, u32[]{:S(2)}, u32[]{:S(2)}) %collective-permute-start.19) | collective-permute-done | bytes 262176 | tf_op jit(solution)/shard_map/ppermute | solution.py:460
  65.4 8.0 %collective-permute-done.15.left_ref = bf16[128,2048]{1,0:T(8,128)(2,1)S(1)} collective-permute-done((bf16[128,2048]{1,0:T(8,128)(2,1)S(1)}, bf16[128,2048]{1,0:T(8,128)(2,1)S(1)}, u32[]{:S(2)}, u32[]{:S(2)}) %collective-permute-start.15) | collective-permute-done | bytes 524320 | tf_op jit(solution)/shard_map/ppermute | solution.py:456
  73.4 1.1 %finish.1 = bf16[128,4096]{1,0:T(8,128)(2,1)} custom-call(f32[128,4096]{1,0:T(8,128)S(1)} %get-tuple-element.79.own_ref, bf16[128,2048]{1,0:T(8,128)(2,1)S(1)} %collective-permute-done.15.left_ref, bf16[128,2048]{1,0:T(8,128)(2,1)S(1)} %collective-permute-done.16.right_ref, bf16[48,4096]{1,0:T(8,128)(2,1)S(1)} %collective-permute-done.17.refs_0_, ...), custom_call_target="tpu_custom_call" | custom-call | flops 2000000 | bytes 5000000 | tf_op jit(solution)/shard_map/finish/pallas_call | solution.py:360
  (21 shorter events, 0.0 us)
Async XLA Ops:
  0.0 1.9 %copy-start.4 = (f32[1024,4]{0,1:T(4,128)S(1)}, f32[1024,4]{0,1:T(4,128)}, u32[]{:S(2)}) copy-start(f32[1024,4]{0,1:T(4,128)} %param.10) | copy-start | bytes 49156
  3.1 6.2 %collective-permute-start = (bf16[528,128]{1,0:T(8,128)(2,1)S(1)}, bf16[528,128]{1,0:T(8,128)(2,1)S(1)}, u32[]{:S(2)}, u32[]{:S(2)}) collective-permute-start(bf16[528,128]{1,0:T(8,128)(2,1)S(1)} %get-tuple-element.45.self_ref), channel_id=1, source_target_pairs={{0,8},{8,0},{16,24},{24,16},{32,40},{40,32},{48,56},{56,48},{64,72... | collective-permute-start | bytes 405512 | tf_op jit(solution)/shard_map/ppermute | solution.py:414
  6.8 11.1 %copy-start.6 = (bf16[1024,4,128]{2,1,0:T(4,128)(2,1)S(1)}, bf16[1024,4,128]{2,1,0:T(4,128)(2,1)}, u32[]{:S(2)}) copy-start(bf16[1024,4,128]{2,1,0:T(4,128)(2,1)} %param.8) | copy-start | bytes 3145732
  6.8 26.0 %collective-permute-start.8 = (bf16[160,2048]{1,0:T(8,128)(2,1)S(1)}, bf16[160,2048]{1,0:T(8,128)(2,1)}, u32[]{:S(2)}, u32[]{:S(2)}) collective-permute-start(bf16[160,2048]{1,0:T(8,128)(2,1)S(1)} %get-tuple-element.83), channel_id=1, source_target_pairs={{0,6},{1,7},{2,4},{3,5},{4,2},{5,3},{6,0},{7,1},{8,14},{9,15},{10,... | collective-permute-start | bytes 1966088 | tf_op jit(solution)/shard_map/ppermute | solution.py:422
  9.3 23.4 %collective-permute-start.7 = (bf16[160,2048]{1,0:T(8,128)(2,1)S(1)}, bf16[160,2048]{1,0:T(8,128)(2,1)}, u32[]{:S(2)}, u32[]{:S(2)}) collective-permute-start(bf16[160,2048]{1,0:T(8,128)(2,1)S(1)} %get-tuple-element.84), channel_id=1, source_target_pairs={{0,2},{1,3},{2,0},{3,1},{4,6},{5,7},{6,4},{7,5},{8,10},{9,11},{10,... | collective-permute-start | bytes 1966088 | tf_op jit(solution)/shard_map/ppermute | solution.py:421
  9.4 8.7 %copy-start.2 = (bf16[528,128]{1,0:T(8,128)(2,1)}, bf16[528,128]{1,0:T(8,128)(2,1)S(1)}, u32[]{:S(2)}) copy-start(bf16[528,128]{1,0:T(8,128)(2,1)S(1)} %collective-permute-done.recv_ref) | copy-start | bytes 405508
  9.4 8.6 %copy-start.8 = (bf16[1024,4,128]{2,1,0:T(4,128)(2,1)S(1)}, bf16[1024,4,128]{2,1,0:T(4,128)(2,1)}, u32[]{:S(2)}) copy-start(bf16[1024,4,128]{2,1,0:T(4,128)(2,1)} %param.7) | copy-start | bytes 3145732
  9.5 5.6 %collective-permute-start.1 = (bf16[528,128]{1,0:T(8,128)(2,1)S(1)}, bf16[528,128]{1,0:T(8,128)(2,1)S(1)}, u32[]{:S(2)}, u32[]{:S(2)}) collective-permute-start(bf16[528,128]{1,0:T(8,128)(2,1)S(1)} %get-tuple-element.46.self_ref), channel_id=1, source_target_pairs={{0,24},{8,16},{16,8},{24,0},{32,56},{40,48},{48,40},{56,32},{64,88... | collective-permute-start | bytes 405512 | tf_op jit(solution)/shard_map/ppermute | solution.py:414
  15.0 26.3 %collective-permute-start.6 = (bf16[192,2048]{1,0:T(8,128)(2,1)}, bf16[192,2048]{1,0:T(8,128)(2,1)}, u32[]{:S(2)}, u32[]{:S(2)}) collective-permute-start(bf16[192,2048]{1,0:T(8,128)(2,1)} %get-tuple-element.65), channel_id=1, source_target_pairs={{0,2},{1,3},{2,0},{3,1},{4,6},{5,7},{6,4},{7,5},{8,10},{9,11},{10,... | collective-permute-start | bytes 2359304 | tf_op jit(solution)/shard_map/ppermute | solution.py:427
  16.1 5.8 %collective-permute-start.2 = (bf16[528,128]{1,0:T(8,128)(2,1)S(1)}, bf16[528,128]{1,0:T(8,128)(2,1)S(1)}, u32[]{:S(2)}, u32[]{:S(2)}) collective-permute-start(bf16[528,128]{1,0:T(8,128)(2,1)S(1)} %get-tuple-element.50.self_ref), channel_id=1, source_target_pairs={{0,32},{8,40},{16,48},{24,56},{32,0},{40,8},{48,16},{56,24},{64,96... | collective-permute-start | bytes 405512 | tf_op jit(solution)/shard_map/ppermute | solution.py:414
  17.9 1.2 %copy-start.7 = (bf16[1024,4,128]{2,1,0:T(4,128)(2,1)S(1)}, bf16[1024,4,128]{2,1,0:T(4,128)(2,1)}, u32[]{:S(2)}) copy-start(bf16[1024,4,128]{2,1,0:T(4,128)(2,1)} %param.9) | copy-start | bytes 3145732
  18.1 1.2 %copy-start.1 = (f32[1024,4,10]{0,1,2:T(4,128)S(1)}, f32[1024,4,10]{0,1,2:T(4,128)}, u32[]{:S(2)}) copy-start(f32[1024,4,10]{0,1,2:T(4,128)} %param.11) | copy-start | bytes 491524
  19.3 6.8 %copy-start.3 = (bf16[528,128]{1,0:T(8,128)(2,1)S(1)}, bf16[528,128]{1,0:T(8,128)(2,1)}, u32[]{:S(2)}) copy-start(bf16[528,128]{1,0:T(8,128)(2,1)} %copy-done.2) | copy-start | bytes 405508
  22.0 6.9 %collective-permute-start.3 = (bf16[528,128]{1,0:T(8,128)(2,1)S(1)}, bf16[528,128]{1,0:T(8,128)(2,1)S(1)}, u32[]{:S(2)}, u32[]{:S(2)}) collective-permute-start(bf16[528,128]{1,0:T(8,128)(2,1)S(1)} %get-tuple-element.57.self_ref), channel_id=1, source_target_pairs={{0,64},{8,72},{16,80},{24,88},{32,96},{40,104},{48,112},{56,120},{... | collective-permute-start | bytes 405512 | tf_op jit(solution)/shard_map/ppermute | solution.py:414
  25.0 17.6 %collective-permute-start.10 = (bf16[192,2048]{1,0:T(8,128)(2,1)}, bf16[192,2048]{1,0:T(8,128)(2,1)}, u32[]{:S(2)}, u32[]{:S(2)}) collective-permute-start(bf16[192,2048]{1,0:T(8,128)(2,1)} %get-tuple-element.69), channel_id=1, source_target_pairs={{0,6},{1,7},{2,4},{3,5},{4,2},{5,3},{6,0},{7,1},{8,14},{9,15},{10,... | collective-permute-start | bytes 2359304 | tf_op jit(solution)/shard_map/ppermute | solution.py:434
  29.6 7.1 %collective-permute-start.4 = (bf16[512,128]{1,0:T(8,128)(2,1)}, bf16[512,128]{1,0:T(8,128)(2,1)}, u32[]{:S(2)}, u32[]{:S(2)}) collective-permute-start(bf16[512,128]{1,0:T(8,128)(2,1)} %get-tuple-element.59), channel_id=1, source_target_pairs={{0,192},{8,200},{16,208},{24,216},{32,224},{40,232},{48,240},{56,2... | collective-permute-start | bytes 393224 | tf_op jit(solution)/shard_map/ppermute | solution.py:414
  32.8 11.9 %collective-permute-start.9 = (bf16[160,2048]{1,0:T(8,128)(2,1)}, bf16[160,2048]{1,0:T(8,128)(2,1)}, u32[]{:S(2)}, u32[]{:S(2)}) collective-permute-start(bf16[160,2048]{1,0:T(8,128)(2,1)} %collective-permute-done.7.refs_1_), channel_id=1, source_target_pairs={{0,8},{8,0},{16,24},{24,16},{32,40},{40,32},{48,56},{56,48},{64,72... | collective-permute-start | bytes 1966088 | tf_op jit(solution)/shard_map/ppermute | solution.py:440
  32.8 13.3 %collective-permute-start.11 = (bf16[160,2048]{1,0:T(8,128)(2,1)}, bf16[160,2048]{1,0:T(8,128)(2,1)}, u32[]{:S(2)}, u32[]{:S(2)}) collective-permute-start(bf16[160,2048]{1,0:T(8,128)(2,1)} %collective-permute-done.8.refs_4_), channel_id=1, source_target_pairs={{0,24},{8,16},{16,8},{24,0},{32,56},{40,48},{48,40},{56,32},{64,88... | collective-permute-start | bytes 1966088 | tf_op jit(solution)/shard_map/ppermute | solution.py:441
  35.0 1.7 %copy-start.5 = (f32[4,128]{1,0:T(4,128)S(1)}, f32[4,128]{1,0:T(4,128)}, u32[]{:S(2)}) copy-start(f32[4,128]{1,0:T(4,128)} %gain_ref.1) | copy-start | bytes 6148
  35.0 6.3 %copy-start = (bf16[512,4096]{1,0:T(8,128)(2,1)S(1)}, bf16[512,4096]{1,0:T(8,128)(2,1)}, u32[]{:S(2)}) copy-start(bf16[512,4096]{1,0:T(8,128)(2,1)} %w_ref.3) | copy-start | bytes 12582916
  38.8 11.7 %collective-permute-start.5 = (bf16[512,512]{1,0:T(8,128)(2,1)S(1)}, bf16[512,512]{1,0:T(8,128)(2,1)S(1)}, u32[]{:S(2)}, u32[]{:S(2)}) collective-permute-start(bf16[512,512]{1,0:T(8,128)(2,1)S(1)} %get-tuple-element.62.near_ref), channel_id=1, source_target_pairs={{0,2},{1,3},{2,0},{3,1},{4,6},{5,7},{6,4},{7,5},{8,10},{9,11},{10,... | collective-permute-start | bytes 1572872 | tf_op jit(solution)/shard_map/ppermute | solution.py:446
  41.3 14.1 %collective-permute-start.13 = (bf16[512,512]{1,0:T(8,128)(2,1)S(1)}, bf16[512,512]{1,0:T(8,128)(2,1)S(1)}, u32[]{:S(2)}, u32[]{:S(2)}) collective-permute-start(bf16[512,512]{1,0:T(8,128)(2,1)S(1)} %get-tuple-element.63.side_ref), channel_id=1, source_target_pairs={{0,6},{1,7},{2,4},{3,5},{4,2},{5,3},{6,0},{7,1},{8,14},{9,15},{10,... | collective-permute-start | bytes 1572872 | tf_op jit(solution)/shard_map/ppermute | solution.py:447
  51.3 7.1 %collective-permute-start.12 = (bf16[128,2048]{1,0:T(8,128)(2,1)S(1)}, bf16[128,2048]{1,0:T(8,128)(2,1)S(1)}, u32[]{:S(2)}, u32[]{:S(2)}) collective-permute-start(bf16[128,2048]{1,0:T(8,128)(2,1)S(1)} %get-tuple-element.73), channel_id=1, source_target_pairs={{0,1},{1,0},{2,3},{3,2},{4,5},{5,4},{6,7},{7,6},{8,9},{9,8},{10,11... | collective-permute-start | bytes 1572872 | tf_op jit(solution)/shard_map/ppermute | solution.py:451
  56.1 3.9 %collective-permute-start.14 = (bf16[128,2048]{1,0:T(8,128)(2,1)S(1)}, bf16[128,2048]{1,0:T(8,128)(2,1)S(1)}, u32[]{:S(2)}, u32[]{:S(2)}) collective-permute-start(bf16[128,2048]{1,0:T(8,128)(2,1)S(1)} %get-tuple-element.77), channel_id=1, source_target_pairs={{0,1},{1,0},{2,3},{3,2},{4,5},{5,4},{6,7},{7,6},{8,9},{9,8},{10,11... | collective-permute-start | bytes 1572872 | tf_op jit(solution)/shard_map/ppermute | solution.py:453
  58.6 14.8 %collective-permute-start.15 = (bf16[128,2048]{1,0:T(8,128)(2,1)S(1)}, bf16[128,2048]{1,0:T(8,128)(2,1)S(1)}, u32[]{:S(2)}, u32[]{:S(2)}) collective-permute-start(bf16[128,2048]{1,0:T(8,128)(2,1)S(1)} %join_left.1), channel_id=1, source_target_pairs={{0,6},{1,7},{2,4},{3,5},{4,2},{5,3},{6,0},{7,1},{8,14},{9,15},{10,... | collective-permute-start | bytes 1572872 | tf_op jit(solution)/shard_map/ppermute | solution.py:456
  60.1 13.3 %collective-permute-start.16 = (bf16[128,2048]{1,0:T(8,128)(2,1)S(1)}, bf16[128,2048]{1,0:T(8,128)(2,1)S(1)}, u32[]{:S(2)}, u32[]{:S(2)}) collective-permute-start(bf16[128,2048]{1,0:T(8,128)(2,1)S(1)} %join_right.1), channel_id=1, source_target_pairs={{0,2},{1,3},{2,0},{3,1},{4,6},{5,7},{6,4},{7,5},{8,10},{9,11},{10,... | collective-permute-start | bytes 1572872 | tf_op jit(solution)/shard_map/ppermute | solution.py:457
  62.6 2.8 %collective-permute-start.17 = (bf16[48,4096]{1,0:T(8,128)(2,1)S(1)}, bf16[48,4096]{1,0:T(8,128)(2,1)S(1)}, u32[]{:S(2)}, u32[]{:S(2)}) collective-permute-start(bf16[48,4096]{1,0:T(8,128)(2,1)S(1)} %get-tuple-element.80), channel_id=1, source_target_pairs={{0,1},{1,0},{2,3},{3,2},{4,5},{5,4},{6,7},{7,6},{8,9},{9,8},{10,11... | collective-permute-start | bytes 1179656 | tf_op jit(solution)/shard_map/ppermute | solution.py:460
  63.1 2.3 %collective-permute-start.18 = (bf16[48,4096]{1,0:T(8,128)(2,1)S(1)}, bf16[48,4096]{1,0:T(8,128)(2,1)S(1)}, u32[]{:S(2)}, u32[]{:S(2)}) collective-permute-start(bf16[48,4096]{1,0:T(8,128)(2,1)S(1)} %get-tuple-element.81), channel_id=1, source_target_pairs={{0,1},{1,0},{2,3},{3,2},{4,5},{5,4},{6,7},{7,6},{8,9},{9,8},{10,11... | collective-permute-start | bytes 1179656 | tf_op jit(solution)/shard_map/ppermute | solution.py:460
  63.2 2.1 %collective-permute-start.19 = (bf16[32,4096]{1,0:T(8,128)(2,1)S(1)}, bf16[32,4096]{1,0:T(8,128)(2,1)S(1)}, u32[]{:S(2)}, u32[]{:S(2)}) collective-permute-start(bf16[32,4096]{1,0:T(8,128)(2,1)S(1)} %get-tuple-element.82), channel_id=1, source_target_pairs={{0,1},{1,0},{2,3},{3,2},{4,5},{5,4},{6,7},{7,6},{8,9},{9,8},{10,11... | collective-permute-start | bytes 786440 | tf_op jit(solution)/shard_map/ppermute | solution.py:460
